TPU v7x, 128 devices: a whole 4x4x4 slice. The times are simulated.
128 devices in a mesh: grp: 4 (over x_lo, core), dev: 32 (over z, y, x_hi).
Axes of the slice: x: 4 (x_hi: 2, x_lo: 2; x = x_hi * 2 + x_lo), y: 4, z: 4, core: 2. Of those that a mesh axis runs over, the one named last changes fastest.
Arguments:
- views_a: bfloat16 [32768, 256], P(('grp', 'dev')), may hold values from -6 to 6
- views_b: bfloat16 [32768, 256], P(('grp', 'dev')), may hold values from -6 to 6
- positives: int32 [32768], P(('grp', 'dev')), may hold values from 0 to 32767, as said below
- plan: int32 [2, 4], replicated, may hold values from 0 to 3, as said below
Outputs:
- grad_a: float32 [32768, 256], P(('grp', 'dev'))
- grad_b: float32 [32768, 256], P(('grp', 'dev'))
Inputs may be any that keep to these rules, and one draw needn't show every extreme that they name: Row r holds a round of one round-robin over the 4 groups: plan[r, plan[r, g]] == g and plan[r, g] != g; no two rows pair the same two groups. positives[i] is i itself or a view of a group that plan pairs with the group of view i in some row.
All inputs are finite; a program needn't handle non-finite values.
Results may differ from a plain program's by a relative error of at most 0.00057.
Values may be sent and summed in bfloat16 or wider, within the bound.
No kernel may reach another device: no remote copies, remote signals or barrier semaphores. Data moves between devices by JAX's collectives and lax.ppermute only.
A program may use at most 128 MiB of HBM per device.

v0:
```python
import math

import jax
import jax.numpy as jnp
from jax import lax
from jax.sharding import PartitionSpec as P

logit_scale = 2.0
logit_bias = -6.0


def weights_for(queries, labels, keys, first, factor):
    logits = (
        lax.dot_general(queries, keys, (((1,), (1,)), ((), ())), preferred_element_type=jnp.float32)
        * factor
        + logit_bias
    )
    columns = first + jnp.arange(keys.shape[0], dtype=jnp.int32)
    hit = (labels[:, None] == columns[None, :]).astype(jnp.float32)
    return (jax.nn.sigmoid(logits) - hit).astype(jnp.bfloat16)


def left_product(weights, values):
    return lax.dot_general(
        weights, values, (((0,), (0,)), ((), ())), preferred_element_type=jnp.float32
    )


def shards(views_a, views_b, positives, plan):
    rows = views_a.shape[0]
    width = views_a.shape[1]
    members = lax.axis_size("dev")
    groups = lax.axis_size("grp")
    group_rows = rows * members
    group = lax.axis_index("grp")
    factor = logit_scale / math.sqrt(width)
    partners = lax.dynamic_index_in_dim(plan, group, 1, keepdims=False)
    rounds = plan.shape[0]

    def score_group(key_shard, owner):
        first = owner * group_rows
        piece = lax.all_gather(key_shard, "dev", axis=0, tiled=True)
        weights = weights_for(views_a, positives, piece, first, factor)
        grad_rows = jnp.dot(weights, piece, preferred_element_type=jnp.float32)
        grad_keys = left_product(weights, views_a)
        grad_rows, grad_keys = (grad_rows, grad_keys)
        return (grad_rows, lax.psum_scatter(grad_keys, "dev", scatter_dimension=0, tiled=True))

    grad_a, grad_b = score_group(views_b, group)
    gathered = lax.all_gather(views_b, "grp", axis=0, tiled=True)
    returned = jnp.zeros((groups, rows, width), jnp.float32)
    for slot in range(rounds):
        partner = partners[slot]
        shard = lax.dynamic_slice_in_dim(gathered, partner * rows, rows, 0)
        grad_rows, share = score_group(shard, partner)
        grad_a = grad_a + grad_rows
        returned = lax.dynamic_update_slice(returned, share[None], (partner, 0, 0))
    back = lax.psum_scatter(returned, "grp", scatter_dimension=0, tiled=True)
    grad_b = grad_b + back[0]
    return (grad_a * factor, grad_b * factor)


def solution(mesh):
    placed = (P(("grp", "dev"), None), P(("grp", "dev"), None), P(("grp", "dev")), P())
    return jax.shard_map(
        shards,
        mesh=mesh,
        in_specs=placed,
        out_specs=(P(("grp", "dev"), None), P(("grp", "dev"), None)),
        check_vma=False,
    )
```

profile of v0, /device:TPU:1, one launch (start us, length us, event | category | flops | bytes accessed | tf_op | source)
XLA Modules:
  0.0 940.6 jit_solution(15006217095677738789)
XLA Ops:
  9.9 8.7 all_gather.13
  21.6 79.5 %all-gather.6.cloned.1.call-done = bf16[8192,256]{1,0:T(8,128)(2,1)} async-done(((bf16[256,256]{1,0:T(8,128)(2,1)}), bf16[8192,256]{1,0:T(8,128)(2,1)}) %all-gather.6.cloned.1.call-update) | async-done | bytes 4194320 | tf_op jit(solution)/shard_map/all_gather | solution.py:42
  101.1 5.8 fusion.18
  106.9 2.1 copy-done.1
  109.0 4.5 fusion.28
  114.3 69.8 %all-gather.8.cloned.1.call-done = bf16[8192,256]{1,0:T(8,128)(2,1)} async-done(((bf16[256,256]{1,0:T(8,128)(2,1)}), bf16[8192,256]{1,0:T(8,128)(2,1)}) %all-gather.8.cloned.1.call-update) | async-done | bytes 4194320 | tf_op jit(solution)/shard_map/all_gather | solution.py:42
  184.1 5.8 fusion.22
  189.9 1.9 copy-done.3
  191.8 4.6 fusion.29
  196.5 70.1 %all-gather.4.cloned.1.call-done = bf16[8192,256]{1,0:T(8,128)(2,1)} async-done(((bf16[256,256]{1,0:T(8,128)(2,1)}), bf16[8192,256]{1,0:T(8,128)(2,1)}) %all-gather.4.cloned.1.call-update) | async-done | bytes 4194320 | tf_op jit(solution)/shard_map/all_gather | solution.py:42
  266.5 5.8 fusion.14
  272.3 1.9 copy-done.5
  274.3 4.6 fusion.27
  283.0 177.7 %reduce-scatter.7.cloned.1.call-done = f32[256,256]{1,0:T(8,128)} async-done(((f32[8192,256]{1,0:T(8,128)}), f32[256,256]{1,0:T(8,128)}) %reduce-scatter.7.cloned.1.call-update) | async-done | bytes 262160 | tf_op jit(solution)/shard_map/reduce_scatter | solution.py:47
  461.8 213.1 %reduce-scatter.9.cloned.1.call-done = f32[256,256]{1,0:T(8,128)} async-done(((f32[8192,256]{1,0:T(8,128)}), f32[256,256]{1,0:T(8,128)}) %reduce-scatter.9.cloned.1.call-update) | async-done | bytes 262160 | tf_op jit(solution)/shard_map/reduce_scatter | solution.py:47
  675.8 1.1 copy-done.6
  676.9 4.8 fusion.26
  681.8 1.0 copy-done.7
  682.8 1.2 convolution_add_fusion.1
  685.0 1.3 copy-done.8
  686.3 1.9 fusion.23
  688.3 201.2 %reduce-scatter.5.cloned.1.call-done = f32[256,256]{1,0:T(8,128)} async-done(((f32[8192,256]{1,0:T(8,128)}), f32[256,256]{1,0:T(8,128)}) %reduce-scatter.5.cloned.1.call-update) | async-done | bytes 262160 | tf_op jit(solution)/shard_map/reduce_scatter | solution.py:47
  889.5 42.5 %reduce-scatter.11.cloned.1.call-done = f32[1,256,256]{2,1,0:T(8,128)} async-done(((f32[4,256,256]{2,1,0:T(8,128)}), f32[1,256,256]{2,1,0:T(8,128)}) %reduce-scatter.11.cloned.1.call-update) | async-done | bytes 262160 | tf_op jit(solution)/shard_map/reduce_scatter | solution.py:58
  932.0 1.8 fusion.24
  (37 shorter events, 7.0 us)
Async XLA Ops:
  7.2 94.0 %copy-start = (bf16[256,256]{1,0:T(8,128)(2,1)S(1)}, bf16[256,256]{1,0:T(8,128)(2,1)}, u32[]{:S(2)}) copy-start(bf16[256,256]{1,0:T(8,128)(2,1)} %param.4) | copy-start | bytes 393220
  7.2 93.9 %all-gather.6.cloned.1.call-start = ((), (), s32[]{:S(2)}) async-start(), calls=%async_computation.5 | async-start | bytes 4325376 | tf_op jit(solution)/shard_map/all_gather | solution.py:42
  19.4 164.8 %all-gather.8.cloned.1.call-start = ((), (), s32[]{:S(2)}) async-start(), calls=%async_computation.6 | async-start | bytes 4325376 | tf_op jit(solution)/shard_map/all_gather | solution.py:42
  20.1 246.4 %all-gather.4.cloned.1.call-start = ((), (), s32[]{:S(2)}) async-start(), calls=%async_computation.4 | async-start | bytes 4325376 | tf_op jit(solution)/shard_map/all_gather | solution.py:42
  20.8 439.9 %reduce-scatter.7.cloned.1.call-start = ((), (), s32[]{:S(2)}) async-start(), calls=%async_computation.8 | async-start | bytes 8650752 | tf_op jit(solution)/shard_map/reduce_scatter | solution.py:47
  106.9 2.1 copy-start.1
  109.0 75.1 %copy-start.9 = (s32[256]{0:T(256)S(1)}, s32[256]{0:T(256)}, u32[]{:S(2)}) copy-start(s32[256]{0:T(256)} %param.6) | copy-start | bytes 3076
  113.6 561.3 %reduce-scatter.9.cloned.1.call-start = ((), (), s32[]{:S(2)}) async-start(), calls=%async_computation.9 | async-start | bytes 8650752 | tf_op jit(solution)/shard_map/reduce_scatter | solution.py:47
  189.9 1.9 copy-start.3
  196.4 693.1 %reduce-scatter.5.cloned.1.call-start = ((), (), s32[]{:S(2)}) async-start(), calls=%async_computation.7 | async-start | bytes 8650752 | tf_op jit(solution)/shard_map/reduce_scatter | solution.py:47
  272.3 1.9 copy-start.5
  278.8 653.1 %reduce-scatter.11.cloned.1.call-start = ((), (), s32[]{:S(2)}) async-start(), calls=%async_computation.10 | async-start | bytes 1310720 | tf_op jit(solution)/shard_map/reduce_scatter | solution.py:58
  675.8 1.1 copy-start.6
  676.9 4.9 copy-start.2
  676.9 5.9 copy-start.7
  682.8 2.2 copy-start.4
  682.8 3.5 copy-start.8
Sparse Core Ops, SparseCore 0:
  19.5 81.6 all-gather.5
  104.8 79.3 all-gather.7
  187.2 79.3 all-gather.3
  268.8 191.8 reduce-scatter.6
  463.0 211.8 reduce-scatter.8
  677.1 212.3 reduce-scatter.4
  891.9 40.0 reduce-scatter.10
where the time goes:
time: 941 us
  waiting for transfers between devices  855 us (91%)
  matrix products  39 us (4%)
  between operations  20.8 us (2%)
  local copies, waits for them, and re-layouts  14.3 us (2%)
    reduce_scatter x3, waiting for transfers between devices, score_group(): lax.psum_scatter(grad_keys, 'dev', scatter_dimension=0, tiled=True)  592 us
    all_gather x3, waiting for transfers between devices, score_group(): piece = lax.all_gather(key_shard, 'dev', axis=0, tiled=True)  219 us
    reduce_scatter x1, waiting for transfers between devices, shards(): back = lax.psum_scatter(returned, 'grp', scatter_dimension=0, tiled=True)  42.5 us
  transfers between devices with their start and end apart: 7, of which 7 were waited for; matrix products, arithmetic and copies ran while one was open for 4% of the time, Pallas kernels for 0%

commit v1 on v0

v1 whole, which is shorter than its diff:
```python
import functools
import math

import jax
import jax.numpy as jnp
from jax import lax
from jax.experimental import pallas as pl
from jax.experimental.pallas import tpu as pltpu
from jax.sharding import Mesh, PartitionSpec as P

logit_scale = 2.0
logit_bias = -6.0
AXES = ("xl", "core", "z", "y", "xh")
ROWS = 256
NOTE = 16


def x_place(x):
    return (x % 2) * 2 + (x // 2) % 2


def along_x(value, shift):
    pairs = [(x_place(x), x_place((x + shift) % 4)) for x in range(4)]
    return lax.ppermute(value, ("xl", "xh"), pairs)


def along_y(value, shift):
    return lax.ppermute(value, "y", [(y, (y + shift) % 4) for y in range(4)])


def swap_low(value):
    return lax.ppermute(value, "z", [(z, z ^ 1) for z in range(4)])


def swap_far(value):
    return lax.ppermute(value, "z", [(z, 3 - z) for z in range(4)])


def swap_core(value):
    return lax.ppermute(value, "core", [(0, 1), (1, 0)])


def gather_ring(shift, pair):
    half = pair.shape[0] // 2
    before = shift(pair, 1)
    after = shift(pair, -1)
    first = shift(before[:half], 1)
    second = shift(after[half:], -1)
    return before, after, first, second


def scatter_ring(shift, own, before, after, opposite):
    half = opposite.shape[0] // 2
    from_before = shift(opposite[:half], 1)
    from_after = shift(opposite[half:], -1)
    after = jnp.concatenate([after[:half] + from_before, after[half:]])
    before = jnp.concatenate([before[:half], before[half:] + from_after])
    return own + shift(after, 1) + shift(before, -1)


def kernel(factor, marks, *refs):
    a_refs, b_refs = refs[:5], refs[5:15]
    ga_ref, gb_ref, a_all, labels, b_all = refs[15:]
    step = ROWS + NOTE
    chunk = 0
    for ref in a_refs:
        for start in range(0, ref.shape[0], step):
            a_all[pl.ds(chunk * ROWS, ROWS), :] = ref[start : start + ROWS, :]
            note = ref[start + ROWS : start + step, :].astype(jnp.float32)
            labels[:, pl.ds(chunk * ROWS, ROWS)] = (note[0:1] * 256.0 + note[1:2]).astype(jnp.int32)
            chunk += 1
    for core in range(2):
        own, before, after, first, second = b_refs[5 * core : 5 * core + 5]
        same, other = core, 2 + core
        b_all[same, 0:512, :] = own[...]
        b_all[same, 512:768, :] = first[...]
        b_all[same, 768:1024, :] = second[...]
        b_all[other, 0:512, :] = before[...]
        b_all[other, 512:1024, :] = after[...]
    ga_ref[...] = jnp.zeros_like(ga_ref)
    gb_ref[marks[3]] = jnp.zeros((4 * ROWS, ROWS), jnp.float32)
    half_scale = 0.5 * factor
    half_bias = 0.5 * logit_bias
    iota = lax.broadcasted_iota(jnp.int32, (ROWS, 8 * ROWS), 0)

    def block(index, carry):
        slot = index // 4
        part = index % 4
        which = marks[slot]
        rows = pl.ds(pl.multiple_of(part * ROWS, ROWS), ROWS)
        keys = b_all[which, rows, :]
        a = a_all[...]
        logits = lax.dot_general(
            keys, a, (((1,), (1,)), ((), ())), preferred_element_type=jnp.float32
        )
        hit = iota == labels[...] - marks[4 + which * 4 + part]
        weights = 0.5 * jnp.tanh(logits * half_scale + half_bias) + jnp.where(hit, -0.5, 0.5)
        weights = weights.astype(jnp.bfloat16)
        gb_ref[which, rows, :] = jnp.dot(weights, a, preferred_element_type=jnp.float32)
        ga_ref[...] += lax.dot_general(
            weights, keys, (((0,), (0,)), ((), ())), preferred_element_type=jnp.float32
        )
        return carry

    lax.fori_loop(0, 12, block, 0)


def score(factor, marks, a_parts, b_parts):
    vmem = pl.BlockSpec(memory_space=pltpu.VMEM)
    return pl.pallas_call(
        functools.partial(kernel, factor),
        out_shape=(
            jax.ShapeDtypeStruct((8 * ROWS, ROWS), jnp.float32),
            jax.ShapeDtypeStruct((4, 4 * ROWS, ROWS), jnp.float32),
        ),
        in_specs=[pl.BlockSpec(memory_space=pltpu.SMEM)] + [vmem] * 15,
        out_specs=(vmem, vmem),
        scratch_shapes=[
            pltpu.VMEM((8 * ROWS, ROWS), jnp.bfloat16),
            pltpu.VMEM((1, 8 * ROWS), jnp.int32),
            pltpu.VMEM((4, 4 * ROWS, ROWS), jnp.bfloat16),
        ],
        compiler_params=pltpu.CompilerParams(vmem_limit_bytes=48 << 20),
        cost_estimate=pl.CostEstimate(
            flops=2 * 3 * 2048 * 3072 * 256, bytes_accessed=10 << 20, transcendentals=2048 * 3072
        ),
    )(marks, *a_parts, *b_parts)


def shards(views_a, views_b, positives, plan):
    factor = logit_scale / math.sqrt(views_a.shape[1])
    xl, core = lax.axis_index("xl"), lax.axis_index("core")
    z, y, xh = lax.axis_index("z"), lax.axis_index("y"), lax.axis_index("xh")
    group = xl * 2 + core
    first, second = plan[0, group] ^ group, plan[1, group] ^ group
    unused = first ^ second
    x = xh * 2 + xl
    places = {}
    for offset in range(4):
        at = (x + offset) % 4
        for far in range(2):
            zz = jnp.where(far == 1, 3 - z, z)
            places[offset, far] = (at % 2) * 16384 + (zz * 8 + y * 2 + at // 2) * 256
    bases = []
    for which in range(4):
        other = core if which % 2 == 0 else 1 - core
        if which < 2:
            order = [(0, 0), (0, 1), (2, 0), (2, 1)]
        else:
            order = [(3, 0), (3, 1), (1, 0), (1, 1)]
        bases += [places[o] + other * 8192 for o in order]
    zero = jnp.int32(0)
    marks = jnp.stack([v.astype(jnp.int32) for v in [zero, first, second, unused] + bases])

    note = jnp.stack([positives // 256, positives % 256]).astype(jnp.bfloat16)
    note = jnp.pad(note, ((0, NOTE - 2), (0, 0)))
    a_own = jnp.concatenate([views_a, note])
    a_own = jnp.concatenate([a_own, swap_low(a_own)])
    b_own = jnp.concatenate([views_b, swap_far(views_b)])
    a_parts = [a_own, *gather_ring(along_y, a_own)]
    b_parts = [b_own, *gather_ring(along_x, b_own)]
    b_parts += [swap_core(part) for part in b_parts]
    grad_a, grad_b = score(factor, marks, a_parts, b_parts)

    step = 2 * ROWS
    a_own, a_before, a_after, a_opposite = [grad_a[i * step : (i + 1) * step] for i in range(4)]
    a_mine = scatter_ring(along_y, a_own, a_before, a_after, a_opposite)
    grad_a = a_mine[:ROWS] + swap_low(a_mine[ROWS:])

    got = swap_core(jnp.stack([grad_b[1], grad_b[3]]))
    same, other = grad_b[0] + got[0], grad_b[2] + got[1]
    b_mine = scatter_ring(along_x, same[:step], other[:step], other[step:], same[step:])
    grad_b = b_mine[:ROWS] + swap_far(b_mine[ROWS:])
    return grad_a * factor, grad_b * factor


def solution(mesh):
    fine = Mesh(mesh.devices.reshape(2, 2, 4, 4, 2), AXES)
    split = P(AXES, None)
    return jax.shard_map(
        shards,
        mesh=fine,
        in_specs=(split, split, P(AXES), P()),
        out_specs=(split, split),
        check_vma=False,
    )
```

time: 941 us -> 106 us (0.11)
  the two profiles are of different devices: /device:TPU:1 before, /device:TPU:0 now
where the time goes in v1:
time: 106 us
  waiting for transfers between devices  43.5 us (41%)
  starting transfers between devices  34.2 us (32%)
  Pallas kernels  17.3 us (16%)
  other arithmetic  5.01 us (5%)
  local copies, waits for them, and re-layouts  3.51 us (3%)
  between operations  2.25 us (2%)
    ppermute x8, waiting for transfers between devices, along_x(): return lax.ppermute(value, ('xl', 'xh'), pairs)  20.1 us
    ppermute x8, waiting for transfers between devices, along_y(): return lax.ppermute(value, 'y', [(y, (y + shift) % 4) for y in range(4)])  19.6 us
    pallas_call x1, Pallas kernels, score(): pl.pallas_call(functools.partial(kernel, factor), out_shape=(jax.ShapeDty...  17.3 us
    ppermute x8, starting transfers between devices, along_x(): return lax.ppermute(value, ('xl', 'xh'), pairs)  13.1 us
    ppermute x8, starting transfers between devices, along_y(): return lax.ppermute(value, 'y', [(y, (y + shift) % 4) for y in range(4)])  9.97 us
    ppermute x2, starting transfers between devices, swap_far(): return lax.ppermute(value, 'z', [(z, 3 - z) for z in range(4)])  6.26 us
    ppermute x2, starting transfers between devices, swap_low(): return lax.ppermute(value, 'z', [(z, z ^ 1) for z in range(4)])  3.7 us
    ppermute x2, waiting for transfers between devices, swap_far(): return lax.ppermute(value, 'z', [(z, 3 - z) for z in range(4)])  3.6 us
  transfers between devices with their start and end apart: 26, of which 10 were waited for; matrix products, arithmetic and copies ran while one was open for 4% of the time, Pallas kernels for 0%

profile of v1, /device:TPU:0, one launch (start us, length us, event | category | flops | bytes accessed | tf_op | source)
XLA Modules:
  0.0 105.7 jit_solution(1559840442332920965)
XLA Ops:
  2.3 2.1 %collective-permute-start = (bf16[272,256]{1,0:T(8,128)(2,1)S(1)}, bf16[272,256]{1,0:T(8,128)(2,1)S(1)}, u32[]{:S(2)}, u32[]{:S(2)}) collective-permute-start(bf16[272,256]{1,0:T(8,128)(2,1)S(1)} %pad_maximum_fusion.6), channel_id=1, source_target_pairs={{0,8},{8,0},{16,24},{24,16},{1,9},{9,1},{17,25},{25,17},{2,10},{10... | collective-permute-start | bytes 417800 | tf_op jit(solution)/shard_map/ppermute | solution.py:32
  4.4 2.5 %collective-permute-start.5 = (bf16[256,256]{1,0:T(8,128)(2,1)}, bf16[256,256]{1,0:T(8,128)(2,1)S(1)}, u32[]{:S(2)}, u32[]{:S(2)}) collective-permute-start(bf16[256,256]{1,0:T(8,128)(2,1)} %param.5), channel_id=1, source_target_pairs={{0,24},{8,16},{16,8},{24,0},{1,25},{9,17},{17,9},{25,1},{2,26},{10... | collective-permute-start | bytes 393224 | tf_op jit(solution)/shard_map/ppermute | solution.py:36
  6.9 0.9 constant_dynamic-update-slice_fusion.1
  9.0 3.1 %collective-permute-start.2 = (bf16[544,256]{1,0:T(8,128)(2,1)S(1)}, bf16[544,256]{1,0:T(8,128)(2,1)S(1)}, u32[]{:S(2)}, u32[]{:S(2)}) collective-permute-start(bf16[544,256]{1,0:T(8,128)(2,1)S(1)} %pad_maximum_fusion.5.refs_0_), channel_id=1, source_target_pairs={{0,6},{2,0},{4,2},{6,4},{1,7},{3,1},{5,3},{7,5},{8,14},{10,8},{12,... | collective-permute-start | bytes 835592 | tf_op jit(solution)/shard_map/ppermute | solution.py:28
  12.1 2.8 %collective-permute-start.7 = (bf16[512,256]{1,0:T(8,128)(2,1)S(1)}, bf16[512,256]{1,0:T(8,128)(2,1)S(1)}, u32[]{:S(2)}, u32[]{:S(2)}) collective-permute-start(bf16[512,256]{1,0:T(8,128)(2,1)S(1)} %constant_dynamic-update-slice_fusion.refs_5_), channel_id=1, source_target_pairs={{0,65},{64,0},{1,64},{65,1},{2,67},{66,2},{3,66},{67,3},{4,69},{68... | collective-permute-start | bytes 786440 | tf_op jit(solution)/shard_map/ppermute | solution.py:24
  14.9 4.6 %collective-permute-done.7.refs_7_ = bf16[512,256]{1,0:T(8,128)(2,1)S(1)} collective-permute-done((bf16[512,256]{1,0:T(8,128)(2,1)S(1)}, bf16[512,256]{1,0:T(8,128)(2,1)S(1)}, u32[]{:S(2)}, u32[]{:S(2)}) %collective-permute-start.7) | collective-permute-done | bytes 262176 | tf_op jit(solution)/shard_map/ppermute | solution.py:24
  19.5 3.8 %collective-permute-start.9 = (bf16[256,256]{1,0:T(8,128)(2,1)S(1)}, bf16[256,256]{1,0:T(8,128)(2,1)S(1)}, u32[]{:S(2)}, u32[]{:S(2)}) collective-permute-start(bf16[256,256]{1,0:T(8,128)(2,1)S(1)} %slice.161), channel_id=1, source_target_pairs={{0,65},{64,0},{1,64},{65,1},{2,67},{66,2},{3,66},{67,3},{4,69},{68... | collective-permute-start | bytes 393224 | tf_op jit(solution)/shard_map/ppermute | solution.py:24
  23.3 3.0 %collective-permute-start.4 = (bf16[272,256]{1,0:T(8,128)(2,1)S(1)}, bf16[272,256]{1,0:T(8,128)(2,1)S(1)}, u32[]{:S(2)}, u32[]{:S(2)}) collective-permute-start(bf16[272,256]{1,0:T(8,128)(2,1)S(1)} %slice.159), channel_id=1, source_target_pairs={{0,6},{2,0},{4,2},{6,4},{1,7},{3,1},{5,3},{7,5},{8,14},{10,8},{12,... | collective-permute-start | bytes 417800 | tf_op jit(solution)/shard_map/ppermute | solution.py:28
  27.1 5.5 %collective-permute-done.8.refs_8_ = bf16[256,256]{1,0:T(8,128)(2,1)S(1)} collective-permute-done((bf16[256,256]{1,0:T(8,128)(2,1)S(1)}, bf16[256,256]{1,0:T(8,128)(2,1)S(1)}, u32[]{:S(2)}, u32[]{:S(2)}) %collective-permute-start.8) | collective-permute-done | bytes 131104 | tf_op jit(solution)/shard_map/ppermute | solution.py:24
  35.2 17.3 %shard_map.59 = (f32[2048,256]{1,0:T(8,128)S(1)}, f32[4,1024,256]{2,1,0:T(8,128)}) custom-call(s32[20]{0:T(128)S(1)} %stack.94.marks, bf16[544,256]{1,0:T(8,128)(2,1)S(1)} %pad_maximum_fusion.5.refs_0_, bf16[544,256]{1,0:T(8,128)(2,1)S(1)} %collective-permute-done.1.refs_1_, bf16[544,256]{1,0:T(8,128)(2,1)S(1)} %collective-permute-done.2.refs_2_, ...), custom_call_target="tpu_custom_call" | custom-call | flops 9663676416 | bytes 10485760 | tf_op jit(solution)/shard_map/pallas_call | solution.py:110
  52.4 1.7 %fusion.11 = (f32[1,1024,256]{2,1,0:T(8,128)S(1)}, f32[1,1024,256]{2,1,0:T(8,128)S(1)}) fusion(f32[4,1024,256]{2,1,0:T(8,128)} %get-tuple-element.5), kind=kLoop, calls=%fused_computation.44 | loop fusion | bytes 4194304 | tf_op jit(solution)/shard_map/slice | solution.py:170
  54.5 9.9 %collective-permute-done.15 = f32[256,256]{1,0:T(8,128)S(1)} collective-permute-done((f32[256,256]{1,0:T(8,128)S(1)}, f32[256,256]{1,0:T(8,128)S(1)}, u32[]{:S(2)}, u32[]{:S(2)}) %collective-permute-start.15) | collective-permute-done | bytes 262176 | tf_op jit(solution)/shard_map/ppermute | solution.py:28
  64.6 2.1 %collective-permute-start.16 = (f32[512,256]{1,0:T(8,128)S(1)}, f32[512,256]{1,0:T(8,128)S(1)}, u32[]{:S(2)}, u32[]{:S(2)}) collective-permute-start(f32[512,256]{1,0:T(8,128)S(1)} %pad_maximum_fusion.1), channel_id=1, source_target_pairs={{0,2},{2,4},{4,6},{6,0},{1,3},{3,5},{5,7},{7,1},{8,10},{10,12},{12... | collective-permute-start | bytes 1572872 | tf_op jit(solution)/shard_map/ppermute | solution.py:28
  66.6 5.8 %collective-permute-done.17 = f32[256,256]{1,0:T(8,128)S(1)} collective-permute-done((f32[256,256]{1,0:T(8,128)S(1)}, f32[256,256]{1,0:T(8,128)S(1)}, u32[]{:S(2)}, u32[]{:S(2)}) %collective-permute-start.17) | collective-permute-done | bytes 262176 | tf_op jit(solution)/shard_map/ppermute | solution.py:28
  72.9 3.2 %collective-permute-start.23 = (f32[256,256]{1,0:T(8,128)S(1)}, f32[256,256]{1,0:T(8,128)S(1)}, u32[]{:S(2)}, u32[]{:S(2)}) collective-permute-start(f32[256,256]{1,0:T(8,128)S(1)} %get-tuple-element.17), channel_id=1, source_target_pairs={{0,65},{64,0},{1,64},{65,1},{2,67},{66,2},{3,66},{67,3},{4,69},{68... | collective-permute-start | bytes 786440 | tf_op jit(solution)/shard_map/ppermute | solution.py:24
  76.2 1.6 %collective-permute-start.18 = (f32[512,256]{1,0:T(8,128)S(1)}, f32[512,256]{1,0:T(8,128)S(1)}, u32[]{:S(2)}, u32[]{:S(2)}) collective-permute-start(f32[512,256]{1,0:T(8,128)S(1)} %pad_maximum_fusion.2), channel_id=1, source_target_pairs={{0,6},{2,0},{4,2},{6,4},{1,7},{3,1},{5,3},{7,5},{8,14},{10,8},{12,... | collective-permute-start | bytes 1572872 | tf_op jit(solution)/shard_map/ppermute | solution.py:28
  77.8 3.4 %collective-permute-done.21 = f32[256,256]{1,0:T(8,128)S(1)} collective-permute-done((f32[256,256]{1,0:T(8,128)S(1)}, f32[256,256]{1,0:T(8,128)S(1)}, u32[]{:S(2)}, u32[]{:S(2)}) %collective-permute-start.21) | collective-permute-done | bytes 262176 | tf_op jit(solution)/shard_map/ppermute | solution.py:24
  81.2 3.0 %collective-permute-start.24 = (f32[512,256]{1,0:T(8,128)S(1)}, f32[512,256]{1,0:T(8,128)S(1)}, u32[]{:S(2)}, u32[]{:S(2)}) collective-permute-start(f32[512,256]{1,0:T(8,128)S(1)} %pad_maximum_fusion.4), channel_id=1, source_target_pairs={{0,65},{64,0},{1,64},{65,1},{2,67},{66,2},{3,66},{67,3},{4,69},{68... | collective-permute-start | bytes 1572872 | tf_op jit(solution)/shard_map/ppermute | solution.py:24
  84.4 3.9 %collective-permute-done.18 = f32[512,256]{1,0:T(8,128)S(1)} collective-permute-done((f32[512,256]{1,0:T(8,128)S(1)}, f32[512,256]{1,0:T(8,128)S(1)}, u32[]{:S(2)}, u32[]{:S(2)}) %collective-permute-start.18) | collective-permute-done | bytes 524320 | tf_op jit(solution)/shard_map/ppermute | solution.py:28
  88.5 1.6 %collective-permute-start.19 = (f32[256,256]{1,0:T(8,128)S(1)}, f32[256,256]{1,0:T(8,128)S(1)}, u32[]{:S(2)}, u32[]{:S(2)}) collective-permute-start(f32[256,256]{1,0:T(8,128)S(1)} %slice.163), channel_id=1, source_target_pairs={{0,8},{8,0},{16,24},{24,16},{1,9},{9,1},{17,25},{25,17},{2,10},{10... | collective-permute-start | bytes 786440 | tf_op jit(solution)/shard_map/ppermute | solution.py:32
  90.1 3.2 %collective-permute-done.24 = f32[512,256]{1,0:T(8,128)S(1)} collective-permute-done((f32[512,256]{1,0:T(8,128)S(1)}, f32[512,256]{1,0:T(8,128)S(1)}, u32[]{:S(2)}, u32[]{:S(2)}) %collective-permute-start.24) | collective-permute-done | bytes 524320 | tf_op jit(solution)/shard_map/ppermute | solution.py:24
  93.2 3.5 %collective-permute-done.22 = f32[512,256]{1,0:T(8,128)S(1)} collective-permute-done((f32[512,256]{1,0:T(8,128)S(1)}, f32[512,256]{1,0:T(8,128)S(1)}, u32[]{:S(2)}, u32[]{:S(2)}) %collective-permute-start.22) | collective-permute-done | bytes 524320 | tf_op jit(solution)/shard_map/ppermute | solution.py:24
  96.9 3.7 %collective-permute-start.25 = (f32[256,256]{1,0:T(8,128)S(1)}, f32[256,256]{1,0:T(8,128)S(1)}, u32[]{:S(2)}, u32[]{:S(2)}) collective-permute-start(f32[256,256]{1,0:T(8,128)S(1)} %slice.174), channel_id=1, source_target_pairs={{0,24},{8,16},{16,8},{24,0},{1,25},{9,17},{17,9},{25,1},{2,26},{10... | collective-permute-start | bytes 786440 | tf_op jit(solution)/shard_map/ppermute | solution.py:36
  101.4 3.6 %collective-permute-done.25 = f32[256,256]{1,0:T(8,128)S(1)} collective-permute-done((f32[256,256]{1,0:T(8,128)S(1)}, f32[256,256]{1,0:T(8,128)S(1)}, u32[]{:S(2)}, u32[]{:S(2)}) %collective-permute-start.25) | collective-permute-done | bytes 262176 | tf_op jit(solution)/shard_map/ppermute | solution.py:36
  (66 shorter events, 7.8 us)
Async XLA Ops:
  2.3 5.8 %collective-permute-start = (bf16[272,256]{1,0:T(8,128)(2,1)S(1)}, bf16[272,256]{1,0:T(8,128)(2,1)S(1)}, u32[]{:S(2)}, u32[]{:S(2)}) collective-permute-start(bf16[272,256]{1,0:T(8,128)(2,1)S(1)} %pad_maximum_fusion.6), channel_id=1, source_target_pairs={{0,8},{8,0},{16,24},{24,16},{1,9},{9,1},{17,25},{25,17},{2,10},{10... | collective-permute-start | bytes 417800 | tf_op jit(solution)/shard_map/ppermute | solution.py:32
  4.4 7.7 %collective-permute-start.5 = (bf16[256,256]{1,0:T(8,128)(2,1)}, bf16[256,256]{1,0:T(8,128)(2,1)S(1)}, u32[]{:S(2)}, u32[]{:S(2)}) collective-permute-start(bf16[256,256]{1,0:T(8,128)(2,1)} %param.5), channel_id=1, source_target_pairs={{0,24},{8,16},{16,8},{24,0},{1,25},{9,17},{17,9},{25,1},{2,26},{10... | collective-permute-start | bytes 393224 | tf_op jit(solution)/shard_map/ppermute | solution.py:36
  9.0 14.3 %collective-permute-start.2 = (bf16[544,256]{1,0:T(8,128)(2,1)S(1)}, bf16[544,256]{1,0:T(8,128)(2,1)S(1)}, u32[]{:S(2)}, u32[]{:S(2)}) collective-permute-start(bf16[544,256]{1,0:T(8,128)(2,1)S(1)} %pad_maximum_fusion.5.refs_0_), channel_id=1, source_target_pairs={{0,6},{2,0},{4,2},{6,4},{1,7},{3,1},{5,3},{7,5},{8,14},{10,8},{12,... | collective-permute-start | bytes 835592 | tf_op jit(solution)/shard_map/ppermute | solution.py:28
  12.1 14.5 %collective-permute-start.1 = (bf16[544,256]{1,0:T(8,128)(2,1)S(1)}, bf16[544,256]{1,0:T(8,128)(2,1)S(1)}, u32[]{:S(2)}, u32[]{:S(2)}) collective-permute-start(bf16[544,256]{1,0:T(8,128)(2,1)S(1)} %pad_maximum_fusion.5.refs_0_), channel_id=1, source_target_pairs={{0,2},{2,4},{4,6},{6,0},{1,3},{3,5},{5,7},{7,1},{8,10},{10,12},{12... | collective-permute-start | bytes 835592 | tf_op jit(solution)/shard_map/ppermute | solution.py:28
  12.1 7.4 %collective-permute-start.7 = (bf16[512,256]{1,0:T(8,128)(2,1)S(1)}, bf16[512,256]{1,0:T(8,128)(2,1)S(1)}, u32[]{:S(2)}, u32[]{:S(2)}) collective-permute-start(bf16[512,256]{1,0:T(8,128)(2,1)S(1)} %constant_dynamic-update-slice_fusion.refs_5_), channel_id=1, source_target_pairs={{0,65},{64,0},{1,64},{65,1},{2,67},{66,2},{3,66},{67,3},{4,69},{68... | collective-permute-start | bytes 786440 | tf_op jit(solution)/shard_map/ppermute | solution.py:24
  14.9 11.4 %collective-permute-start.6 = (bf16[512,256]{1,0:T(8,128)(2,1)S(1)}, bf16[512,256]{1,0:T(8,128)(2,1)S(1)}, u32[]{:S(2)}, u32[]{:S(2)}) collective-permute-start(bf16[512,256]{1,0:T(8,128)(2,1)S(1)} %constant_dynamic-update-slice_fusion.refs_5_), channel_id=1, source_target_pairs={{0,64},{64,1},{1,65},{65,0},{2,66},{66,3},{3,67},{67,2},{4,68},{68... | collective-permute-start | bytes 786440 | tf_op jit(solution)/shard_map/ppermute | solution.py:24
  14.9 11.5 %collective-permute-start.10 = (bf16[512,256]{1,0:T(8,128)(2,1)S(1)}, bf16[512,256]{1,0:T(8,128)(2,1)S(1)}, u32[]{:S(2)}, u32[]{:S(2)}) collective-permute-start(bf16[512,256]{1,0:T(8,128)(2,1)S(1)} %constant_dynamic-update-slice_fusion.refs_5_), channel_id=1, source_target_pairs={{0,32},{32,0},{1,33},{33,1},{2,34},{34,2},{3,35},{35,3},{4,36},{36... | collective-permute-start | bytes 786440 | tf_op jit(solution)/shard_map/ppermute | solution.py:40
  19.5 7.5 %collective-permute-start.9 = (bf16[256,256]{1,0:T(8,128)(2,1)S(1)}, bf16[256,256]{1,0:T(8,128)(2,1)S(1)}, u32[]{:S(2)}, u32[]{:S(2)}) collective-permute-start(bf16[256,256]{1,0:T(8,128)(2,1)S(1)} %slice.161), channel_id=1, source_target_pairs={{0,65},{64,0},{1,64},{65,1},{2,67},{66,2},{3,66},{67,3},{4,69},{68... | collective-permute-start | bytes 393224 | tf_op jit(solution)/shard_map/ppermute | solution.py:24
  23.3 9.3 %collective-permute-start.4 = (bf16[272,256]{1,0:T(8,128)(2,1)S(1)}, bf16[272,256]{1,0:T(8,128)(2,1)S(1)}, u32[]{:S(2)}, u32[]{:S(2)}) collective-permute-start(bf16[272,256]{1,0:T(8,128)(2,1)S(1)} %slice.159), channel_id=1, source_target_pairs={{0,6},{2,0},{4,2},{6,4},{1,7},{3,1},{5,3},{7,5},{8,14},{10,8},{12,... | collective-permute-start | bytes 417800 | tf_op jit(solution)/shard_map/ppermute | solution.py:28
  26.3 6.2 %collective-permute-start.8 = (bf16[256,256]{1,0:T(8,128)(2,1)S(1)}, bf16[256,256]{1,0:T(8,128)(2,1)S(1)}, u32[]{:S(2)}, u32[]{:S(2)}) collective-permute-start(bf16[256,256]{1,0:T(8,128)(2,1)S(1)} %slice.160), channel_id=1, source_target_pairs={{0,64},{64,1},{1,65},{65,0},{2,66},{66,3},{3,67},{67,2},{4,68},{68... | collective-permute-start | bytes 393224 | tf_op jit(solution)/shard_map/ppermute | solution.py:24
  26.4 8.7 %collective-permute-start.12 = (bf16[512,256]{1,0:T(8,128)(2,1)S(1)}, bf16[512,256]{1,0:T(8,128)(2,1)S(1)}, u32[]{:S(2)}, u32[]{:S(2)}) collective-permute-start(bf16[512,256]{1,0:T(8,128)(2,1)S(1)} %collective-permute-done.7.refs_7_), channel_id=1, source_target_pairs={{0,32},{32,0},{1,33},{33,1},{2,34},{34,2},{3,35},{35,3},{4,36},{36... | collective-permute-start | bytes 786440 | tf_op jit(solution)/shard_map/ppermute | solution.py:40
  26.5 8.6 %collective-permute-start.11 = (bf16[512,256]{1,0:T(8,128)(2,1)S(1)}, bf16[512,256]{1,0:T(8,128)(2,1)S(1)}, u32[]{:S(2)}, u32[]{:S(2)}) collective-permute-start(bf16[512,256]{1,0:T(8,128)(2,1)S(1)} %collective-permute-done.6.refs_6_), channel_id=1, source_target_pairs={{0,32},{32,0},{1,33},{33,1},{2,34},{34,2},{3,35},{35,3},{4,36},{36... | collective-permute-start | bytes 786440 | tf_op jit(solution)/shard_map/ppermute | solution.py:40
  27.1 8.1 %collective-permute-start.3 = (bf16[272,256]{1,0:T(8,128)(2,1)S(1)}, bf16[272,256]{1,0:T(8,128)(2,1)S(1)}, u32[]{:S(2)}, u32[]{:S(2)}) collective-permute-start(bf16[272,256]{1,0:T(8,128)(2,1)S(1)} %slice.158), channel_id=1, source_target_pairs={{0,2},{2,4},{4,6},{6,0},{1,3},{3,5},{5,7},{7,1},{8,10},{10,12},{12... | collective-permute-start | bytes 417800 | tf_op jit(solution)/shard_map/ppermute | solution.py:28
  54.2 18.2 %collective-permute-start.20 = (f32[2,1024,256]{2,1,0:T(8,128)S(1)}, f32[2,1024,256]{2,1,0:T(8,128)S(1)}, u32[]{:S(2)}, u32[]{:S(2)}) collective-permute-start(f32[2,1024,256]{2,1,0:T(8,128)S(1)} %pad_maximum_fusion), channel_id=1, source_target_pairs={{0,32},{32,0},{1,33},{33,1},{2,34},{34,2},{3,35},{35,3},{4,36},{36... | collective-permute-start | bytes 6291464 | tf_op jit(solution)/shard_map/ppermute | solution.py:40
  54.4 10.0 %collective-permute-start.15 = (f32[256,256]{1,0:T(8,128)S(1)}, f32[256,256]{1,0:T(8,128)S(1)}, u32[]{:S(2)}, u32[]{:S(2)}) collective-permute-start(f32[256,256]{1,0:T(8,128)S(1)} %slice.129), channel_id=1, source_target_pairs={{0,2},{2,4},{4,6},{6,0},{1,3},{3,5},{5,7},{7,1},{8,10},{10,12},{12... | collective-permute-start | bytes 786440 | tf_op jit(solution)/shard_map/ppermute | solution.py:28
  64.4 8.0 %collective-permute-start.17 = (f32[256,256]{1,0:T(8,128)S(1)}, f32[256,256]{1,0:T(8,128)S(1)}, u32[]{:S(2)}, u32[]{:S(2)}) collective-permute-start(f32[256,256]{1,0:T(8,128)S(1)} %get-tuple-element.11), channel_id=1, source_target_pairs={{0,6},{2,0},{4,2},{6,4},{1,7},{3,1},{5,3},{7,5},{8,14},{10,8},{12,... | collective-permute-start | bytes 786440 | tf_op jit(solution)/shard_map/ppermute | solution.py:28
  64.6 19.8 %collective-permute-start.16 = (f32[512,256]{1,0:T(8,128)S(1)}, f32[512,256]{1,0:T(8,128)S(1)}, u32[]{:S(2)}, u32[]{:S(2)}) collective-permute-start(f32[512,256]{1,0:T(8,128)S(1)} %pad_maximum_fusion.1), channel_id=1, source_target_pairs={{0,2},{2,4},{4,6},{6,0},{1,3},{3,5},{5,7},{7,1},{8,10},{10,12},{12... | collective-permute-start | bytes 1572872 | tf_op jit(solution)/shard_map/ppermute | solution.py:28
  72.8 8.3 %collective-permute-start.21 = (f32[256,256]{1,0:T(8,128)S(1)}, f32[256,256]{1,0:T(8,128)S(1)}, u32[]{:S(2)}, u32[]{:S(2)}) collective-permute-start(f32[256,256]{1,0:T(8,128)S(1)} %get-tuple-element.16), channel_id=1, source_target_pairs={{0,64},{64,1},{1,65},{65,0},{2,66},{66,3},{3,67},{67,2},{4,68},{68... | collective-permute-start | bytes 786440 | tf_op jit(solution)/shard_map/ppermute | solution.py:24
  72.9 8.2 %collective-permute-start.23 = (f32[256,256]{1,0:T(8,128)S(1)}, f32[256,256]{1,0:T(8,128)S(1)}, u32[]{:S(2)}, u32[]{:S(2)}) collective-permute-start(f32[256,256]{1,0:T(8,128)S(1)} %get-tuple-element.17), channel_id=1, source_target_pairs={{0,65},{64,0},{1,64},{65,1},{2,67},{66,2},{3,66},{67,3},{4,69},{68... | collective-permute-start | bytes 786440 | tf_op jit(solution)/shard_map/ppermute | solution.py:24
  76.2 12.2 %collective-permute-start.18 = (f32[512,256]{1,0:T(8,128)S(1)}, f32[512,256]{1,0:T(8,128)S(1)}, u32[]{:S(2)}, u32[]{:S(2)}) collective-permute-start(f32[512,256]{1,0:T(8,128)S(1)} %pad_maximum_fusion.2), channel_id=1, source_target_pairs={{0,6},{2,0},{4,2},{6,4},{1,7},{3,1},{5,3},{7,5},{8,14},{10,8},{12,... | collective-permute-start | bytes 1572872 | tf_op jit(solution)/shard_map/ppermute | solution.py:28
  81.2 12.0 %collective-permute-start.24 = (f32[512,256]{1,0:T(8,128)S(1)}, f32[512,256]{1,0:T(8,128)S(1)}, u32[]{:S(2)}, u32[]{:S(2)}) collective-permute-start(f32[512,256]{1,0:T(8,128)S(1)} %pad_maximum_fusion.4), channel_id=1, source_target_pairs={{0,65},{64,0},{1,64},{65,1},{2,67},{66,2},{3,66},{67,3},{4,69},{68... | collective-permute-start | bytes 1572872 | tf_op jit(solution)/shard_map/ppermute | solution.py:24
  84.3 12.4 %collective-permute-start.22 = (f32[512,256]{1,0:T(8,128)S(1)}, f32[512,256]{1,0:T(8,128)S(1)}, u32[]{:S(2)}, u32[]{:S(2)}) collective-permute-start(f32[512,256]{1,0:T(8,128)S(1)} %pad_maximum_fusion.3), channel_id=1, source_target_pairs={{0,64},{64,1},{1,65},{65,0},{2,66},{66,3},{3,67},{67,2},{4,68},{68... | collective-permute-start | bytes 1572872 | tf_op jit(solution)/shard_map/ppermute | solution.py:24
  88.5 12.2 %collective-permute-start.19 = (f32[256,256]{1,0:T(8,128)S(1)}, f32[256,256]{1,0:T(8,128)S(1)}, u32[]{:S(2)}, u32[]{:S(2)}) collective-permute-start(f32[256,256]{1,0:T(8,128)S(1)} %slice.163), channel_id=1, source_target_pairs={{0,8},{8,0},{16,24},{24,16},{1,9},{9,1},{17,25},{25,17},{2,10},{10... | collective-permute-start | bytes 786440 | tf_op jit(solution)/shard_map/ppermute | solution.py:32
  96.9 8.1 %collective-permute-start.25 = (f32[256,256]{1,0:T(8,128)S(1)}, f32[256,256]{1,0:T(8,128)S(1)}, u32[]{:S(2)}, u32[]{:S(2)}) collective-permute-start(f32[256,256]{1,0:T(8,128)S(1)} %slice.174), channel_id=1, source_target_pairs={{0,24},{8,16},{16,8},{24,0},{1,25},{9,17},{17,9},{25,1},{2,26},{10... | collective-permute-start | bytes 786440 | tf_op jit(solution)/shard_map/ppermute | solution.py:36
  (4 other events, 55.7 us)

commit v2 on v0

v2 whole, which is shorter than its diff:
```python
import functools
import math

import jax
import jax.numpy as jnp
from jax import lax
from jax.experimental import pallas as pl
from jax.experimental.pallas import tpu as pltpu
from jax.sharding import Mesh, PartitionSpec as P

logit_scale = 2.0
logit_bias = -6.0
AXES = ("xl", "core", "z", "y", "xh")
ROWS = 256
NOTE = 16
PEAK = 32000.0
VMEM = pl.BlockSpec(memory_space=pltpu.VMEM)
SMEM = pl.BlockSpec(memory_space=pltpu.SMEM)


def member(xl, core, z, y, xh):
    return (((xl * 2 + core) * 4 + z) * 4 + y) * 2 + xh


def teams():
    out = []
    for pair in ((0, 1), (2, 3)):
        for x in range(4):
            out.append([member(x % 2, 0, z, y, x // 2) for z in pair for y in range(4)])
    for pair in ((0, 3), (1, 2)):
        for y in range(4):
            out.append([member(x % 2, 1, z, y, x // 2) for z in pair for x in range(4)])
    return out


def meet(value):
    return lax.all_to_all(value, AXES, 0, 0, axis_index_groups=teams(), tiled=True)


def swap_core(value):
    return lax.ppermute(value, "core", [(0, 1), (1, 0)])


def encode(block):
    top = jnp.maximum(jnp.max(jnp.abs(block), axis=0, keepdims=True), 2.0**-100)
    power = jnp.ceil(jnp.log2(top) * 128.0) + 1.0
    scaled = block * (PEAK * jnp.exp2(power * (-1.0 / 128.0)))
    return jnp.floor(scaled + 0.5).astype(jnp.int16), power


def decode(code, power):
    return code.astype(jnp.float32) * (jnp.exp2(power * (1.0 / 128.0)) * (1.0 / PEAK))


def notes(powers):
    powers = powers + [jnp.zeros((1, ROWS), jnp.float32)] * (NOTE - len(powers))
    return jnp.concatenate(powers, axis=0).astype(jnp.int16)


def source_of(marks, base, index):
    group = marks[base + index // 4]
    x = (index // 2) % 2 * 2 + group // 2
    return group, index % 2 * 4 + x


def score_kernel(factor, marks, mine, theirs, keep, send, a_all, labels, b_all, ga, gb):
    core, z, y = marks[0], marks[1], marks[2]

    def fill(a_from, a_start, b_from):
        for s in range(8):
            a_all[s * ROWS : (s + 1) * ROWS, :] = a_from[s, a_start : a_start + ROWS, :]
            note = a_from[s, a_start + ROWS : a_start + ROWS + NOTE, :].astype(jnp.float32)
            labels[:, s * ROWS : (s + 1) * ROWS] = (note[0:1] * 256.0 + note[1:2]).astype(jnp.int32)
            for c in range(2):
                start = c * (ROWS + NOTE)
                b_all[2 * s + c] = b_from[s, start : start + ROWS, :]

    @pl.when(core == 0)
    def _():
        fill(mine, 0, theirs)

    @pl.when(core == 1)
    def _():
        fill(theirs, ROWS + NOTE, mine)

    ga[...] = jnp.zeros_like(ga)
    half_scale = 0.5 * factor
    half_bias = 0.5 * logit_bias
    iota = lax.broadcasted_iota(jnp.int32, (ROWS, 8 * ROWS), 0)

    def block(index, carry):
        group, source = source_of(marks, 3, index)
        outer = jnp.logical_or(z == 0, z == 3)
        far = source // 4
        level = jnp.where(outer, 3 * far, 1 + far)
        first = group * 8192 + (level * 8 + y * 2 + source % 4 // 2) * ROWS
        which = source * 2 + group % 2
        keys = b_all[which]
        a = a_all[...]
        logits = lax.dot_general(
            keys, a, (((1,), (1,)), ((), ())), preferred_element_type=jnp.float32
        )
        hit = iota == labels[...] - first
        weights = 0.5 * jnp.tanh(logits * half_scale + half_bias) + jnp.where(hit, -0.5, 0.5)
        weights = weights.astype(jnp.bfloat16)
        gb[index] = jnp.dot(weights, a, preferred_element_type=jnp.float32)
        ga[...] += lax.dot_general(
            weights, keys, (((0,), (0,)), ((), ())), preferred_element_type=jnp.float32
        )
        return carry

    lax.fori_loop(0, 12, block, 0)

    @pl.when(core == 0)
    def _():
        powers = []
        for i in range(12):
            code, power = encode(gb[i])
            send[i * ROWS : (i + 1) * ROWS, :] = code
            powers.append(power)
        send[12 * ROWS :, :] = notes(powers)
        for i in range(8):
            keep[i] = ga[i * ROWS : (i + 1) * ROWS, :]

    @pl.when(core == 1)
    def _():
        powers = []
        for i in range(8):
            code, power = encode(ga[i * ROWS : (i + 1) * ROWS, :])
            send[i * ROWS : (i + 1) * ROWS, :] = code
            powers.append(power)
        send[12 * ROWS :, :] = notes(powers)
        for i in range(12):
            keep[i] = gb[i]


def pack_kernel(marks, keep, got, out, total):
    core = marks[0]

    @pl.when(core == 0)
    def _():
        for s in range(8):
            code, power = encode(keep[s])
            out[s, 0:ROWS, :] = code
            out[s, ROWS : 2 * ROWS, :] = got[s * ROWS : (s + 1) * ROWS, :]
            other = got[12 * ROWS :, :].astype(jnp.float32)[s : s + 1]
            out[s, 2 * ROWS :, :] = notes([power, other])

    @pl.when(core == 1)
    def _():
        for group in range(4):
            for i in range(4):
                total[group * 4 + i] = jnp.zeros((ROWS, ROWS), jnp.float32)
        for i in range(12):
            group = marks[3 + i // 4]
            total[group * 4 + i % 4] += keep[i]
        powers = got[12 * ROWS :, :].astype(jnp.float32)
        for i in range(12):
            group = marks[7 + i // 4]
            total[group * 4 + i % 4] += decode(got[i * ROWS : (i + 1) * ROWS, :], powers[i : i + 1])
        for s in range(8):
            x, far = s % 4, s // 4
            powers = []
            for c in range(2):
                code, power = encode(total[(x % 2 * 2 + c) * 4 + x // 2 * 2 + far])
                out[s, c * ROWS : (c + 1) * ROWS, :] = code
                powers.append(power)
            out[s, 2 * ROWS :, :] = notes(powers)


def sum_kernel(factor, marks, got, keep, send):
    core = marks[0]
    sums = [jnp.zeros((ROWS, ROWS), jnp.float32) for _ in range(2)]
    for s in range(8):
        powers = got[s, 2 * ROWS :, :].astype(jnp.float32)
        for c in range(2):
            sums[c] += decode(got[s, c * ROWS : (c + 1) * ROWS, :], powers[c : c + 1])
    first, second = sums[0] * factor, sums[1] * factor
    keep[...] = jnp.where(core == 0, first, second)
    send[...] = jnp.where(core == 0, second, first)


def call(kernel, shapes, scratch, flops, *operands):
    return pl.pallas_call(
        kernel,
        out_shape=shapes,
        in_specs=[SMEM] + [VMEM] * (len(operands) - 1),
        out_specs=jax.tree.map(lambda _: VMEM, shapes),
        scratch_shapes=scratch,
        compiler_params=pltpu.CompilerParams(vmem_limit_bytes=40 << 20),
        cost_estimate=pl.CostEstimate(flops=flops, bytes_accessed=8 << 20, transcendentals=0),
    )(*operands)


def shards(views_a, views_b, positives, plan):
    factor = logit_scale / math.sqrt(views_a.shape[1])
    xl, core = lax.axis_index("xl"), lax.axis_index("core")
    group = xl * 2 + core
    mate = group ^ 1
    marks = [core, lax.axis_index("z"), lax.axis_index("y")]
    marks += [group, plan[0, group], plan[1, group], group, mate, plan[0, mate], plan[1, mate]]
    marks = jnp.stack([v.astype(jnp.int32) for v in marks])

    note = jnp.stack([positives // 256, positives % 256]).astype(jnp.bfloat16)
    note = jnp.pad(note, ((0, NOTE - 2), (0, 0)))
    a_own = jnp.concatenate([views_a, note])
    b_own = jnp.pad(views_b, ((0, NOTE), (0, 0)))
    got = swap_core(jnp.where(core == 0, b_own, a_own))
    one = jnp.where(core == 0, a_own, got)
    two = jnp.where(core == 0, got, b_own)
    pair = jnp.concatenate([one, two])
    mine = meet(jnp.tile(pair[None], (8, 1, 1)))
    theirs = swap_core(mine)

    f32, i16 = jnp.float32, jnp.int16
    keep, send = call(
        functools.partial(score_kernel, factor),
        (
            jax.ShapeDtypeStruct((12, ROWS, ROWS), f32),
            jax.ShapeDtypeStruct((12 * ROWS + NOTE, ROWS), i16),
        ),
        [
            pltpu.VMEM((8 * ROWS, ROWS), jnp.bfloat16),
            pltpu.VMEM((1, 8 * ROWS), jnp.int32),
            pltpu.VMEM((16, ROWS, ROWS), jnp.bfloat16),
            pltpu.VMEM((8 * ROWS, ROWS), f32),
            pltpu.VMEM((12, ROWS, ROWS), f32),
        ],
        2 * 3 * 2048 * 3072 * 256,
        marks,
        mine,
        theirs,
    )
    packed = call(
        pack_kernel,
        jax.ShapeDtypeStruct((8, 2 * ROWS + NOTE, ROWS), i16),
        [pltpu.VMEM((16, ROWS, ROWS), f32)],
        1 << 20,
        marks,
        keep,
        swap_core(send),
    )
    keep, send = call(
        functools.partial(sum_kernel, factor),
        (jax.ShapeDtypeStruct((ROWS, ROWS), f32), jax.ShapeDtypeStruct((ROWS, ROWS), f32)),
        [],
        1 << 20,
        marks,
        meet(packed),
    )
    got = swap_core(send)
    return jnp.where(core == 0, keep, got), jnp.where(core == 0, got, keep)


def solution(mesh):
    fine = Mesh(mesh.devices.reshape(2, 2, 4, 4, 2), AXES)
    split = P(AXES, None)
    return jax.shard_map(
        shards,
        mesh=fine,
        in_specs=(split, split, P(AXES), P()),
        out_specs=(split, split),
        check_vma=False,
    )
```

time: 941 us -> 85.1 us (0.09)
  waiting for transfers between devices: 855 us -> 6.73 us
  matrix products: 39 us -> 0 us
  blocking collectives: 8.73 us -> 47.3 us
  Pallas kernels: 0 us -> 20.9 us
  between operations: 20.8 us -> 0.71 us
  local copies, waits for them, and re-layouts: 14.3 us -> 3.47 us
    reduce_scatter x4 -> x0, waiting for transfers between devices: 635 us -> none  [the longest x3 592 us: score_group(): lax.psum_scatter(grad_keys, 'dev', scatter_dimension=0, tiled=True)]
    all_gather x3 -> x0, waiting for transfers between devices: 219 us -> none  [score_group(): piece = lax.all_gather(key_shard, 'dev', axis=0, tiled=True)]
    all_to_all x0 -> x2, blocking collectives: none -> 47.3 us  [meet(): lax.all_to_all(value, AXES, 0, 0, axis_index_groups=teams(), tiled=True)]
    dot_general x9 -> x0, matrix products: 39 us -> none  [the longest x3 17.3 us: weights_for(): lax.dot_general(queries, keys, (((1,), (1,)), ((), ())), preferred_elemen...]
    pallas_call x0 -> x3, Pallas kernels: none -> 20.9 us  [call(): pl.pallas_call(kernel, out_shape=shapes, in_specs=[SMEM] + [VMEM] * (len(...]
    unnamed x20 -> x2, local copies, waits for them, and re-layouts: 10.3 us -> 0.01 us
  transfers between devices with their start and end apart: 7 -> 4, of which waited for: 7 -> 4; matrix products, arithmetic and copies ran while one was open for 4% -> 4% of each run, Pallas kernels for 0% -> 0%
where the time goes in v2:
time: 85.1 us; the launch traced here: 84.8 us
  blocking collectives  47.3 us (56%)
  Pallas kernels  20.9 us (25%)
  waiting for transfers between devices  6.73 us (8%)
  other arithmetic  3.59 us (4%)
  local copies, waits for them, and re-layouts  3.47 us (4%)
  starting transfers between devices  2.07 us (2%)
    all_to_all x2, blocking collectives, meet(): lax.all_to_all(value, AXES, 0, 0, axis_index_groups=teams(), tiled=True)  47.3 us
    pallas_call x3, Pallas kernels, call(): pl.pallas_call(kernel, out_shape=shapes, in_specs=[SMEM] + [VMEM] * (len(...  20.9 us
    ppermute x4, waiting for transfers between devices, swap_core(): return lax.ppermute(value, 'core', [(0, 1), (1, 0)])  6.73 us
    another operation x1, local copies, waits for them, and re-layouts, shards(): marks = jnp.stack([v.astype(jnp.int32) for v in marks])  2.64 us
    ppermute x4, starting transfers between devices, swap_core(): return lax.ppermute(value, 'core', [(0, 1), (1, 0)])  2.07 us
  transfers between devices with their start and end apart: 4, of which 4 were waited for; matrix products, arithmetic and copies ran while one was open for 4% of the time, Pallas kernels for 0%

profile of v2, /device:TPU:1, one launch (start us, length us, event | category | flops | bytes accessed | tf_op | source)
XLA Modules:
  0.0 84.8 jit_solution(1328980750236322252)
XLA Ops:
  0.6 0.7 fusion.4
  1.4 1.0 %broadcast_select_fusion.2 = bf16[272,256]{1,0:T(8,128)(2,1)S(1)} fusion(pred[]{:T(512)S(6)} %eq.4, bf16[256,256]{1,0:T(8,128)(2,1)} %param.5, bf16[16,256]{1,0:T(8,128)(2,1)S(1)} %fusion.2, bf16[256,256]{1,0:T(8,128)(2,1)} %param.4), kind=kLoop, calls=%fused_computation.4 | loop fusion | flops 348160 | bytes 409601 | tf_op jit(solution)/shard_map/jit(_where)/select_n | solution.py:208
  2.4 1.5 %collective-permute-start = (bf16[272,256]{1,0:T(8,128)(2,1)S(1)}, bf16[272,256]{1,0:T(8,128)(2,1)S(1)}, u32[]{:S(2)}, u32[]{:S(2)}) collective-permute-start(bf16[272,256]{1,0:T(8,128)(2,1)S(1)} %broadcast_select_fusion.2), channel_id=1, source_target_pairs={{0,32},{32,0},{1,33},{33,1},{2,34},{34,2},{3,35},{35,3},{4,36},{36... | collective-permute-start | bytes 417800 | tf_op jit(solution)/shard_map/ppermute | solution.py:41
  3.9 1.0 %collective-permute-done = bf16[272,256]{1,0:T(8,128)(2,1)S(1)} collective-permute-done((bf16[272,256]{1,0:T(8,128)(2,1)S(1)}, bf16[272,256]{1,0:T(8,128)(2,1)S(1)}, u32[]{:S(2)}, u32[]{:S(2)}) %collective-permute-start) | collective-permute-done | bytes 139296 | tf_op jit(solution)/shard_map/ppermute | solution.py:41
  4.9 1.0 %broadcast_select_fusion.1 = (bf16[272,256]{1,0:T(8,128)(2,1)S(1)}, bf16[272,256]{1,0:T(8,128)(2,1)S(1)}) fusion(bf16[272,256]{1,0:T(8,128)(2,1)S(1)} %collective-permute-done, pred[]{:T(512)S(6)} %eq.4, bf16[16,256]{1,0:T(8,128)(2,1)S(1)} %fusion.2, bf16[256,256]{1,0:T(8,128)(2,1)} %param.4, bf16[256,256]{1,0:T(8,128)(2,1)} %param.5), kind=kLoop, calls=%fused_computation.3 | loop fusion | flops 417792 | bytes 688129 | tf_op jit(solution)/shard_map/jit(_where)/select_n | solution.py:209
  5.9 0.1 tile.2
  6.1 0.0 copy-start
  6.1 25.3 %all_to_all.10.mine = bf16[8,544,256]{2,1,0:T(8,128)(2,1)S(1)} all-to-all(bf16[8,544,256]{2,1,0:T(8,128)(2,1)S(1)} %tile.2), channel_id=1, replica_groups={{0,2,4,6,8,10,12,14},{64,66,68,70,72,74,76,78},{1,3,5,7,9,11,13,15},{65..., dimensions={0} | all-to-all | bytes 4456448 | tf_op jit(solution)/shard_map/all_to_all | solution.py:37
  31.4 0.0 collective-permute-start.1
  31.4 0.0 copy-done
  31.4 0.7 constant_dynamic-slice_fusion
  32.0 2.6 %stack.36.marks = s32[10]{0:T(128)S(1)} concatenate(s32[1]{0:T(128)} %bitcast, s32[1]{0:T(128)} %bitcast.1, s32[1]{0:T(128)} %bitcast.2, s32[1]{0:T(128)} %bitcast.3, s32[1]{0:T(128)} %bitcast.4, s32[1]{0:T(128)} %bitcast.5, s32[1]{0:T(128)} %bitcast.3, s32[1]{0:T(128)} %bitcast.6, s32[1]{0:T(128)} %bitcast.7, s32[1]{0:T(128)} %bitcast.8), dimensions={0} | concatenate | bytes 80 | tf_op jit(solution)/shard_map/stack | solution.py:202
  34.7 1.2 %collective-permute-done.1.theirs = bf16[8,544,256]{2,1,0:T(8,128)(2,1)} collective-permute-done((bf16[8,544,256]{2,1,0:T(8,128)(2,1)S(1)}, bf16[8,544,256]{2,1,0:T(8,128)(2,1)}, u32[]{:S(2)}, u32[]{:S(2)}) %collective-permute-start.1) | collective-permute-done | bytes 2228256 | tf_op jit(solution)/shard_map/ppermute | solution.py:41
  35.8 16.7 %shard_map.59 = (f32[12,256,256]{2,1,0:T(8,128)S(1)}, s16[3088,256]{1,0:T(8,128)(2,1)S(1)}) custom-call(s32[10]{0:T(128)S(1)} %stack.36.marks, bf16[8,544,256]{2,1,0:T(8,128)(2,1)S(1)} %all_to_all.10.mine, bf16[8,544,256]{2,1,0:T(8,128)(2,1)} %collective-permute-done.1.theirs), custom_call_target="tpu_custom_call" | custom-call | flops 9663676416 | bytes 8388608 | tf_op jit(solution)/shard_map/pallas_call | solution.py:184
  52.5 0.5 collective-permute-start.2
  53.0 3.0 %collective-permute-done.2.got = s16[3088,256]{1,0:T(8,128)(2,1)S(1)} collective-permute-done((s16[3088,256]{1,0:T(8,128)(2,1)S(1)}, s16[3088,256]{1,0:T(8,128)(2,1)S(1)}, u32[]{:S(2)}, u32[]{:S(2)}) %collective-permute-start.2) | collective-permute-done | bytes 1581088 | tf_op jit(solution)/shard_map/ppermute | solution.py:41
  56.0 3.1 %shard_map.60 = s16[8,528,256]{2,1,0:T(8,128)(2,1)S(1)} custom-call(s32[10]{0:T(128)S(1)} %stack.36.marks, f32[12,256,256]{2,1,0:T(8,128)S(1)} %get-tuple-element.6.keep, s16[3088,256]{1,0:T(8,128)(2,1)S(1)} %collective-permute-done.2.got), custom_call_target="tpu_custom_call" | custom-call | flops 1048576 | bytes 8388608 | tf_op jit(solution)/shard_map/pallas_call | solution.py:184
  59.1 22.1 %all_to_all.11.got = s16[8,528,256]{2,1,0:T(8,128)(2,1)S(1)} all-to-all(s16[8,528,256]{2,1,0:T(8,128)(2,1)S(1)} %shard_map.60), channel_id=1, replica_groups={{0,2,4,6,8,10,12,14},{64,66,68,70,72,74,76,78},{1,3,5,7,9,11,13,15},{65..., dimensions={0} | all-to-all | bytes 4325376 | tf_op jit(solution)/shard_map/all_to_all | solution.py:37
  81.2 1.2 %shard_map.61 = (f32[256,256]{1,0:T(8,128)S(1)}, f32[256,256]{1,0:T(8,128)S(1)}) custom-call(s32[10]{0:T(128)S(1)} %stack.36.marks, s16[8,528,256]{2,1,0:T(8,128)(2,1)S(1)} %all_to_all.11.got), custom_call_target="tpu_custom_call" | custom-call | flops 1048576 | bytes 8388608 | tf_op jit(solution)/shard_map/pallas_call | solution.py:184
  82.4 0.1 collective-permute-start.3
  82.5 1.5 %collective-permute-done.3 = f32[256,256]{1,0:T(8,128)S(1)} collective-permute-done((f32[256,256]{1,0:T(8,128)S(1)}, f32[256,256]{1,0:T(8,128)S(1)}, u32[]{:S(2)}, u32[]{:S(2)}) %collective-permute-start.3) | collective-permute-done | bytes 262176 | tf_op jit(solution)/shard_map/ppermute | solution.py:41
  84.0 0.8 broadcast_select_fusion.3
  (4 shorter events, 0.0 us)
Async XLA Ops:
  2.4 2.5 %collective-permute-start = (bf16[272,256]{1,0:T(8,128)(2,1)S(1)}, bf16[272,256]{1,0:T(8,128)(2,1)S(1)}, u32[]{:S(2)}, u32[]{:S(2)}) collective-permute-start(bf16[272,256]{1,0:T(8,128)(2,1)S(1)} %broadcast_select_fusion.2), channel_id=1, source_target_pairs={{0,32},{32,0},{1,33},{33,1},{2,34},{34,2},{3,35},{35,3},{4,36},{36... | collective-permute-start | bytes 417800 | tf_op jit(solution)/shard_map/ppermute | solution.py:41
  6.1 25.3 %copy-start = (s32[2,4]{1,0:T(2,128)S(1)}, s32[2,4]{1,0:T(2,128)}, u32[]{:S(2)}) copy-start(s32[2,4]{1,0:T(2,128)} %param.7) | copy-start | bytes 100
  31.4 4.5 %collective-permute-start.1 = (bf16[8,544,256]{2,1,0:T(8,128)(2,1)S(1)}, bf16[8,544,256]{2,1,0:T(8,128)(2,1)}, u32[]{:S(2)}, u32[]{:S(2)}) collective-permute-start(bf16[8,544,256]{2,1,0:T(8,128)(2,1)S(1)} %all_to_all.10.mine), channel_id=1, source_target_pairs={{0,32},{32,0},{1,33},{33,1},{2,34},{34,2},{3,35},{35,3},{4,36},{36... | collective-permute-start | bytes 6684680 | tf_op jit(solution)/shard_map/ppermute | solution.py:41
  52.5 3.5 %collective-permute-start.2 = (s16[3088,256]{1,0:T(8,128)(2,1)S(1)}, s16[3088,256]{1,0:T(8,128)(2,1)S(1)}, u32[]{:S(2)}, u32[]{:S(2)}) collective-permute-start(s16[3088,256]{1,0:T(8,128)(2,1)S(1)} %get-tuple-element.7), channel_id=1, source_target_pairs={{0,32},{32,0},{1,33},{33,1},{2,34},{34,2},{3,35},{35,3},{4,36},{36... | collective-permute-start | bytes 4743176 | tf_op jit(solution)/shard_map/ppermute | solution.py:41
  82.4 1.6 %collective-permute-start.3 = (f32[256,256]{1,0:T(8,128)S(1)}, f32[256,256]{1,0:T(8,128)S(1)}, u32[]{:S(2)}, u32[]{:S(2)}) collective-permute-start(f32[256,256]{1,0:T(8,128)S(1)} %get-tuple-element.9), channel_id=1, source_target_pairs={{0,32},{32,0},{1,33},{33,1},{2,34},{34,2},{3,35},{35,3},{4,36},{36... | collective-permute-start | bytes 786440 | tf_op jit(solution)/shard_map/ppermute | solution.py:41

commit v3 on v2

v3 whole, which is shorter than its diff:
```python
import functools
import math

import jax
import jax.numpy as jnp
from jax import lax
from jax.experimental import pallas as pl
from jax.experimental.pallas import tpu as pltpu
from jax.sharding import Mesh, PartitionSpec as P

logit_scale = 2.0
logit_bias = -6.0
AXES = ("xl", "core", "z", "y", "xh")
ROWS = 256
NOTE = 16
PEAK = 32000.0
VMEM = pl.BlockSpec(memory_space=pltpu.VMEM)
SMEM = pl.BlockSpec(memory_space=pltpu.SMEM)


def member(xl, core, z, y, xh):
    return (((xl * 2 + core) * 4 + z) * 4 + y) * 2 + xh


def teams():
    out = []
    for pair in ((0, 1), (2, 3)):
        for x in range(4):
            out.append([member(x % 2, 0, z, y, x // 2) for z in pair for y in range(4)])
    for pair in ((0, 3), (1, 2)):
        for y in range(4):
            out.append([member(x % 2, 1, z, y, x // 2) for z in pair for x in range(4)])
    return out


def meet(value):
    return lax.all_to_all(value, AXES, 0, 0, axis_index_groups=teams(), tiled=True)


def swap_core(value):
    return lax.ppermute(value, "core", [(0, 1), (1, 0)])


def encode(block):
    top = jnp.maximum(jnp.max(jnp.abs(block), axis=0, keepdims=True), 2.0**-100)
    power = jnp.ceil(jnp.log2(top) * 128.0) + 1.0
    scaled = block * (PEAK * jnp.exp2(power * (-1.0 / 128.0)))
    return jnp.floor(scaled + 0.5).astype(jnp.int16), power


def decode(code, power):
    return code.astype(jnp.float32) * (jnp.exp2(power * (1.0 / 128.0)) * (1.0 / PEAK))


def notes(powers):
    powers = powers + [jnp.zeros((1, ROWS), jnp.float32)] * (NOTE - len(powers))
    return jnp.concatenate(powers, axis=0).astype(jnp.int16)


def build_kernel(marks, a, b, ids, a_got, b_got, ids_got, out):
    core = marks[0]

    def note(ref):
        value = ref[...]
        high, low = lax.shift_right_logical(value, 8), value & 255
        rows = [high.astype(jnp.float32), low.astype(jnp.float32)]
        rows += [jnp.zeros((NOTE - 2, ROWS), jnp.float32)]
        return jnp.concatenate(rows, axis=0).astype(jnp.bfloat16)

    def write(one, two, one_note, two_note):
        for s in range(8):
            out[s, 0:ROWS, :] = one[...]
            out[s, ROWS : ROWS + NOTE, :] = one_note
            out[s, ROWS + NOTE : 2 * ROWS + NOTE, :] = two[...]
            out[s, 2 * ROWS + NOTE :, :] = two_note

    @pl.when(core == 0)
    def _():
        write(a, a_got, note(ids), note(ids_got))

    @pl.when(core == 1)
    def _():
        nothing = jnp.zeros((NOTE, ROWS), jnp.bfloat16)
        write(b_got, b, nothing, nothing)


def score_kernel(factor, half, marks, mine, theirs, *refs):
    sums, send, a_all, labels, b_all = refs[-5:]
    core, z, y = marks[0], marks[1], marks[2]

    def fill(a_from, a_start, b_from):
        for s in range(a_from.shape[0]):
            a_all[s * ROWS : (s + 1) * ROWS, :] = a_from[s, a_start : a_start + ROWS, :]
            note = a_from[s, a_start + ROWS : a_start + ROWS + NOTE, :].astype(jnp.float32)
            labels[:, s * ROWS : (s + 1) * ROWS] = (note[0:1] * 256.0 + note[1:2]).astype(jnp.int32)
        for s in range(b_from.shape[0]):
            for c in range(2):
                start = c * (ROWS + NOTE)
                x, level = s % 4, s // 4
                to = (level * 4 + x % 2 * 2 + c) * 2 + x // 2
                b_all[to] = b_from[s, start : start + ROWS, :]

    @pl.when(core == 0)
    def _():
        fill(mine, 0, theirs)

    @pl.when(core == 1)
    def _():
        fill(theirs, ROWS + NOTE, mine)

    if half == 0:
        sums[...] = jnp.zeros_like(sums)
    else:
        sums[12:18] = jnp.zeros((6, ROWS, ROWS), jnp.float32)
    half_scale = 0.5 * factor
    half_bias = 0.5 * logit_bias
    wide, deep = 4 * ROWS, 2 * ROWS
    iota = lax.broadcasted_iota(jnp.int32, (deep, wide), 0)
    first = core == 0
    outer = jnp.logical_or(z == 0, z == 3)

    for tile in range(6):
        unit, slot = tile // 3, tile % 3
        group = marks[3 + slot]
        far = jnp.where(first, half, unit)
        level = jnp.where(outer, 3 * far, 1 + far)
        a_rows = pl.ds(pl.multiple_of(jnp.where(first, unit, 0) * wide, wide), wide)
        keys = b_all[pl.ds((jnp.where(first, 0, unit) * 4 + group) * 2, 2)].reshape(deep, ROWS)
        a = a_all[a_rows, :]
        ids = labels[:, a_rows]
        ids = jnp.where(lax.shift_right_logical(ids, 9) == group * 16 + level * 4 + y, ids & 511, -1)
        logits = lax.dot_general(
            keys, a, (((1,), (1,)), ((), ())), preferred_element_type=jnp.float32
        )
        weights = 0.5 * jnp.tanh(logits * half_scale + half_bias) + jnp.where(iota == ids, -0.5, 0.5)
        weights = weights.astype(jnp.bfloat16)
        gb = jnp.dot(weights, a, preferred_element_type=jnp.float32)
        ga = lax.dot_general(
            weights, keys, (((0,), (0,)), ((), ())), preferred_element_type=jnp.float32
        )
        gb_at = pl.ds(jnp.where(first, 12 + slot * 2, slot * 4 + unit * 2), 2)
        ga_at = pl.ds(jnp.where(first, unit * 4, 12), 4)
        sums[gb_at] += gb.reshape(2, ROWS, ROWS)
        sums[ga_at] += ga.reshape(4, ROWS, ROWS)

    powers = []
    for i in range(6):
        code, power = encode(sums[12 + i])
        send[i * ROWS : (i + 1) * ROWS, :] = code
        powers.append(power)
    send[6 * ROWS :, :] = notes(powers)


def place_in(marks, base, group):
    one, two = marks[base + 1] == group, marks[base + 2] == group
    used = jnp.logical_or(marks[base] == group, jnp.logical_or(one, two))
    return jnp.where(one, 1, jnp.where(two, 2, 0)), jnp.where(used, 1.0, 0.0)


def pack_kernel(marks, sums, got_near, got_far, out, total, powers):
    core = marks[0]
    for far, got in enumerate((got_near, got_far)):
        powers[far] = got[6 * ROWS :, :].astype(jnp.float32)

    @pl.when(core == 0)
    def _():
        for s in range(8):
            got, i = (got_near, got_far)[s // 4], s % 4
            code, power = encode(sums[s])
            out[s, 0:ROWS, :] = code
            out[s, ROWS : 2 * ROWS, :] = got[i * ROWS : (i + 1) * ROWS, :]
            out[s, 2 * ROWS :, :] = notes([power, powers[s // 4, i : i + 1, :]])

    @pl.when(core == 1)
    def _():
        for s in range(8):
            far, got = s // 4, (got_near, got_far)[s // 4]
            written = []
            for c in range(2):
                group, xh = s % 2 * 2 + c, s % 4 // 2
                own_slot, own_used = place_in(marks, 3, group)
                slot, used = place_in(marks, 6, group)
                own = sums[own_slot * 4 + far * 2 + xh]
                index = slot * 2 + xh
                power = powers[far, pl.ds(index, 1), :]
                scale = jnp.exp2(power * (1.0 / 128.0)) * (used * (1.0 / PEAK))
                code = got[pl.ds(pl.multiple_of(index * ROWS, ROWS), ROWS), :]
                total[...] = own * own_used + code.astype(jnp.float32) * scale
                code, power = encode(total[...])
                out[s, c * ROWS : (c + 1) * ROWS, :] = code
                written.append(power)
            out[s, 2 * ROWS :, :] = notes(written)


def sum_kernel(factor, marks, got, keep, send):
    core = marks[0]
    sums = [jnp.zeros((ROWS, ROWS), jnp.float32) for _ in range(2)]
    for s in range(8):
        powers = got[s, 2 * ROWS :, :].astype(jnp.float32)
        for c in range(2):
            sums[c] += decode(got[s, c * ROWS : (c + 1) * ROWS, :], powers[c : c + 1])
    first, second = sums[0] * factor, sums[1] * factor
    keep[...] = jnp.where(core == 0, first, second)
    send[...] = jnp.where(core == 0, second, first)


def call(kernel, shapes, scratch, flops, *operands, aliases={}):
    return pl.pallas_call(
        kernel,
        out_shape=shapes,
        in_specs=[SMEM] + [VMEM] * (len(operands) - 1),
        out_specs=jax.tree.map(lambda _: VMEM, shapes),
        scratch_shapes=scratch,
        input_output_aliases=aliases,
        compiler_params=pltpu.CompilerParams(vmem_limit_bytes=36 << 20),
        cost_estimate=pl.CostEstimate(flops=flops, bytes_accessed=8 << 20, transcendentals=0),
    )(*operands)


def shards(views_a, views_b, positives, plan):
    factor = logit_scale / math.sqrt(views_a.shape[1])
    xl, core = lax.axis_index("xl"), lax.axis_index("core")
    group = xl * 2 + core
    mate = group ^ 1
    marks = [core, lax.axis_index("z"), lax.axis_index("y"), group, plan[0, group], plan[1, group]]
    marks += [mate, plan[0, mate], plan[1, mate]]
    marks = jnp.stack([v.astype(jnp.int32) for v in marks])

    f32, i16, bf16 = jnp.float32, jnp.int16, jnp.bfloat16
    ids = positives.reshape(1, ROWS)
    shared = call(
        build_kernel,
        jax.ShapeDtypeStruct((8, 2 * (ROWS + NOTE), ROWS), bf16),
        [],
        1 << 20,
        marks,
        views_a,
        views_b,
        ids,
        swap_core(views_a),
        swap_core(views_b),
        swap_core(ids),
    )
    mine = meet(shared)
    near, far = swap_core(mine[:4]), swap_core(mine[4:])

    def score(half, theirs, *sums):
        return call(
            functools.partial(score_kernel, factor, half),
            (
                jax.ShapeDtypeStruct((18, ROWS, ROWS), f32),
                jax.ShapeDtypeStruct((6 * ROWS + NOTE, ROWS), i16),
            ),
            [
                pltpu.VMEM((8 * ROWS, ROWS), bf16),
                pltpu.VMEM((1, 8 * ROWS), jnp.int32),
                pltpu.VMEM((16, ROWS, ROWS), bf16),
            ],
            3 * 2048 * 3072 * 256,
            marks,
            mine,
            theirs,
            *sums,
            aliases={3: 0} if sums else {},
        )

    sums, send_near = score(0, near)
    got_near = swap_core(send_near)
    sums, send_far = score(1, far, sums)
    packed = call(
        pack_kernel,
        jax.ShapeDtypeStruct((8, 2 * ROWS + NOTE, ROWS), i16),
        [pltpu.VMEM((ROWS, ROWS), f32), pltpu.VMEM((2, NOTE, ROWS), f32)],
        1 << 20,
        marks,
        sums,
        got_near,
        swap_core(send_far),
    )
    keep, send = call(
        functools.partial(sum_kernel, factor),
        (jax.ShapeDtypeStruct((ROWS, ROWS), f32), jax.ShapeDtypeStruct((ROWS, ROWS), f32)),
        [],
        1 << 20,
        marks,
        meet(packed),
    )
    got = swap_core(send)
    return jnp.where(core == 0, keep, got), jnp.where(core == 0, got, keep)


def solution(mesh):
    fine = Mesh(mesh.devices.reshape(2, 2, 4, 4, 2), AXES)
    split = P(AXES, None)
    return jax.shard_map(
        shards,
        mesh=fine,
        in_specs=(split, split, P(AXES), P()),
        out_specs=(split, split),
        check_vma=False,
    )
```

time: 85.1 us -> 87.4 us (1.027)
  local copies, waits for them, and re-layouts: 3.47 us -> 6.71 us
  other arithmetic: 3.59 us -> 0.83 us
  Pallas kernels: 20.9 us -> 22.1 us
  starting transfers between devices: 2.07 us -> 3.27 us
    unnamed x2 -> x6, local copies, waits for them, and re-layouts: 0.01 us -> 2.48 us
    select_n x2 -> x0, other arithmetic: 2.04 us -> none  [the longest x1 1.03 us: shards(): one = jnp.where(core == 0, a_own, got)]
    ppermute x4 -> x8, starting transfers between devices: 2.07 us -> 3.27 us  [swap_core(): return lax.ppermute(value, 'core', [(0, 1), (1, 0)])]
    pallas_call x3 -> x5, Pallas kernels: 20.9 us -> 22.1 us  [call(): pl.pallas_call(kernel, out_shape=shapes, in_specs=[SMEM] + [VMEM] * (len(...]
    ppermute x4 -> x8, waiting for transfers between devices: 6.73 us -> 6.69 us  [swap_core(): return lax.ppermute(value, 'core', [(0, 1), (1, 0)])]
  transfers between devices with their start and end apart: 4 -> 8, of which waited for: 4 -> 4; matrix products, arithmetic and copies ran while one was open for 4% -> 5% of each run, Pallas kernels for 0% -> 10%
where the time goes in v3:
time: 87.4 us; the launch traced here: 87.1 us
  blocking collectives  46.8 us (54%)
  Pallas kernels  22.1 us (25%)
  local copies, waits for them, and re-layouts  6.71 us (8%)
  waiting for transfers between devices  6.69 us (8%)
  starting transfers between devices  3.27 us (4%)
    all_to_all x2, blocking collectives, meet(): lax.all_to_all(value, AXES, 0, 0, axis_index_groups=teams(), tiled=True)  46.8 us
    pallas_call x5, Pallas kernels, call(): pl.pallas_call(kernel, out_shape=shapes, in_specs=[SMEM] + [VMEM] * (len(...  22.1 us
    ppermute x8, waiting for transfers between devices, swap_core(): return lax.ppermute(value, 'core', [(0, 1), (1, 0)])  6.69 us
    ppermute x8, starting transfers between devices, swap_core(): return lax.ppermute(value, 'core', [(0, 1), (1, 0)])  3.27 us
    another operation x1, local copies, waits for them, and re-layouts, shards(): marks = jnp.stack([v.astype(jnp.int32) for v in marks])  2.58 us
    unnamed x6, local copies, waits for them, and re-layouts  2.48 us
  transfers between devices with their start and end apart: 8, of which 4 were waited for; matrix products, arithmetic and copies ran while one was open for 5% of the time, Pallas kernels for 10%

profile of v3, /device:TPU:1, one launch (start us, length us, event | category | flops | bytes accessed | tf_op | source)
XLA Modules:
  0.0 87.1 jit_solution(14221569897817243306)
XLA Ops:
  0.6 1.5 %collective-permute-start = (bf16[256,256]{1,0:T(8,128)(2,1)}, bf16[256,256]{1,0:T(8,128)(2,1)S(1)}, u32[]{:S(2)}, u32[]{:S(2)}) collective-permute-start(bf16[256,256]{1,0:T(8,128)(2,1)} %a.1), channel_id=1, source_target_pairs={{0,32},{32,0},{1,33},{33,1},{2,34},{34,2},{3,35},{35,3},{4,36},{36... | collective-permute-start | bytes 393224 | tf_op jit(solution)/shard_map/ppermute | solution.py:41
  2.1 0.1 collective-permute-start.1
  2.2 0.4 collective-permute-start.2
  2.6 1.5 %constant_dynamic-slice_fusion = (s32[1,1]{1,0:T(1,128)}, s32[1,1]{1,0:T(1,128)}, s32[1,1]{1,0:T(1,128)}, s32[1,1]{1,0:T(1,128)}) fusion(s32[2,4]{1,0:T(2,128)} %param.7, s32[]{:T(128)S(6)} %select_n.22, s32[]{:T(128)S(6)} %select_n.21), kind=kLoop, calls=%fused_computation.2 | loop fusion | bytes 40 | tf_op jit(solution)/shard_map/dynamic_slice | solution.py:226
  4.1 2.6 %stack.23.marks = s32[9]{0:T(128)S(1)} concatenate(s32[1]{0:T(128)} %bitcast, s32[1]{0:T(128)} %bitcast.1, s32[1]{0:T(128)} %bitcast.2, s32[1]{0:T(128)} %bitcast.3, s32[1]{0:T(128)} %bitcast.4, s32[1]{0:T(128)} %bitcast.5, s32[1]{0:T(128)} %bitcast.6, s32[1]{0:T(128)} %bitcast.7, s32[1]{0:T(128)} %bitcast.8), dimensions={0} | concatenate | bytes 72 | tf_op jit(solution)/shard_map/stack | solution.py:227
  6.8 0.9 %copy-done = bf16[256,256]{1,0:T(8,128)(2,1)S(1)} copy-done((bf16[256,256]{1,0:T(8,128)(2,1)S(1)}, bf16[256,256]{1,0:T(8,128)(2,1)}, u32[]{:S(2)}) %copy-start) | copy-done | bytes 131096
  7.7 0.9 %copy-done.1 = bf16[256,256]{1,0:T(8,128)(2,1)S(1)} copy-done((bf16[256,256]{1,0:T(8,128)(2,1)S(1)}, bf16[256,256]{1,0:T(8,128)(2,1)}, u32[]{:S(2)}) %copy-start.1) | copy-done | bytes 131096
  8.6 0.7 copy-done.2
  9.2 0.7 shard_map.59
  9.9 25.3 %all_to_all.10.mine = bf16[8,544,256]{2,1,0:T(8,128)(2,1)S(1)} all-to-all(bf16[8,544,256]{2,1,0:T(8,128)(2,1)S(1)} %shard_map.59), channel_id=1, replica_groups={{0,2,4,6,8,10,12,14},{64,66,68,70,72,74,76,78},{1,3,5,7,9,11,13,15},{65..., dimensions={0} | all-to-all | bytes 4456448 | tf_op jit(solution)/shard_map/all_to_all | solution.py:37
  35.2 0.1 fusion
  35.4 0.5 collective-permute-start.3
  35.9 2.2 %collective-permute-done.4.theirs = bf16[4,544,256]{2,1,0:T(8,128)(2,1)S(1)} collective-permute-done((bf16[4,544,256]{2,1,0:T(8,128)(2,1)S(1)}, bf16[4,544,256]{2,1,0:T(8,128)(2,1)S(1)}, u32[]{:S(2)}, u32[]{:S(2)}) %collective-permute-start.4) | collective-permute-done | bytes 1114144 | tf_op jit(solution)/shard_map/ppermute | solution.py:41
  38.2 8.8 %shard_map.60 = (f32[18,256,256]{2,1,0:T(8,128)S(1)}, s16[1552,256]{1,0:T(8,128)(2,1)S(1)}) custom-call(s32[9]{0:T(128)S(1)} %stack.23.marks, bf16[8,544,256]{2,1,0:T(8,128)(2,1)S(1)} %all_to_all.10.mine, bf16[4,544,256]{2,1,0:T(8,128)(2,1)S(1)} %collective-permute-done.4.theirs), custom_call_target="tpu_custom_call" | custom-call | flops 4831838208 | bytes 8388608 | tf_op jit(solution)/shard_map/pallas_call | solution.py:208
  47.0 8.8 %shard_map.61 = (f32[18,256,256]{2,1,0:T(8,128)S(1)}, s16[1552,256]{1,0:T(8,128)(2,1)S(1)}) custom-call(s32[9]{0:T(128)S(1)} %stack.23.marks, bf16[8,544,256]{2,1,0:T(8,128)(2,1)S(1)} %all_to_all.10.mine, bf16[4,544,256]{2,1,0:T(8,128)(2,1)S(1)} %collective-permute-done.3.theirs, ...), custom_call_target="tpu_custom_call", output_to_operand_aliasing={{0}: (3, {})} | custom-call | flops 4831838208 | bytes 8388608 | tf_op jit(solution)/shard_map/pallas_call | solution.py:208
  55.8 0.1 collective-permute-start.6
  55.9 0.5 collective-permute-start.5
  56.4 1.8 %collective-permute-done.6.got_far = s16[1552,256]{1,0:T(8,128)(2,1)S(1)} collective-permute-done((s16[1552,256]{1,0:T(8,128)(2,1)S(1)}, s16[1552,256]{1,0:T(8,128)(2,1)S(1)}, u32[]{:S(2)}, u32[]{:S(2)}) %collective-permute-start.6) | collective-permute-done | bytes 794656 | tf_op jit(solution)/shard_map/ppermute | solution.py:41
  58.2 1.1 %collective-permute-done.5.got_near = s16[1552,256]{1,0:T(8,128)(2,1)S(1)} collective-permute-done((s16[1552,256]{1,0:T(8,128)(2,1)S(1)}, s16[1552,256]{1,0:T(8,128)(2,1)S(1)}, u32[]{:S(2)}, u32[]{:S(2)}) %collective-permute-start.5) | collective-permute-done | bytes 794656 | tf_op jit(solution)/shard_map/ppermute | solution.py:41
  59.3 2.6 %shard_map.62 = s16[8,528,256]{2,1,0:T(8,128)(2,1)S(1)} custom-call(s32[9]{0:T(128)S(1)} %stack.23.marks, f32[18,256,256]{2,1,0:T(8,128)S(1)} %get-tuple-element.9.sums, s16[1552,256]{1,0:T(8,128)(2,1)S(1)} %collective-permute-done.5.got_near, s16[1552,256]{1,0:T(8,128)(2,1)S(1)} %collective-permute-done.6.got_far), custom_call_target="tpu_custom_call" | custom-call | flops 1048576 | bytes 8388608 | tf_op jit(solution)/shard_map/pallas_call | solution.py:208
  62.0 21.6 %all_to_all.11.got = s16[8,528,256]{2,1,0:T(8,128)(2,1)S(1)} all-to-all(s16[8,528,256]{2,1,0:T(8,128)(2,1)S(1)} %shard_map.62), channel_id=1, replica_groups={{0,2,4,6,8,10,12,14},{64,66,68,70,72,74,76,78},{1,3,5,7,9,11,13,15},{65..., dimensions={0} | all-to-all | bytes 4325376 | tf_op jit(solution)/shard_map/all_to_all | solution.py:37
  83.5 1.2 %shard_map.63 = (f32[256,256]{1,0:T(8,128)S(1)}, f32[256,256]{1,0:T(8,128)S(1)}) custom-call(s32[9]{0:T(128)S(1)} %stack.23.marks, s16[8,528,256]{2,1,0:T(8,128)(2,1)S(1)} %all_to_all.11.got), custom_call_target="tpu_custom_call" | custom-call | flops 1048576 | bytes 8388608 | tf_op jit(solution)/shard_map/pallas_call | solution.py:208
  84.8 1.5 %collective-permute-done.7 = f32[256,256]{1,0:T(8,128)S(1)} collective-permute-done((f32[256,256]{1,0:T(8,128)S(1)}, f32[256,256]{1,0:T(8,128)S(1)}, u32[]{:S(2)}, u32[]{:S(2)}) %collective-permute-start.7) | collective-permute-done | bytes 262176 | tf_op jit(solution)/shard_map/ppermute | solution.py:41
  86.3 0.8 broadcast_select_fusion
  (9 shorter events, 0.2 us)
Async XLA Ops:
  0.6 6.1 %collective-permute-start = (bf16[256,256]{1,0:T(8,128)(2,1)}, bf16[256,256]{1,0:T(8,128)(2,1)S(1)}, u32[]{:S(2)}, u32[]{:S(2)}) collective-permute-start(bf16[256,256]{1,0:T(8,128)(2,1)} %a.1), channel_id=1, source_target_pairs={{0,32},{32,0},{1,33},{33,1},{2,34},{34,2},{3,35},{35,3},{4,36},{36... | collective-permute-start | bytes 393224 | tf_op jit(solution)/shard_map/ppermute | solution.py:41
  2.1 4.6 %collective-permute-start.1 = (bf16[256,256]{1,0:T(8,128)(2,1)}, bf16[256,256]{1,0:T(8,128)(2,1)S(1)}, u32[]{:S(2)}, u32[]{:S(2)}) collective-permute-start(bf16[256,256]{1,0:T(8,128)(2,1)} %b.1), channel_id=1, source_target_pairs={{0,32},{32,0},{1,33},{33,1},{2,34},{34,2},{3,35},{35,3},{4,36},{36... | collective-permute-start | bytes 393224 | tf_op jit(solution)/shard_map/ppermute | solution.py:41
  2.2 4.5 %collective-permute-start.2 = (s32[1,256]{1,0:T(1,128)}, s32[1,256]{1,0:T(1,128)S(1)}, u32[]{:S(2)}, u32[]{:S(2)}) collective-permute-start(s32[1,256]{1,0:T(1,128)} %bitcast.10), channel_id=1, source_target_pairs={{0,32},{32,0},{1,33},{33,1},{2,34},{34,2},{3,35},{35,3},{4,36},{36... | collective-permute-start | bytes 3080 | tf_op jit(solution)/shard_map/ppermute | solution.py:41
  6.7 0.9 %copy-start = (bf16[256,256]{1,0:T(8,128)(2,1)S(1)}, bf16[256,256]{1,0:T(8,128)(2,1)}, u32[]{:S(2)}) copy-start(bf16[256,256]{1,0:T(8,128)(2,1)} %a.1) | copy-start | bytes 393220
  7.7 0.9 %copy-start.1 = (bf16[256,256]{1,0:T(8,128)(2,1)S(1)}, bf16[256,256]{1,0:T(8,128)(2,1)}, u32[]{:S(2)}) copy-start(bf16[256,256]{1,0:T(8,128)(2,1)} %b.1) | copy-start | bytes 393220
  8.6 0.7 copy-start.2
  35.3 2.8 %collective-permute-start.4 = (bf16[4,544,256]{2,1,0:T(8,128)(2,1)S(1)}, bf16[4,544,256]{2,1,0:T(8,128)(2,1)S(1)}, u32[]{:S(2)}, u32[]{:S(2)}) collective-permute-start(bf16[4,544,256]{2,1,0:T(8,128)(2,1)S(1)} %get-tuple-element.14), channel_id=1, source_target_pairs={{0,32},{32,0},{1,33},{33,1},{2,34},{34,2},{3,35},{35,3},{4,36},{36... | collective-permute-start | bytes 3342344 | tf_op jit(solution)/shard_map/ppermute | solution.py:41
  35.4 11.6 %collective-permute-start.3 = (bf16[4,544,256]{2,1,0:T(8,128)(2,1)S(1)}, bf16[4,544,256]{2,1,0:T(8,128)(2,1)S(1)}, u32[]{:S(2)}, u32[]{:S(2)}) collective-permute-start(bf16[4,544,256]{2,1,0:T(8,128)(2,1)S(1)} %get-tuple-element.15), channel_id=1, source_target_pairs={{0,32},{32,0},{1,33},{33,1},{2,34},{34,2},{3,35},{35,3},{4,36},{36... | collective-permute-start | bytes 3342344 | tf_op jit(solution)/shard_map/ppermute | solution.py:41
  55.8 2.4 %collective-permute-start.6 = (s16[1552,256]{1,0:T(8,128)(2,1)S(1)}, s16[1552,256]{1,0:T(8,128)(2,1)S(1)}, u32[]{:S(2)}, u32[]{:S(2)}) collective-permute-start(s16[1552,256]{1,0:T(8,128)(2,1)S(1)} %get-tuple-element.11), channel_id=1, source_target_pairs={{0,32},{32,0},{1,33},{33,1},{2,34},{34,2},{3,35},{35,3},{4,36},{36... | collective-permute-start | bytes 2383880 | tf_op jit(solution)/shard_map/ppermute | solution.py:41
  55.9 3.4 %collective-permute-start.5 = (s16[1552,256]{1,0:T(8,128)(2,1)S(1)}, s16[1552,256]{1,0:T(8,128)(2,1)S(1)}, u32[]{:S(2)}, u32[]{:S(2)}) collective-permute-start(s16[1552,256]{1,0:T(8,128)(2,1)S(1)} %get-tuple-element.10), channel_id=1, source_target_pairs={{0,32},{32,0},{1,33},{33,1},{2,34},{34,2},{3,35},{35,3},{4,36},{36... | collective-permute-start | bytes 2383880 | tf_op jit(solution)/shard_map/ppermute | solution.py:41
  84.7 1.6 %collective-permute-start.7 = (f32[256,256]{1,0:T(8,128)S(1)}, f32[256,256]{1,0:T(8,128)S(1)}, u32[]{:S(2)}, u32[]{:S(2)}) collective-permute-start(f32[256,256]{1,0:T(8,128)S(1)} %get-tuple-element.13), channel_id=1, source_target_pairs={{0,32},{32,0},{1,33},{33,1},{2,34},{34,2},{3,35},{35,3},{4,36},{36... | collective-permute-start | bytes 786440 | tf_op jit(solution)/shard_map/ppermute | solution.py:41

commit v4 on v0

v4 whole, which is shorter than its diff:
```python
import functools
import math

import jax
import jax.numpy as jnp
from jax import lax
from jax.experimental import pallas as pl
from jax.experimental.pallas import tpu as pltpu
from jax.sharding import Mesh, PartitionSpec as P

logit_scale = 2.0
logit_bias = -6.0
AXES = ("xl", "core", "z", "y", "xh")
ROWS = 256
NOTE = 16
PEAK = 32000.0
VMEM = pl.BlockSpec(memory_space=pltpu.VMEM)
SMEM = pl.BlockSpec(memory_space=pltpu.SMEM)


def member(xl, core, z, y, xh):
    return (((xl * 2 + core) * 4 + z) * 4 + y) * 2 + xh


def teams():
    out = []
    for pair in ((0, 1), (2, 3)):
        for x in range(4):
            out.append([member(x % 2, 0, z, y, x // 2) for z in pair for y in range(4)])
    for pair in ((0, 3), (1, 2)):
        for y in range(4):
            out.append([member(x % 2, 1, z, y, x // 2) for z in pair for x in range(4)])
    return out


def meet(value):
    return lax.all_to_all(value, AXES, 0, 0, axis_index_groups=teams(), tiled=True)


def swap_core(value):
    return lax.ppermute(value, "core", [(0, 1), (1, 0)])


def encode(block):
    top = jnp.maximum(jnp.max(jnp.abs(block), axis=0, keepdims=True), 2.0**-100)
    power = jnp.ceil(jnp.log2(top) * 128.0) + 1.0
    scaled = block * (PEAK * jnp.exp2(power * (-1.0 / 128.0)))
    return jnp.floor(scaled + 0.5).astype(jnp.int16), power


def decode(code, power):
    return code.astype(jnp.float32) * (jnp.exp2(power * (1.0 / 128.0)) * (1.0 / PEAK))


def notes(powers):
    powers = powers + [jnp.zeros((1, ROWS), jnp.float32)] * (NOTE - len(powers))
    return jnp.concatenate(powers, axis=0).astype(jnp.int16)


def on_core(body):
    core = lax.axis_index("core")
    for number in range(2):
        pl.when(core == number)(functools.partial(body, number))


def window(plan, core):
    group = lax.axis_index("xl") * 2 + core
    return [group, plan[0, group], plan[1, group]]


def place_in(owners, group):
    hits = [owner == group for owner in owners]
    used = jnp.logical_or(hits[0], jnp.logical_or(hits[1], hits[2]))
    return jnp.where(hits[1], 1, jnp.where(hits[2], 2, 0)), jnp.where(used, 1.0, 0.0)


def build_kernel(a, b, ids, a_got, b_got, ids_got, out):
    def body(core):
        one, two = (a, a_got) if core == 0 else (b_got, b)
        rows = []
        for ref in (ids, ids_got) if core == 0 else ():
            value = ref[...]
            rows.append(lax.shift_right_logical(value, 8).astype(jnp.float32))
            rows.append((value & 255).astype(jnp.float32))
        rows.append(jnp.zeros((NOTE - len(rows), ROWS), jnp.float32))
        note = jnp.concatenate(rows, axis=0).astype(jnp.bfloat16)
        for s in range(8):
            out[s, 0:ROWS, :] = one[...]
            out[s, ROWS : 2 * ROWS, :] = two[...]
            out[s, 2 * ROWS :, :] = note

    on_core(body)


def score_kernel(factor, half, plan, mine, theirs, *refs):
    keep, send, sums = refs[-3:]
    half_scale = 0.5 * factor
    half_bias = 0.5 * logit_bias
    wide, deep = 4 * ROWS, 2 * ROWS
    z, y = lax.axis_index("z"), lax.axis_index("y")
    outer = jnp.logical_or(z == 0, z == 3)

    def add(ref, start, value, fresh):
        count = value.shape[0] // ROWS
        value = value.reshape(count, ROWS, ROWS)
        if not fresh:
            value = value + ref[start : start + count]
        ref[start : start + count] = value

    def body(core):
        owners = window(plan, core)
        for unit in range(2):
            a_from, a_source = (mine, 4 * unit) if core == 0 else (theirs, 0)
            a = [a_from[a_source + s, core * ROWS : (core + 1) * ROWS, :] for s in range(4)]
            a = jnp.concatenate(a, axis=0)
            ids = []
            for s in range(4):
                note = a_from[a_source + s, 2 * ROWS :, :].astype(jnp.float32)[2 * core : 2 * core + 2]
                ids.append((note[0:1] * 256.0 + note[1:2]).astype(jnp.int32))
            ids = jnp.concatenate(ids, axis=1)
            far = half if core == 0 else unit
            level = jnp.where(outer, 3 * far, 1 + far)
            for slot in range(3):
                group = owners[slot]
                b_from, b_source = (theirs, 0) if core == 0 else (mine, 4 * unit)
                b_rows = pl.ds(pl.multiple_of(group % 2 * ROWS, ROWS), ROWS)
                keys = [b_from[b_source + 2 * xh + group // 2, b_rows, :] for xh in range(2)]
                keys = jnp.concatenate(keys, axis=0)
                here = lax.shift_right_logical(ids, 9) == group * 16 + level * 4 + y
                rows = jnp.where(here, ids & 511, -1)
                hit = lax.broadcasted_iota(jnp.int32, (deep, wide), 0) == rows
                logits = lax.dot_general(
                    keys, a, (((1,), (1,)), ((), ())), preferred_element_type=jnp.float32
                )
                weights = 0.5 * jnp.tanh(logits * half_scale + half_bias) + jnp.where(hit, -0.5, 0.5)
                weights = weights.astype(jnp.bfloat16)
                gb = jnp.dot(weights, a, preferred_element_type=jnp.float32)
                ga = lax.dot_general(
                    weights, keys, (((0,), (0,)), ((), ())), preferred_element_type=jnp.float32
                )
                if core == 0:
                    add(sums, slot * 2, gb, unit == 0)
                    add(keep, unit * 4, ga, half == 0 and slot == 0)
                else:
                    add(keep, slot * 4 + unit * 2, gb, half == 0)
                    add(sums, 0, ga, unit == 0 and slot == 0)
        powers = []
        for i in range(6 if core == 0 else 4):
            code, power = encode(sums[i])
            send[i * ROWS : (i + 1) * ROWS, :] = code
            powers.append(power)
        send[6 * ROWS :, :] = notes(powers)

    on_core(body)


def pack_kernel(half, plan, keep, got, *refs):
    out, total, powers = refs[-3:]

    def body(core):
        if core == 0:
            got_powers = got[6 * ROWS :, :].astype(jnp.float32)
        else:
            powers[...] = got[6 * ROWS :, :].astype(jnp.float32)
            own, mate = window(plan, 1), window(plan, 0)
        for i in range(4):
            s = half * 4 + i
            written = []
            if core == 0:
                code, power = encode(keep[s])
                out[s, 0:ROWS, :] = code
                out[s, ROWS : 2 * ROWS, :] = got[i * ROWS : (i + 1) * ROWS, :]
                written = [power, got_powers[i : i + 1]]
            else:
                for c in range(2):
                    group, xh = i % 2 * 2 + c, i // 2
                    slot, kept = place_in(own, group)
                    value = keep[slot * 4 + half * 2 + xh] * kept
                    slot, used = place_in(mate, group)
                    index = slot * 2 + xh
                    scale = jnp.exp2(powers[pl.ds(index, 1), :] * (1.0 / 128.0)) * (used * (1.0 / PEAK))
                    code = got[pl.ds(pl.multiple_of(index * ROWS, ROWS), ROWS), :]
                    total[...] = value + code.astype(jnp.float32) * scale
                    code, power = encode(total[...])
                    out[s, c * ROWS : (c + 1) * ROWS, :] = code
                    written.append(power)
            out[s, 2 * ROWS :, :] = notes(written)

    on_core(body)


def sum_kernel(factor, got, keep, send):
    def body(core):
        for c in range(2):
            total = jnp.zeros((ROWS, ROWS), jnp.float32)
            for s in range(8):
                power = got[s, 2 * ROWS :, :].astype(jnp.float32)[c : c + 1]
                total += decode(got[s, c * ROWS : (c + 1) * ROWS, :], power)
            (keep if c == core else send)[...] = total * factor

    on_core(body)


def call(kernel, shapes, scratch, flops, *operands, plan=None, aliases={}):
    operands = operands if plan is None else (plan, *operands)
    return pl.pallas_call(
        kernel,
        out_shape=shapes,
        in_specs=[VMEM if plan is None or i else SMEM for i in range(len(operands))],
        out_specs=jax.tree.map(lambda _: VMEM, shapes),
        scratch_shapes=scratch,
        input_output_aliases=aliases,
        compiler_params=pltpu.CompilerParams(vmem_limit_bytes=36 << 20),
        cost_estimate=pl.CostEstimate(flops=flops, bytes_accessed=8 << 20, transcendentals=0),
    )(*operands)


def shards(views_a, views_b, positives, plan):
    factor = logit_scale / math.sqrt(views_a.shape[1])
    f32, i16, bf16 = jnp.float32, jnp.int16, jnp.bfloat16
    height = 2 * ROWS + NOTE
    ids = positives.reshape(1, ROWS)
    got = [swap_core(value) for value in (views_a, views_b, ids)]
    built = jax.ShapeDtypeStruct((8, height, ROWS), bf16)
    mine = meet(call(build_kernel, built, [], 1 << 20, views_a, views_b, ids, *got))
    near, far = swap_core(mine[:4]), swap_core(mine[4:])

    def score(half, theirs, *keep):
        return call(
            functools.partial(score_kernel, factor, half),
            (
                jax.ShapeDtypeStruct((12, ROWS, ROWS), f32),
                jax.ShapeDtypeStruct((6 * ROWS + NOTE, ROWS), i16),
            ),
            [pltpu.VMEM((6, ROWS, ROWS), f32)],
            3 * 2048 * 3072 * 256,
            mine,
            theirs,
            *keep,
            plan=plan,
            aliases={3: 0} if keep else {},
        )

    def pack(half, keep, got, *packed):
        return call(
            functools.partial(pack_kernel, half),
            jax.ShapeDtypeStruct((8, height, ROWS), i16),
            [pltpu.VMEM((ROWS, ROWS), f32), pltpu.VMEM((NOTE, ROWS), f32)],
            1 << 20,
            keep,
            got,
            *packed,
            plan=plan,
            aliases={3: 0} if packed else {},
        )

    keep, send_near = score(0, near)
    got_near = swap_core(send_near)
    keep, send_far = score(1, far, keep)
    got_far = swap_core(send_far)
    packed = pack(1, keep, got_far, pack(0, keep, got_near))
    one = jax.ShapeDtypeStruct((ROWS, ROWS), f32)
    keep, send = call(functools.partial(sum_kernel, factor), (one, one), [], 1 << 20, meet(packed))
    got = swap_core(send)
    core = lax.axis_index("core")
    return jnp.where(core == 0, keep, got), jnp.where(core == 0, got, keep)


def solution(mesh):
    fine = Mesh(mesh.devices.reshape(2, 2, 4, 4, 2), AXES)
    split = P(AXES, None)
    return jax.shard_map(
        shards,
        mesh=fine,
        in_specs=(split, split, P(AXES), P()),
        out_specs=(split, split),
        check_vma=False,
    )
```

time: 941 us -> 78.6 us (0.08)
  waiting for transfers between devices: 855 us -> 5.11 us
  matrix products: 39 us -> 0 us
  blocking collectives: 8.73 us -> 47 us
  between operations: 20.8 us -> 0.71 us
  Pallas kernels: 0 us -> 18.4 us
  local copies, waits for them, and re-layouts: 14.3 us -> 2.63 us
    reduce_scatter x4 -> x0, waiting for transfers between devices: 635 us -> none  [the longest x3 592 us: score_group(): lax.psum_scatter(grad_keys, 'dev', scatter_dimension=0, tiled=True)]
    all_gather x3 -> x0, waiting for transfers between devices: 219 us -> none  [score_group(): piece = lax.all_gather(key_shard, 'dev', axis=0, tiled=True)]
    all_to_all x0 -> x2, blocking collectives: none -> 47 us  [meet(): lax.all_to_all(value, AXES, 0, 0, axis_index_groups=teams(), tiled=True)]
    dot_general x9 -> x0, matrix products: 39 us -> none  [the longest x3 17.3 us: weights_for(): lax.dot_general(queries, keys, (((1,), (1,)), ((), ())), preferred_elemen...]
    pallas_call x0 -> x6, Pallas kernels: none -> 18.4 us  [call(): pl.pallas_call(kernel, out_shape=shapes, in_specs=[VMEM if plan is None o...]
  transfers between devices with their start and end apart: 7 -> 8, of which waited for: 7 -> 4; matrix products, arithmetic and copies ran while one was open for 4% -> 0% of each run, Pallas kernels for 0% -> 21%
where the time goes in v4:
time: 78.6 us; the launch traced here: 78.4 us
  blocking collectives  47 us (60%)
  Pallas kernels  18.4 us (23%)
  waiting for transfers between devices  5.11 us (7%)
  starting transfers between devices  3.65 us (5%)
  local copies, waits for them, and re-layouts  2.63 us (3%)
  other arithmetic  0.83 us (1%)
    all_to_all x2, blocking collectives, meet(): lax.all_to_all(value, AXES, 0, 0, axis_index_groups=teams(), tiled=True)  47 us
    pallas_call x6, Pallas kernels, call(): pl.pallas_call(kernel, out_shape=shapes, in_specs=[VMEM if plan is None o...  18.4 us
    ppermute x8, waiting for transfers between devices, swap_core(): return lax.ppermute(value, 'core', [(0, 1), (1, 0)])  5.11 us
    ppermute x8, starting transfers between devices, swap_core(): return lax.ppermute(value, 'core', [(0, 1), (1, 0)])  3.65 us
    unnamed x8, local copies, waits for them, and re-layouts  2.49 us
  transfers between devices with their start and end apart: 8, of which 4 were waited for; matrix products, arithmetic and copies ran while one was open for 0% of the time, Pallas kernels for 21%

profile of v4, /device:TPU:1, one launch (start us, length us, event | category | flops | bytes accessed | tf_op | source)
XLA Modules:
  0.0 78.4 jit_solution(16902108304415463933)
XLA Ops:
  0.6 1.5 %collective-permute-start = (bf16[256,256]{1,0:T(8,128)(2,1)}, bf16[256,256]{1,0:T(8,128)(2,1)S(1)}, u32[]{:S(2)}, u32[]{:S(2)}) collective-permute-start(bf16[256,256]{1,0:T(8,128)(2,1)} %a.1), channel_id=1, source_target_pairs={{0,32},{32,0},{1,33},{33,1},{2,34},{34,2},{3,35},{35,3},{4,36},{36... | collective-permute-start | bytes 393224 | tf_op jit(solution)/shard_map/ppermute | solution.py:41
  2.1 0.1 collective-permute-start.1
  2.2 0.4 collective-permute-start.2
  2.6 1.0 %collective-permute-done.2.ids_got = s32[1,256]{1,0:T(1,128)S(1)} collective-permute-done((s32[1,256]{1,0:T(1,128)}, s32[1,256]{1,0:T(1,128)S(1)}, u32[]{:S(2)}, u32[]{:S(2)}) %collective-permute-start.2) | collective-permute-done | bytes 1056 | tf_op jit(solution)/shard_map/ppermute | solution.py:41
  3.7 0.9 %copy-done = bf16[256,256]{1,0:T(8,128)(2,1)S(1)} copy-done((bf16[256,256]{1,0:T(8,128)(2,1)S(1)}, bf16[256,256]{1,0:T(8,128)(2,1)}, u32[]{:S(2)}) %copy-start) | copy-done | bytes 131096
  4.6 0.9 %copy-done.1 = bf16[256,256]{1,0:T(8,128)(2,1)S(1)} copy-done((bf16[256,256]{1,0:T(8,128)(2,1)S(1)}, bf16[256,256]{1,0:T(8,128)(2,1)}, u32[]{:S(2)}) %copy-start.1) | copy-done | bytes 131096
  5.5 0.7 copy-done.3
  6.2 0.1 shard_map.59
  6.3 25.0 %all_to_all.10.mine = bf16[8,528,256]{2,1,0:T(8,128)(2,1)S(1)} all-to-all(bf16[8,528,256]{2,1,0:T(8,128)(2,1)S(1)} %shard_map.59), channel_id=1, replica_groups={{0,2,4,6,8,10,12,14},{64,66,68,70,72,74,76,78},{1,3,5,7,9,11,13,15},{65..., dimensions={0} | all-to-all | bytes 4325376 | tf_op jit(solution)/shard_map/all_to_all | solution.py:37
  31.4 0.1 fusion
  31.5 0.1 collective-permute-start.4
  31.6 0.5 collective-permute-start.3
  32.1 2.2 %collective-permute-done.4.theirs = bf16[4,528,256]{2,1,0:T(8,128)(2,1)S(1)} collective-permute-done((bf16[4,528,256]{2,1,0:T(8,128)(2,1)S(1)}, bf16[4,528,256]{2,1,0:T(8,128)(2,1)S(1)}, u32[]{:S(2)}, u32[]{:S(2)}) %collective-permute-start.4) | collective-permute-done | bytes 1081376 | tf_op jit(solution)/shard_map/ppermute | solution.py:41
  34.3 7.2 %shard_map.60 = (f32[12,256,256]{2,1,0:T(8,128)S(1)}, s16[1552,256]{1,0:T(8,128)(2,1)S(1)}) custom-call(s32[2,4]{1,0:T(2,128)S(1)} %copy-done.2, bf16[8,528,256]{2,1,0:T(8,128)(2,1)S(1)} %all_to_all.10.mine, bf16[4,528,256]{2,1,0:T(8,128)(2,1)S(1)} %collective-permute-done.4.theirs), custom_call_target="tpu_custom_call" | custom-call | flops 4831838208 | bytes 8388608 | tf_op jit(solution)/shard_map/pallas_call | solution.py:206
  41.5 0.6 collective-permute-start.6
  42.0 7.3 %shard_map.61 = (f32[12,256,256]{2,1,0:T(8,128)S(1)}, s16[1552,256]{1,0:T(8,128)(2,1)S(1)}) custom-call(s32[2,4]{1,0:T(2,128)S(1)} %copy-done.2, bf16[8,528,256]{2,1,0:T(8,128)(2,1)S(1)} %all_to_all.10.mine, bf16[4,528,256]{2,1,0:T(8,128)(2,1)S(1)} %collective-permute-done.3.theirs, ...), custom_call_target="tpu_custom_call", output_to_operand_aliasing={{0}: (3, {})} | custom-call | flops 4831838208 | bytes 8388608 | tf_op jit(solution)/shard_map/pallas_call | solution.py:206
  49.4 0.4 collective-permute-start.5
  49.8 1.6 %shard_map.62.refs_0_ = s16[8,528,256]{2,1,0:T(8,128)(2,1)S(1)} custom-call(s32[2,4]{1,0:T(2,128)S(1)} %copy-done.2, f32[12,256,256]{2,1,0:T(8,128)S(1)} %get-tuple-element.9.keep, s16[1552,256]{1,0:T(8,128)(2,1)S(1)} %collective-permute-done.6.got), custom_call_target="tpu_custom_call" | custom-call | flops 1048576 | bytes 8388608 | tf_op jit(solution)/shard_map/pallas_call | solution.py:206
  51.4 0.3 collective-permute-done.5.got
  51.7 1.6 %shard_map.63 = s16[8,528,256]{2,1,0:T(8,128)(2,1)S(1)} custom-call(s32[2,4]{1,0:T(2,128)S(1)} %copy-done.2, f32[12,256,256]{2,1,0:T(8,128)S(1)} %get-tuple-element.9.keep, s16[1552,256]{1,0:T(8,128)(2,1)S(1)} %collective-permute-done.5.got, s16[8,528,256]{2,1,0:T(8,128)(2,1)S(1)} %shard_map.62.refs_0_), custom_call_target="tpu_custom_call", output_to_operand_aliasing={{}: (3, {})} | custom-call | flops 1048576 | bytes 8388608 | tf_op jit(solution)/shard_map/pallas_call | solution.py:206
  53.4 22.0 %all_to_all.11.got = s16[8,528,256]{2,1,0:T(8,128)(2,1)S(1)} all-to-all(s16[8,528,256]{2,1,0:T(8,128)(2,1)S(1)} %shard_map.63), channel_id=1, replica_groups={{0,2,4,6,8,10,12,14},{64,66,68,70,72,74,76,78},{1,3,5,7,9,11,13,15},{65..., dimensions={0} | all-to-all | bytes 4325376 | tf_op jit(solution)/shard_map/all_to_all | solution.py:37
  75.4 0.6 shard_map.64
  76.1 1.5 %collective-permute-done.7 = f32[256,256]{1,0:T(8,128)S(1)} collective-permute-done((f32[256,256]{1,0:T(8,128)S(1)}, f32[256,256]{1,0:T(8,128)S(1)}, u32[]{:S(2)}, u32[]{:S(2)}) %collective-permute-start.7) | collective-permute-done | bytes 262176 | tf_op jit(solution)/shard_map/ppermute | solution.py:41
  77.6 0.8 %broadcast_select_fusion = (f32[256,256]{1,0:T(8,128)}, f32[256,256]{1,0:T(8,128)}) fusion(f32[256,256]{1,0:T(8,128)S(1)} %collective-permute-done.7, f32[256,256]{1,0:T(8,128)S(1)} %get-tuple-element.12, pred[]{:T(512)S(6)} %eq.4), kind=kLoop, calls=%fused_computation | loop fusion | flops 131072 | bytes 1048577 | tf_op jit(solution)/shard_map/jit(_where)/select_n | solution.py:266
  (10 shorter events, 0.1 us)
Async XLA Ops:
  0.6 3.1 %collective-permute-start = (bf16[256,256]{1,0:T(8,128)(2,1)}, bf16[256,256]{1,0:T(8,128)(2,1)S(1)}, u32[]{:S(2)}, u32[]{:S(2)}) collective-permute-start(bf16[256,256]{1,0:T(8,128)(2,1)} %a.1), channel_id=1, source_target_pairs={{0,32},{32,0},{1,33},{33,1},{2,34},{34,2},{3,35},{35,3},{4,36},{36... | collective-permute-start | bytes 393224 | tf_op jit(solution)/shard_map/ppermute | solution.py:41
  2.1 1.6 %collective-permute-start.1 = (bf16[256,256]{1,0:T(8,128)(2,1)}, bf16[256,256]{1,0:T(8,128)(2,1)S(1)}, u32[]{:S(2)}, u32[]{:S(2)}) collective-permute-start(bf16[256,256]{1,0:T(8,128)(2,1)} %b.1), channel_id=1, source_target_pairs={{0,32},{32,0},{1,33},{33,1},{2,34},{34,2},{3,35},{35,3},{4,36},{36... | collective-permute-start | bytes 393224 | tf_op jit(solution)/shard_map/ppermute | solution.py:41
  2.2 1.5 %collective-permute-start.2 = (s32[1,256]{1,0:T(1,128)}, s32[1,256]{1,0:T(1,128)S(1)}, u32[]{:S(2)}, u32[]{:S(2)}) collective-permute-start(s32[1,256]{1,0:T(1,128)} %bitcast.1), channel_id=1, source_target_pairs={{0,32},{32,0},{1,33},{33,1},{2,34},{34,2},{3,35},{35,3},{4,36},{36... | collective-permute-start | bytes 3080 | tf_op jit(solution)/shard_map/ppermute | solution.py:41
  3.7 0.9 %copy-start = (bf16[256,256]{1,0:T(8,128)(2,1)S(1)}, bf16[256,256]{1,0:T(8,128)(2,1)}, u32[]{:S(2)}) copy-start(bf16[256,256]{1,0:T(8,128)(2,1)} %a.1) | copy-start | bytes 393220
  4.6 0.9 %copy-start.1 = (bf16[256,256]{1,0:T(8,128)(2,1)S(1)}, bf16[256,256]{1,0:T(8,128)(2,1)}, u32[]{:S(2)}) copy-start(bf16[256,256]{1,0:T(8,128)(2,1)} %b.1) | copy-start | bytes 393220
  5.5 0.7 copy-start.3
  31.4 2.9 %copy-start.2 = (s32[2,4]{1,0:T(2,128)S(1)}, s32[2,4]{1,0:T(2,128)}, u32[]{:S(2)}) copy-start(s32[2,4]{1,0:T(2,128)} %plan.7) | copy-start | bytes 100
  31.5 2.8 %collective-permute-start.4 = (bf16[4,528,256]{2,1,0:T(8,128)(2,1)S(1)}, bf16[4,528,256]{2,1,0:T(8,128)(2,1)S(1)}, u32[]{:S(2)}, u32[]{:S(2)}) collective-permute-start(bf16[4,528,256]{2,1,0:T(8,128)(2,1)S(1)} %get-tuple-element.14), channel_id=1, source_target_pairs={{0,32},{32,0},{1,33},{33,1},{2,34},{34,2},{3,35},{35,3},{4,36},{36... | collective-permute-start | bytes 3244040 | tf_op jit(solution)/shard_map/ppermute | solution.py:41
  31.6 10.4 %collective-permute-start.3 = (bf16[4,528,256]{2,1,0:T(8,128)(2,1)S(1)}, bf16[4,528,256]{2,1,0:T(8,128)(2,1)S(1)}, u32[]{:S(2)}, u32[]{:S(2)}) collective-permute-start(bf16[4,528,256]{2,1,0:T(8,128)(2,1)S(1)} %get-tuple-element.15), channel_id=1, source_target_pairs={{0,32},{32,0},{1,33},{33,1},{2,34},{34,2},{3,35},{35,3},{4,36},{36... | collective-permute-start | bytes 3244040 | tf_op jit(solution)/shard_map/ppermute | solution.py:41
  41.5 8.3 %collective-permute-start.6 = (s16[1552,256]{1,0:T(8,128)(2,1)S(1)}, s16[1552,256]{1,0:T(8,128)(2,1)S(1)}, u32[]{:S(2)}, u32[]{:S(2)}) collective-permute-start(s16[1552,256]{1,0:T(8,128)(2,1)S(1)} %get-tuple-element.11), channel_id=1, source_target_pairs={{0,32},{32,0},{1,33},{33,1},{2,34},{34,2},{3,35},{35,3},{4,36},{36... | collective-permute-start | bytes 2383880 | tf_op jit(solution)/shard_map/ppermute | solution.py:41
  49.4 2.4 %collective-permute-start.5 = (s16[1552,256]{1,0:T(8,128)(2,1)S(1)}, s16[1552,256]{1,0:T(8,128)(2,1)S(1)}, u32[]{:S(2)}, u32[]{:S(2)}) collective-permute-start(s16[1552,256]{1,0:T(8,128)(2,1)S(1)} %get-tuple-element.10), channel_id=1, source_target_pairs={{0,32},{32,0},{1,33},{33,1},{2,34},{34,2},{3,35},{35,3},{4,36},{36... | collective-permute-start | bytes 2383880 | tf_op jit(solution)/shard_map/ppermute | solution.py:41
  76.0 1.6 %collective-permute-start.7 = (f32[256,256]{1,0:T(8,128)S(1)}, f32[256,256]{1,0:T(8,128)S(1)}, u32[]{:S(2)}, u32[]{:S(2)}) collective-permute-start(f32[256,256]{1,0:T(8,128)S(1)} %get-tuple-element.13), channel_id=1, source_target_pairs={{0,32},{32,0},{1,33},{33,1},{2,34},{34,2},{3,35},{35,3},{4,36},{36... | collective-permute-start | bytes 786440 | tf_op jit(solution)/shard_map/ppermute | solution.py:41

commit v5 on v4

--- a/solution.py
+++ b/solution.py
@@ -74,15 +74,14 @@
     return jnp.where(hits[1], 1, jnp.where(hits[2], 2, 0)), jnp.where(used, 1.0, 0.0)
 
 
-def build_kernel(a, b, ids, a_got, b_got, ids_got, out):
-    def body(core):
-        one, two = (a, a_got) if core == 0 else (b_got, b)
-        rows = []
-        for ref in (ids, ids_got) if core == 0 else ():
-            value = ref[...]
-            rows.append(lax.shift_right_logical(value, 8).astype(jnp.float32))
-            rows.append((value & 255).astype(jnp.float32))
-        rows.append(jnp.zeros((NOTE - len(rows), ROWS), jnp.float32))
+def build_kernel(own, ids, a_got, b_got, ids_got, out):
+    def body(core):
+        one, two = (own, a_got) if core == 0 else (b_got, own)
+        value = ids_got[...]
+        rows = [ids[...].astype(jnp.float32)]
+        rows.append(lax.shift_right_logical(value, 8).astype(jnp.float32))
+        rows.append((value & 255).astype(jnp.float32))
+        rows.append(jnp.zeros((NOTE - 4, ROWS), jnp.float32))
         note = jnp.concatenate(rows, axis=0).astype(jnp.bfloat16)
         for s in range(8):
             out[s, 0:ROWS, :] = one[...]
@@ -219,10 +218,13 @@
     factor = logit_scale / math.sqrt(views_a.shape[1])
     f32, i16, bf16 = jnp.float32, jnp.int16, jnp.bfloat16
     height = 2 * ROWS + NOTE
+    core = lax.axis_index("core")
     ids = positives.reshape(1, ROWS)
     got = [swap_core(value) for value in (views_a, views_b, ids)]
+    own = jnp.where(core == 0, views_a, views_b)
+    own_ids = jnp.stack([positives // 256, positives % 256]).astype(bf16)
     built = jax.ShapeDtypeStruct((8, height, ROWS), bf16)
-    mine = meet(call(build_kernel, built, [], 1 << 20, views_a, views_b, ids, *got))
+    mine = meet(call(build_kernel, built, [], 1 << 10, own, own_ids, *got))
     near, far = swap_core(mine[:4]), swap_core(mine[4:])
 
     def score(half, theirs, *keep):
@@ -262,7 +264,6 @@
     one = jax.ShapeDtypeStruct((ROWS, ROWS), f32)
     keep, send = call(functools.partial(sum_kernel, factor), (one, one), [], 1 << 20, meet(packed))
     got = swap_core(send)
-    core = lax.axis_index("core")
     return jnp.where(core == 0, keep, got), jnp.where(core == 0, got, keep)
 
 

time: 78.6 us -> 76.6 us (0.975)
  local copies, waits for them, and re-layouts: 2.63 us -> 0.15 us
  other arithmetic: 0.83 us -> 2.45 us
  waiting for transfers between devices: 5.11 us -> 4.07 us
    unnamed x8 -> x2, local copies, waits for them, and re-layouts: 2.49 us -> 0.01 us
    ppermute x8, waiting for transfers between devices: 5.11 us -> 4.07 us  [swap_core(): return lax.ppermute(value, 'core', [(0, 1), (1, 0)])]
    select_n x0 -> x1, other arithmetic: none -> 0.92 us  [shards(): own = jnp.where(core == 0, views_a, views_b)]
  transfers between devices with their start and end apart: 8 -> 8, of which waited for: 4 -> 3; matrix products, arithmetic and copies ran while one was open for 0% -> 2% of each run, Pallas kernels for 21% -> 21%
where the time goes in v5:
time: 76.6 us; the launch traced here: 76.3 us
  blocking collectives  46.8 us (61%)
  Pallas kernels  18.5 us (24%)
  waiting for transfers between devices  4.07 us (5%)
  starting transfers between devices  3.65 us (5%)
  other arithmetic  2.45 us (3%)
    all_to_all x2, blocking collectives, meet(): lax.all_to_all(value, AXES, 0, 0, axis_index_groups=teams(), tiled=True)  46.8 us
    pallas_call x6, Pallas kernels, call(): pl.pallas_call(kernel, out_shape=shapes, in_specs=[VMEM if plan is None o...  18.5 us
    ppermute x8, waiting for transfers between devices, swap_core(): return lax.ppermute(value, 'core', [(0, 1), (1, 0)])  4.07 us
    ppermute x8, starting transfers between devices, swap_core(): return lax.ppermute(value, 'core', [(0, 1), (1, 0)])  3.65 us
  transfers between devices with their start and end apart: 8, of which 3 were waited for; matrix products, arithmetic and copies ran while one was open for 2% of the time, Pallas kernels for 21%

profile of v5, /device:TPU:1, one launch (start us, length us, event | category | flops | bytes accessed | tf_op | source)
XLA Modules:
  0.0 76.3 jit_solution(12079835570383850493)
XLA Ops:
  0.6 1.5 %collective-permute-start.2 = (s32[1,256]{1,0:T(1,128)}, s32[1,256]{1,0:T(1,128)S(1)}, u32[]{:S(2)}, u32[]{:S(2)}) collective-permute-start(s32[1,256]{1,0:T(1,128)} %bitcast.1), channel_id=1, source_target_pairs={{0,32},{32,0},{1,33},{33,1},{2,34},{34,2},{3,35},{35,3},{4,36},{36... | collective-permute-start | bytes 3080 | tf_op jit(solution)/shard_map/ppermute | solution.py:41
  2.1 0.1 collective-permute-start
  2.2 0.4 collective-permute-start.1
  2.6 0.9 %broadcast_select_fusion.2.own = bf16[256,256]{1,0:T(8,128)(2,1)S(1)} fusion(bf16[256,256]{1,0:T(8,128)(2,1)} %param.4, bf16[256,256]{1,0:T(8,128)(2,1)} %param.5, pred[]{:T(512)S(6)} %eq.4), kind=kLoop, calls=%fused_computation.2 | loop fusion | flops 65536 | bytes 393217 | tf_op jit(solution)/shard_map/jit(_where)/select_n | solution.py:224
  3.6 0.7 fusion.1
  4.3 0.0 collective-permute-done.2.ids_got
  4.3 0.2 shard_map.59
  4.5 25.0 %all_to_all.10.mine = bf16[8,528,256]{2,1,0:T(8,128)(2,1)S(1)} all-to-all(bf16[8,528,256]{2,1,0:T(8,128)(2,1)S(1)} %shard_map.59), channel_id=1, replica_groups={{0,2,4,6,8,10,12,14},{64,66,68,70,72,74,76,78},{1,3,5,7,9,11,13,15},{65..., dimensions={0} | all-to-all | bytes 4325376 | tf_op jit(solution)/shard_map/all_to_all | solution.py:37
  29.5 0.1 fusion.2
  29.7 0.1 collective-permute-start.4
  29.7 0.5 collective-permute-start.3
  30.2 2.2 %collective-permute-done.4.theirs = bf16[4,528,256]{2,1,0:T(8,128)(2,1)S(1)} collective-permute-done((bf16[4,528,256]{2,1,0:T(8,128)(2,1)S(1)}, bf16[4,528,256]{2,1,0:T(8,128)(2,1)S(1)}, u32[]{:S(2)}, u32[]{:S(2)}) %collective-permute-start.4) | collective-permute-done | bytes 1081376 | tf_op jit(solution)/shard_map/ppermute | solution.py:41
  32.4 7.2 %shard_map.60 = (f32[12,256,256]{2,1,0:T(8,128)S(1)}, s16[1552,256]{1,0:T(8,128)(2,1)S(1)}) custom-call(s32[2,4]{1,0:T(2,128)S(1)} %copy-done, bf16[8,528,256]{2,1,0:T(8,128)(2,1)S(1)} %all_to_all.10.mine, bf16[4,528,256]{2,1,0:T(8,128)(2,1)S(1)} %collective-permute-done.4.theirs), custom_call_target="tpu_custom_call" | custom-call | flops 4831838208 | bytes 8388608 | tf_op jit(solution)/shard_map/pallas_call | solution.py:205
  39.6 0.6 collective-permute-start.6
  40.2 7.3 %shard_map.61 = (f32[12,256,256]{2,1,0:T(8,128)S(1)}, s16[1552,256]{1,0:T(8,128)(2,1)S(1)}) custom-call(s32[2,4]{1,0:T(2,128)S(1)} %copy-done, bf16[8,528,256]{2,1,0:T(8,128)(2,1)S(1)} %all_to_all.10.mine, bf16[4,528,256]{2,1,0:T(8,128)(2,1)S(1)} %collective-permute-done.3.theirs, ...), custom_call_target="tpu_custom_call", output_to_operand_aliasing={{0}: (3, {})} | custom-call | flops 4831838208 | bytes 8388608 | tf_op jit(solution)/shard_map/pallas_call | solution.py:205
  47.5 0.4 collective-permute-start.5
  47.9 1.6 %shard_map.62.refs_0_ = s16[8,528,256]{2,1,0:T(8,128)(2,1)S(1)} custom-call(s32[2,4]{1,0:T(2,128)S(1)} %copy-done, f32[12,256,256]{2,1,0:T(8,128)S(1)} %get-tuple-element.9.keep, s16[1552,256]{1,0:T(8,128)(2,1)S(1)} %collective-permute-done.6.got), custom_call_target="tpu_custom_call" | custom-call | flops 1048576 | bytes 8388608 | tf_op jit(solution)/shard_map/pallas_call | solution.py:205
  49.6 0.3 collective-permute-done.5.got
  49.9 1.6 %shard_map.63 = s16[8,528,256]{2,1,0:T(8,128)(2,1)S(1)} custom-call(s32[2,4]{1,0:T(2,128)S(1)} %copy-done, f32[12,256,256]{2,1,0:T(8,128)S(1)} %get-tuple-element.9.keep, s16[1552,256]{1,0:T(8,128)(2,1)S(1)} %collective-permute-done.5.got, s16[8,528,256]{2,1,0:T(8,128)(2,1)S(1)} %shard_map.62.refs_0_), custom_call_target="tpu_custom_call", output_to_operand_aliasing={{}: (3, {})} | custom-call | flops 1048576 | bytes 8388608 | tf_op jit(solution)/shard_map/pallas_call | solution.py:205
  51.5 21.8 %all_to_all.11.got = s16[8,528,256]{2,1,0:T(8,128)(2,1)S(1)} all-to-all(s16[8,528,256]{2,1,0:T(8,128)(2,1)S(1)} %shard_map.63), channel_id=1, replica_groups={{0,2,4,6,8,10,12,14},{64,66,68,70,72,74,76,78},{1,3,5,7,9,11,13,15},{65..., dimensions={0} | all-to-all | bytes 4325376 | tf_op jit(solution)/shard_map/all_to_all | solution.py:37
  73.3 0.6 shard_map.64
  73.9 0.1 collective-permute-start.7
  74.0 1.5 %collective-permute-done.7 = f32[256,256]{1,0:T(8,128)S(1)} collective-permute-done((f32[256,256]{1,0:T(8,128)S(1)}, f32[256,256]{1,0:T(8,128)S(1)}, u32[]{:S(2)}, u32[]{:S(2)}) %collective-permute-start.7) | collective-permute-done | bytes 262176 | tf_op jit(solution)/shard_map/ppermute | solution.py:41
  75.5 0.8 %broadcast_select_fusion = (f32[256,256]{1,0:T(8,128)}, f32[256,256]{1,0:T(8,128)}) fusion(f32[256,256]{1,0:T(8,128)S(1)} %collective-permute-done.7, f32[256,256]{1,0:T(8,128)S(1)} %get-tuple-element.12, pred[]{:T(512)S(6)} %eq.4), kind=kLoop, calls=%fused_computation | loop fusion | flops 131072 | bytes 1048577 | tf_op jit(solution)/shard_map/jit(_where)/select_n | solution.py:267
  (9 shorter events, 0.0 us)
Async XLA Ops:
  0.6 3.7 %collective-permute-start.2 = (s32[1,256]{1,0:T(1,128)}, s32[1,256]{1,0:T(1,128)S(1)}, u32[]{:S(2)}, u32[]{:S(2)}) collective-permute-start(s32[1,256]{1,0:T(1,128)} %bitcast.1), channel_id=1, source_target_pairs={{0,32},{32,0},{1,33},{33,1},{2,34},{34,2},{3,35},{35,3},{4,36},{36... | collective-permute-start | bytes 3080 | tf_op jit(solution)/shard_map/ppermute | solution.py:41
  2.1 2.2 %collective-permute-start = (bf16[256,256]{1,0:T(8,128)(2,1)}, bf16[256,256]{1,0:T(8,128)(2,1)S(1)}, u32[]{:S(2)}, u32[]{:S(2)}) collective-permute-start(bf16[256,256]{1,0:T(8,128)(2,1)} %param.4), channel_id=1, source_target_pairs={{0,32},{32,0},{1,33},{33,1},{2,34},{34,2},{3,35},{35,3},{4,36},{36... | collective-permute-start | bytes 393224 | tf_op jit(solution)/shard_map/ppermute | solution.py:41
  2.2 2.1 %collective-permute-start.1 = (bf16[256,256]{1,0:T(8,128)(2,1)}, bf16[256,256]{1,0:T(8,128)(2,1)S(1)}, u32[]{:S(2)}, u32[]{:S(2)}) collective-permute-start(bf16[256,256]{1,0:T(8,128)(2,1)} %param.5), channel_id=1, source_target_pairs={{0,32},{32,0},{1,33},{33,1},{2,34},{34,2},{3,35},{35,3},{4,36},{36... | collective-permute-start | bytes 393224 | tf_op jit(solution)/shard_map/ppermute | solution.py:41
  29.5 2.9 %copy-start = (s32[2,4]{1,0:T(2,128)S(1)}, s32[2,4]{1,0:T(2,128)}, u32[]{:S(2)}) copy-start(s32[2,4]{1,0:T(2,128)} %plan.7) | copy-start | bytes 100
  29.7 2.8 %collective-permute-start.4 = (bf16[4,528,256]{2,1,0:T(8,128)(2,1)S(1)}, bf16[4,528,256]{2,1,0:T(8,128)(2,1)S(1)}, u32[]{:S(2)}, u32[]{:S(2)}) collective-permute-start(bf16[4,528,256]{2,1,0:T(8,128)(2,1)S(1)} %get-tuple-element.14), channel_id=1, source_target_pairs={{0,32},{32,0},{1,33},{33,1},{2,34},{34,2},{3,35},{35,3},{4,36},{36... | collective-permute-start | bytes 3244040 | tf_op jit(solution)/shard_map/ppermute | solution.py:41
  29.7 10.4 %collective-permute-start.3 = (bf16[4,528,256]{2,1,0:T(8,128)(2,1)S(1)}, bf16[4,528,256]{2,1,0:T(8,128)(2,1)S(1)}, u32[]{:S(2)}, u32[]{:S(2)}) collective-permute-start(bf16[4,528,256]{2,1,0:T(8,128)(2,1)S(1)} %get-tuple-element.15), channel_id=1, source_target_pairs={{0,32},{32,0},{1,33},{33,1},{2,34},{34,2},{3,35},{35,3},{4,36},{36... | collective-permute-start | bytes 3244040 | tf_op jit(solution)/shard_map/ppermute | solution.py:41
  39.6 8.3 %collective-permute-start.6 = (s16[1552,256]{1,0:T(8,128)(2,1)S(1)}, s16[1552,256]{1,0:T(8,128)(2,1)S(1)}, u32[]{:S(2)}, u32[]{:S(2)}) collective-permute-start(s16[1552,256]{1,0:T(8,128)(2,1)S(1)} %get-tuple-element.11), channel_id=1, source_target_pairs={{0,32},{32,0},{1,33},{33,1},{2,34},{34,2},{3,35},{35,3},{4,36},{36... | collective-permute-start | bytes 2383880 | tf_op jit(solution)/shard_map/ppermute | solution.py:41
  47.5 2.4 %collective-permute-start.5 = (s16[1552,256]{1,0:T(8,128)(2,1)S(1)}, s16[1552,256]{1,0:T(8,128)(2,1)S(1)}, u32[]{:S(2)}, u32[]{:S(2)}) collective-permute-start(s16[1552,256]{1,0:T(8,128)(2,1)S(1)} %get-tuple-element.10), channel_id=1, source_target_pairs={{0,32},{32,0},{1,33},{33,1},{2,34},{34,2},{3,35},{35,3},{4,36},{36... | collective-permute-start | bytes 2383880 | tf_op jit(solution)/shard_map/ppermute | solution.py:41
  73.9 1.6 %collective-permute-start.7 = (f32[256,256]{1,0:T(8,128)S(1)}, f32[256,256]{1,0:T(8,128)S(1)}, u32[]{:S(2)}, u32[]{:S(2)}) collective-permute-start(f32[256,256]{1,0:T(8,128)S(1)} %get-tuple-element.13), channel_id=1, source_target_pairs={{0,32},{32,0},{1,33},{33,1},{2,34},{34,2},{3,35},{35,3},{4,36},{36... | collective-permute-start | bytes 786440 | tf_op jit(solution)/shard_map/ppermute | solution.py:41

commit v6 on v5

--- a/solution.py
+++ b/solution.py
@@ -41,11 +41,16 @@
     return lax.ppermute(value, "core", [(0, 1), (1, 0)])
 
 
-def encode(block):
-    top = jnp.maximum(jnp.max(jnp.abs(block), axis=0, keepdims=True), 2.0**-100)
-    power = jnp.ceil(jnp.log2(top) * 128.0) + 1.0
-    scaled = block * (PEAK * jnp.exp2(power * (-1.0 / 128.0)))
-    return jnp.floor(scaled + 0.5).astype(jnp.int16), power
+def encode(out, start, load):
+    powers = []
+    for first in range(0, ROWS, 128):
+        block = load(first, first + 128)
+        top = jnp.maximum(jnp.max(jnp.abs(block), axis=0, keepdims=True), 2.0**-100)
+        power = jnp.ceil(jnp.log2(top) * 128.0) + 1.0
+        scaled = block * (PEAK * jnp.exp2(power * (-1.0 / 128.0)))
+        out[start : start + ROWS, first : first + 128] = scaled.astype(jnp.int16)
+        powers.append(power)
+    return jnp.concatenate(powers, axis=1)
 
 
 def decode(code, power):
@@ -93,7 +98,7 @@
 
 def score_kernel(factor, half, plan, mine, theirs, *refs):
     keep, send, sums = refs[-3:]
-    half_scale = 0.5 * factor
+    half_scale = jnp.bfloat16(0.5 * factor)
     half_bias = 0.5 * logit_bias
     wide, deep = 4 * ROWS, 2 * ROWS
     z, y = lax.axis_index("z"), lax.axis_index("y")
@@ -129,9 +134,9 @@
                 rows = jnp.where(here, ids & 511, -1)
                 hit = lax.broadcasted_iota(jnp.int32, (deep, wide), 0) == rows
                 logits = lax.dot_general(
-                    keys, a, (((1,), (1,)), ((), ())), preferred_element_type=jnp.float32
+                    keys * half_scale, a, (((1,), (1,)), ((), ())), preferred_element_type=jnp.float32
                 )
-                weights = 0.5 * jnp.tanh(logits * half_scale + half_bias) + jnp.where(hit, -0.5, 0.5)
+                weights = jnp.tanh(logits + half_bias) + jnp.where(hit, -1.0, 1.0)
                 weights = weights.astype(jnp.bfloat16)
                 gb = jnp.dot(weights, a, preferred_element_type=jnp.float32)
                 ga = lax.dot_general(
@@ -145,16 +150,14 @@
                     add(sums, 0, ga, unit == 0 and slot == 0)
         powers = []
         for i in range(6 if core == 0 else 4):
-            code, power = encode(sums[i])
-            send[i * ROWS : (i + 1) * ROWS, :] = code
-            powers.append(power)
+            powers.append(encode(send, i * ROWS, lambda first, last: sums[i, :, first:last]))
         send[6 * ROWS :, :] = notes(powers)
 
     on_core(body)
 
 
 def pack_kernel(half, plan, keep, got, *refs):
-    out, total, powers = refs[-3:]
+    out, powers = refs[-2:]
 
     def body(core):
         if core == 0:
@@ -166,23 +169,24 @@
             s = half * 4 + i
             written = []
             if core == 0:
-                code, power = encode(keep[s])
-                out[s, 0:ROWS, :] = code
+                power = encode(out.at[s], 0, lambda first, last: keep[s, :, first:last])
                 out[s, ROWS : 2 * ROWS, :] = got[i * ROWS : (i + 1) * ROWS, :]
                 written = [power, got_powers[i : i + 1]]
             else:
                 for c in range(2):
                     group, xh = i % 2 * 2 + c, i // 2
                     slot, kept = place_in(own, group)
-                    value = keep[slot * 4 + half * 2 + xh] * kept
+                    block = slot * 4 + half * 2 + xh
                     slot, used = place_in(mate, group)
                     index = slot * 2 + xh
                     scale = jnp.exp2(powers[pl.ds(index, 1), :] * (1.0 / 128.0)) * (used * (1.0 / PEAK))
-                    code = got[pl.ds(pl.multiple_of(index * ROWS, ROWS), ROWS), :]
-                    total[...] = value + code.astype(jnp.float32) * scale
-                    code, power = encode(total[...])
-                    out[s, c * ROWS : (c + 1) * ROWS, :] = code
-                    written.append(power)
+                    rows = pl.ds(pl.multiple_of(index * ROWS, ROWS), ROWS)
+
+                    def load(first, last):
+                        code = got[rows, first:last].astype(jnp.float32)
+                        return keep[block, :, first:last] * kept + code * scale[:, first:last]
+
+                    written.append(encode(out.at[s], c * ROWS, load))
             out[s, 2 * ROWS :, :] = notes(written)
 
     on_core(body)
@@ -247,7 +251,7 @@
         return call(
             functools.partial(pack_kernel, half),
             jax.ShapeDtypeStruct((8, height, ROWS), i16),
-            [pltpu.VMEM((ROWS, ROWS), f32), pltpu.VMEM((NOTE, ROWS), f32)],
+            [pltpu.VMEM((NOTE, ROWS), f32)],
             1 << 20,
             keep,
             got,
@@ -262,7 +266,7 @@
     got_far = swap_core(send_far)
     packed = pack(1, keep, got_far, pack(0, keep, got_near))
     one = jax.ShapeDtypeStruct((ROWS, ROWS), f32)
-    keep, send = call(functools.partial(sum_kernel, factor), (one, one), [], 1 << 20, meet(packed))
+    keep, send = call(functools.partial(sum_kernel, 0.5 * factor), (one, one), [], 1 << 20, meet(packed))
     got = swap_core(send)
     return jnp.where(core == 0, keep, got), jnp.where(core == 0, got, keep)
 

time: 76.6 us -> 75.1 us (0.980)
  Pallas kernels: 18.5 us -> 16.9 us
    pallas_call x6, Pallas kernels: 18.5 us -> 16.9 us  [call(): pl.pallas_call(kernel, out_shape=shapes, in_specs=[VMEM if plan is None o...]
  transfers between devices with their start and end apart: 8 -> 8, of which waited for: 3 -> 3; matrix products, arithmetic and copies ran while one was open for 2% -> 2% of each run, Pallas kernels for 21% -> 20%
where the time goes in v6:
time: 75.1 us; the launch traced here: 74.9 us
  blocking collectives  46.8 us (62%)
  Pallas kernels  16.9 us (23%)
  waiting for transfers between devices  4.13 us (5%)
  starting transfers between devices  3.68 us (5%)
  other arithmetic  2.45 us (3%)
    all_to_all x2, blocking collectives, meet(): lax.all_to_all(value, AXES, 0, 0, axis_index_groups=teams(), tiled=True)  46.8 us
    pallas_call x6, Pallas kernels, call(): pl.pallas_call(kernel, out_shape=shapes, in_specs=[VMEM if plan is None o...  16.9 us
    ppermute x8, waiting for transfers between devices, swap_core(): return lax.ppermute(value, 'core', [(0, 1), (1, 0)])  4.13 us
    ppermute x8, starting transfers between devices, swap_core(): return lax.ppermute(value, 'core', [(0, 1), (1, 0)])  3.68 us
  transfers between devices with their start and end apart: 8, of which 3 were waited for; matrix products, arithmetic and copies ran while one was open for 2% of the time, Pallas kernels for 20%

profile of v6, /device:TPU:1, one launch (start us, length us, event | category | flops | bytes accessed | tf_op | source)
XLA Modules:
  0.0 74.9 jit_solution(9214604396221503179)
XLA Ops:
  0.6 1.5 %collective-permute-start.2 = (s32[1,256]{1,0:T(1,128)}, s32[1,256]{1,0:T(1,128)S(1)}, u32[]{:S(2)}, u32[]{:S(2)}) collective-permute-start(s32[1,256]{1,0:T(1,128)} %bitcast.1), channel_id=1, source_target_pairs={{0,32},{32,0},{1,33},{33,1},{2,34},{34,2},{3,35},{35,3},{4,36},{36... | collective-permute-start | bytes 3080 | tf_op jit(solution)/shard_map/ppermute | solution.py:41
  2.1 0.1 collective-permute-start
  2.2 0.4 collective-permute-start.1
  2.6 0.9 %broadcast_select_fusion.2.own = bf16[256,256]{1,0:T(8,128)(2,1)S(1)} fusion(bf16[256,256]{1,0:T(8,128)(2,1)} %param.4, bf16[256,256]{1,0:T(8,128)(2,1)} %param.5, pred[]{:T(512)S(6)} %eq.4), kind=kLoop, calls=%fused_computation.2 | loop fusion | flops 65536 | bytes 393217 | tf_op jit(solution)/shard_map/jit(_where)/select_n | solution.py:228
  3.6 0.7 fusion.1
  4.3 0.0 collective-permute-done.2.ids_got
  4.3 0.2 shard_map.59
  4.5 25.0 %all_to_all.10.mine = bf16[8,528,256]{2,1,0:T(8,128)(2,1)S(1)} all-to-all(bf16[8,528,256]{2,1,0:T(8,128)(2,1)S(1)} %shard_map.59), channel_id=1, replica_groups={{0,2,4,6,8,10,12,14},{64,66,68,70,72,74,76,78},{1,3,5,7,9,11,13,15},{65..., dimensions={0} | all-to-all | bytes 4325376 | tf_op jit(solution)/shard_map/all_to_all | solution.py:37
  29.5 0.1 fusion.2
  29.7 0.1 collective-permute-start.4
  29.7 0.5 collective-permute-start.3
  30.2 2.2 %collective-permute-done.4.theirs = bf16[4,528,256]{2,1,0:T(8,128)(2,1)S(1)} collective-permute-done((bf16[4,528,256]{2,1,0:T(8,128)(2,1)S(1)}, bf16[4,528,256]{2,1,0:T(8,128)(2,1)S(1)}, u32[]{:S(2)}, u32[]{:S(2)}) %collective-permute-start.4) | collective-permute-done | bytes 1081376 | tf_op jit(solution)/shard_map/ppermute | solution.py:41
  32.4 6.6 %shard_map.60 = (f32[12,256,256]{2,1,0:T(8,128)S(1)}, s16[1552,256]{1,0:T(8,128)(2,1)S(1)}) custom-call(s32[2,4]{1,0:T(2,128)S(1)} %copy-done, bf16[8,528,256]{2,1,0:T(8,128)(2,1)S(1)} %all_to_all.10.mine, bf16[4,528,256]{2,1,0:T(8,128)(2,1)S(1)} %collective-permute-done.4.theirs), custom_call_target="tpu_custom_call" | custom-call | flops 4831838208 | bytes 8388608 | tf_op jit(solution)/shard_map/pallas_call | solution.py:209
  39.0 0.6 collective-permute-start.6
  39.6 6.6 %shard_map.61 = (f32[12,256,256]{2,1,0:T(8,128)S(1)}, s16[1552,256]{1,0:T(8,128)(2,1)S(1)}) custom-call(s32[2,4]{1,0:T(2,128)S(1)} %copy-done, bf16[8,528,256]{2,1,0:T(8,128)(2,1)S(1)} %all_to_all.10.mine, bf16[4,528,256]{2,1,0:T(8,128)(2,1)S(1)} %collective-permute-done.3.theirs, ...), custom_call_target="tpu_custom_call", output_to_operand_aliasing={{0}: (3, {})} | custom-call | flops 4831838208 | bytes 8388608 | tf_op jit(solution)/shard_map/pallas_call | solution.py:209
  46.2 0.4 collective-permute-start.5
  46.7 1.5 %shard_map.62.refs_0_ = s16[8,528,256]{2,1,0:T(8,128)(2,1)S(1)} custom-call(s32[2,4]{1,0:T(2,128)S(1)} %copy-done, f32[12,256,256]{2,1,0:T(8,128)S(1)} %get-tuple-element.9.keep, s16[1552,256]{1,0:T(8,128)(2,1)S(1)} %collective-permute-done.6.got), custom_call_target="tpu_custom_call" | custom-call | flops 1048576 | bytes 8388608 | tf_op jit(solution)/shard_map/pallas_call | solution.py:209
  48.2 0.4 collective-permute-done.5.got
  48.6 1.5 %shard_map.63 = s16[8,528,256]{2,1,0:T(8,128)(2,1)S(1)} custom-call(s32[2,4]{1,0:T(2,128)S(1)} %copy-done, f32[12,256,256]{2,1,0:T(8,128)S(1)} %get-tuple-element.9.keep, s16[1552,256]{1,0:T(8,128)(2,1)S(1)} %collective-permute-done.5.got, s16[8,528,256]{2,1,0:T(8,128)(2,1)S(1)} %shard_map.62.refs_0_), custom_call_target="tpu_custom_call", output_to_operand_aliasing={{}: (3, {})} | custom-call | flops 1048576 | bytes 8388608 | tf_op jit(solution)/shard_map/pallas_call | solution.py:209
  50.1 21.8 %all_to_all.11.got = s16[8,528,256]{2,1,0:T(8,128)(2,1)S(1)} all-to-all(s16[8,528,256]{2,1,0:T(8,128)(2,1)S(1)} %shard_map.63), channel_id=1, replica_groups={{0,2,4,6,8,10,12,14},{64,66,68,70,72,74,76,78},{1,3,5,7,9,11,13,15},{65..., dimensions={0} | all-to-all | bytes 4325376 | tf_op jit(solution)/shard_map/all_to_all | solution.py:37
  71.9 0.6 shard_map.64
  72.5 0.1 collective-permute-start.7
  72.6 1.5 %collective-permute-done.7 = f32[256,256]{1,0:T(8,128)S(1)} collective-permute-done((f32[256,256]{1,0:T(8,128)S(1)}, f32[256,256]{1,0:T(8,128)S(1)}, u32[]{:S(2)}, u32[]{:S(2)}) %collective-permute-start.7) | collective-permute-done | bytes 262176 | tf_op jit(solution)/shard_map/ppermute | solution.py:41
  74.1 0.8 %broadcast_select_fusion = (f32[256,256]{1,0:T(8,128)}, f32[256,256]{1,0:T(8,128)}) fusion(f32[256,256]{1,0:T(8,128)S(1)} %collective-permute-done.7, f32[256,256]{1,0:T(8,128)S(1)} %get-tuple-element.12, pred[]{:T(512)S(6)} %eq.4), kind=kLoop, calls=%fused_computation | loop fusion | flops 131072 | bytes 1048577 | tf_op jit(solution)/shard_map/jit(_where)/select_n | solution.py:271
  (9 shorter events, 0.0 us)
Async XLA Ops:
  0.6 3.7 %collective-permute-start.2 = (s32[1,256]{1,0:T(1,128)}, s32[1,256]{1,0:T(1,128)S(1)}, u32[]{:S(2)}, u32[]{:S(2)}) collective-permute-start(s32[1,256]{1,0:T(1,128)} %bitcast.1), channel_id=1, source_target_pairs={{0,32},{32,0},{1,33},{33,1},{2,34},{34,2},{3,35},{35,3},{4,36},{36... | collective-permute-start | bytes 3080 | tf_op jit(solution)/shard_map/ppermute | solution.py:41
  2.1 2.2 %collective-permute-start = (bf16[256,256]{1,0:T(8,128)(2,1)}, bf16[256,256]{1,0:T(8,128)(2,1)S(1)}, u32[]{:S(2)}, u32[]{:S(2)}) collective-permute-start(bf16[256,256]{1,0:T(8,128)(2,1)} %param.4), channel_id=1, source_target_pairs={{0,32},{32,0},{1,33},{33,1},{2,34},{34,2},{3,35},{35,3},{4,36},{36... | collective-permute-start | bytes 393224 | tf_op jit(solution)/shard_map/ppermute | solution.py:41
  2.2 2.1 %collective-permute-start.1 = (bf16[256,256]{1,0:T(8,128)(2,1)}, bf16[256,256]{1,0:T(8,128)(2,1)S(1)}, u32[]{:S(2)}, u32[]{:S(2)}) collective-permute-start(bf16[256,256]{1,0:T(8,128)(2,1)} %param.5), channel_id=1, source_target_pairs={{0,32},{32,0},{1,33},{33,1},{2,34},{34,2},{3,35},{35,3},{4,36},{36... | collective-permute-start | bytes 393224 | tf_op jit(solution)/shard_map/ppermute | solution.py:41
  29.5 2.9 %copy-start = (s32[2,4]{1,0:T(2,128)S(1)}, s32[2,4]{1,0:T(2,128)}, u32[]{:S(2)}) copy-start(s32[2,4]{1,0:T(2,128)} %plan.7) | copy-start | bytes 100
  29.7 2.8 %collective-permute-start.4 = (bf16[4,528,256]{2,1,0:T(8,128)(2,1)S(1)}, bf16[4,528,256]{2,1,0:T(8,128)(2,1)S(1)}, u32[]{:S(2)}, u32[]{:S(2)}) collective-permute-start(bf16[4,528,256]{2,1,0:T(8,128)(2,1)S(1)} %get-tuple-element.14), channel_id=1, source_target_pairs={{0,32},{32,0},{1,33},{33,1},{2,34},{34,2},{3,35},{35,3},{4,36},{36... | collective-permute-start | bytes 3244040 | tf_op jit(solution)/shard_map/ppermute | solution.py:41
  29.7 9.8 %collective-permute-start.3 = (bf16[4,528,256]{2,1,0:T(8,128)(2,1)S(1)}, bf16[4,528,256]{2,1,0:T(8,128)(2,1)S(1)}, u32[]{:S(2)}, u32[]{:S(2)}) collective-permute-start(bf16[4,528,256]{2,1,0:T(8,128)(2,1)S(1)} %get-tuple-element.15), channel_id=1, source_target_pairs={{0,32},{32,0},{1,33},{33,1},{2,34},{34,2},{3,35},{35,3},{4,36},{36... | collective-permute-start | bytes 3244040 | tf_op jit(solution)/shard_map/ppermute | solution.py:41
  39.0 7.7 %collective-permute-start.6 = (s16[1552,256]{1,0:T(8,128)(2,1)S(1)}, s16[1552,256]{1,0:T(8,128)(2,1)S(1)}, u32[]{:S(2)}, u32[]{:S(2)}) collective-permute-start(s16[1552,256]{1,0:T(8,128)(2,1)S(1)} %get-tuple-element.11), channel_id=1, source_target_pairs={{0,32},{32,0},{1,33},{33,1},{2,34},{34,2},{3,35},{35,3},{4,36},{36... | collective-permute-start | bytes 2383880 | tf_op jit(solution)/shard_map/ppermute | solution.py:41
  46.2 2.4 %collective-permute-start.5 = (s16[1552,256]{1,0:T(8,128)(2,1)S(1)}, s16[1552,256]{1,0:T(8,128)(2,1)S(1)}, u32[]{:S(2)}, u32[]{:S(2)}) collective-permute-start(s16[1552,256]{1,0:T(8,128)(2,1)S(1)} %get-tuple-element.10), channel_id=1, source_target_pairs={{0,32},{32,0},{1,33},{33,1},{2,34},{34,2},{3,35},{35,3},{4,36},{36... | collective-permute-start | bytes 2383880 | tf_op jit(solution)/shard_map/ppermute | solution.py:41
  72.5 1.6 %collective-permute-start.7 = (f32[256,256]{1,0:T(8,128)S(1)}, f32[256,256]{1,0:T(8,128)S(1)}, u32[]{:S(2)}, u32[]{:S(2)}) collective-permute-start(f32[256,256]{1,0:T(8,128)S(1)} %get-tuple-element.13), channel_id=1, source_target_pairs={{0,32},{32,0},{1,33},{33,1},{2,34},{34,2},{3,35},{35,3},{4,36},{36... | collective-permute-start | bytes 786440 | tf_op jit(solution)/shard_map/ppermute | solution.py:41

commit v7 on v6

--- a/solution.py
+++ b/solution.py
@@ -41,16 +41,14 @@
     return lax.ppermute(value, "core", [(0, 1), (1, 0)])
 
 
-def encode(out, start, load):
-    powers = []
-    for first in range(0, ROWS, 128):
-        block = load(first, first + 128)
-        top = jnp.maximum(jnp.max(jnp.abs(block), axis=0, keepdims=True), 2.0**-100)
-        power = jnp.ceil(jnp.log2(top) * 128.0) + 1.0
-        scaled = block * (PEAK * jnp.exp2(power * (-1.0 / 128.0)))
-        out[start : start + ROWS, first : first + 128] = scaled.astype(jnp.int16)
-        powers.append(power)
-    return jnp.concatenate(powers, axis=1)
+def encode(blocks):
+    tops = [jnp.max(jnp.abs(load()), axis=0, keepdims=True) for load, _ in blocks]
+    top = jnp.maximum(jnp.concatenate(tops, axis=0), 2.0**-100)
+    power = jnp.ceil(jnp.log2(top) * 128.0) + 1.0
+    scale = PEAK * jnp.exp2(power * (-1.0 / 128.0))
+    for i, (load, store) in enumerate(blocks):
+        store((load() * scale[i : i + 1]).astype(jnp.int16))
+    return power
 
 
 def decode(code, power):
@@ -58,7 +56,7 @@
 
 
 def notes(powers):
-    powers = powers + [jnp.zeros((1, ROWS), jnp.float32)] * (NOTE - len(powers))
+    powers = powers + [jnp.zeros((NOTE - sum(p.shape[0] for p in powers), ROWS), jnp.float32)]
     return jnp.concatenate(powers, axis=0).astype(jnp.int16)
 
 
@@ -148,46 +146,62 @@
                 else:
                     add(keep, slot * 4 + unit * 2, gb, half == 0)
                     add(sums, 0, ga, unit == 0 and slot == 0)
-        powers = []
-        for i in range(6 if core == 0 else 4):
-            powers.append(encode(send, i * ROWS, lambda first, last: sums[i, :, first:last]))
-        send[6 * ROWS :, :] = notes(powers)
+
+        def block(i):
+            def store(code):
+                send[i * ROWS : (i + 1) * ROWS, :] = code
+
+            return lambda: sums[i], store
+
+        power = encode([block(i) for i in range(6 if core == 0 else 4)])
+        send[6 * ROWS :, :] = notes([power])
 
     on_core(body)
 
 
 def pack_kernel(half, plan, keep, got, *refs):
-    out, powers = refs[-2:]
-
-    def body(core):
+    out, scales = refs[-2:]
+
+    def body(core):
+        got_powers = got[6 * ROWS :, :].astype(jnp.float32)
+        if core == 1:
+            scales[...] = jnp.exp2(got_powers * (1.0 / 128.0)) * (1.0 / PEAK)
+            own, mate = window(plan, 1), window(plan, 0)
+
+        def kept_block(i):
+            s = half * 4 + i
+
+            def store(code):
+                out[s, 0:ROWS, :] = code
+
+            return lambda: keep[s], store
+
+        def summed_block(i, c):
+            group, xh = i % 2 * 2 + c, i // 2
+            slot, kept = place_in(own, group)
+            block = slot * 4 + half * 2 + xh
+            slot, used = place_in(mate, group)
+            index = slot * 2 + xh
+            rows = pl.ds(pl.multiple_of(index * ROWS, ROWS), ROWS)
+
+            def load():
+                code = got[rows, :].astype(jnp.float32)
+                return keep[block] * kept + code * (scales[pl.ds(index, 1), :] * used)
+
+            def store(code):
+                out[half * 4 + i, c * ROWS : (c + 1) * ROWS, :] = code
+
+            return load, store
+
         if core == 0:
-            got_powers = got[6 * ROWS :, :].astype(jnp.float32)
+            power = encode([kept_block(i) for i in range(4)])
+            for i in range(4):
+                out[half * 4 + i, ROWS : 2 * ROWS, :] = got[i * ROWS : (i + 1) * ROWS, :]
+                out[half * 4 + i, 2 * ROWS :, :] = notes([power[i : i + 1], got_powers[i : i + 1]])
         else:
-            powers[...] = got[6 * ROWS :, :].astype(jnp.float32)
-            own, mate = window(plan, 1), window(plan, 0)
-        for i in range(4):
-            s = half * 4 + i
-            written = []
-            if core == 0:
-                power = encode(out.at[s], 0, lambda first, last: keep[s, :, first:last])
-                out[s, ROWS : 2 * ROWS, :] = got[i * ROWS : (i + 1) * ROWS, :]
-                written = [power, got_powers[i : i + 1]]
-            else:
-                for c in range(2):
-                    group, xh = i % 2 * 2 + c, i // 2
-                    slot, kept = place_in(own, group)
-                    block = slot * 4 + half * 2 + xh
-                    slot, used = place_in(mate, group)
-                    index = slot * 2 + xh
-                    scale = jnp.exp2(powers[pl.ds(index, 1), :] * (1.0 / 128.0)) * (used * (1.0 / PEAK))
-                    rows = pl.ds(pl.multiple_of(index * ROWS, ROWS), ROWS)
-
-                    def load(first, last):
-                        code = got[rows, first:last].astype(jnp.float32)
-                        return keep[block, :, first:last] * kept + code * scale[:, first:last]
-
-                    written.append(encode(out.at[s], c * ROWS, load))
-            out[s, 2 * ROWS :, :] = notes(written)
+            power = encode([summed_block(i, c) for i in range(4) for c in range(2)])
+            for i in range(4):
+                out[half * 4 + i, 2 * ROWS :, :] = notes([power[2 * i : 2 * i + 2]])
 
     on_core(body)
 

time: 75.1 us -> 75.3 us (level)
  no operation moved by 1% of the time
where the time goes in v7:
time: 75.3 us; the launch traced here: 75.1 us
  blocking collectives  46.8 us (62%)
  Pallas kernels  17.6 us (23%)
  waiting for transfers between devices  3.91 us (5%)
  starting transfers between devices  3.38 us (4%)
  other arithmetic  2.45 us (3%)
    all_to_all x2, blocking collectives, meet(): lax.all_to_all(value, AXES, 0, 0, axis_index_groups=teams(), tiled=True)  46.8 us
    pallas_call x6, Pallas kernels, call(): pl.pallas_call(kernel, out_shape=shapes, in_specs=[VMEM if plan is None o...  17.6 us
    ppermute x8, waiting for transfers between devices, swap_core(): return lax.ppermute(value, 'core', [(0, 1), (1, 0)])  3.91 us
    ppermute x8, starting transfers between devices, swap_core(): return lax.ppermute(value, 'core', [(0, 1), (1, 0)])  3.38 us
  transfers between devices with their start and end apart: 8, of which 3 were waited for; matrix products, arithmetic and copies ran while one was open for 2% of the time, Pallas kernels for 20%

profile of v7, /device:TPU:1, one launch (start us, length us, event | category | flops | bytes accessed | tf_op | source)
XLA Modules:
  0.0 75.1 jit_solution(17528027597843239343)
XLA Ops:
  0.6 1.5 %collective-permute-start.2 = (s32[1,256]{1,0:T(1,128)}, s32[1,256]{1,0:T(1,128)S(1)}, u32[]{:S(2)}, u32[]{:S(2)}) collective-permute-start(s32[1,256]{1,0:T(1,128)} %bitcast.1), channel_id=1, source_target_pairs={{0,32},{32,0},{1,33},{33,1},{2,34},{34,2},{3,35},{35,3},{4,36},{36... | collective-permute-start | bytes 3080 | tf_op jit(solution)/shard_map/ppermute | solution.py:41
  2.1 0.1 collective-permute-start
  2.2 0.4 collective-permute-start.1
  2.6 0.9 %broadcast_select_fusion.2.own = bf16[256,256]{1,0:T(8,128)(2,1)S(1)} fusion(bf16[256,256]{1,0:T(8,128)(2,1)} %param.4, bf16[256,256]{1,0:T(8,128)(2,1)} %param.5, pred[]{:T(512)S(6)} %eq.4), kind=kLoop, calls=%fused_computation.2 | loop fusion | flops 65536 | bytes 393217 | tf_op jit(solution)/shard_map/jit(_where)/select_n | solution.py:242
  3.6 0.7 fusion.1
  4.3 0.0 collective-permute-done.2.ids_got
  4.3 0.2 shard_map.59
  4.5 25.0 %all_to_all.10.mine = bf16[8,528,256]{2,1,0:T(8,128)(2,1)S(1)} all-to-all(bf16[8,528,256]{2,1,0:T(8,128)(2,1)S(1)} %shard_map.59), channel_id=1, replica_groups={{0,2,4,6,8,10,12,14},{64,66,68,70,72,74,76,78},{1,3,5,7,9,11,13,15},{65..., dimensions={0} | all-to-all | bytes 4325376 | tf_op jit(solution)/shard_map/all_to_all | solution.py:37
  29.5 0.1 fusion.2
  29.7 0.1 collective-permute-start.4
  29.7 0.5 collective-permute-start.3
  30.2 2.2 %collective-permute-done.4.theirs = bf16[4,528,256]{2,1,0:T(8,128)(2,1)S(1)} collective-permute-done((bf16[4,528,256]{2,1,0:T(8,128)(2,1)S(1)}, bf16[4,528,256]{2,1,0:T(8,128)(2,1)S(1)}, u32[]{:S(2)}, u32[]{:S(2)}) %collective-permute-start.4) | collective-permute-done | bytes 1081376 | tf_op jit(solution)/shard_map/ppermute | solution.py:41
  32.4 6.6 %shard_map.60 = (f32[12,256,256]{2,1,0:T(8,128)S(1)}, s16[1552,256]{1,0:T(8,128)(2,1)S(1)}) custom-call(s32[2,4]{1,0:T(2,128)S(1)} %copy-done, bf16[8,528,256]{2,1,0:T(8,128)(2,1)S(1)} %all_to_all.10.mine, bf16[4,528,256]{2,1,0:T(8,128)(2,1)S(1)} %collective-permute-done.4.theirs), custom_call_target="tpu_custom_call" | custom-call | flops 4831838208 | bytes 8388608 | tf_op jit(solution)/shard_map/pallas_call | solution.py:223
  39.1 0.3 collective-permute-start.6
  39.4 6.7 %shard_map.61 = (f32[12,256,256]{2,1,0:T(8,128)S(1)}, s16[1552,256]{1,0:T(8,128)(2,1)S(1)}) custom-call(s32[2,4]{1,0:T(2,128)S(1)} %copy-done, bf16[8,528,256]{2,1,0:T(8,128)(2,1)S(1)} %all_to_all.10.mine, bf16[4,528,256]{2,1,0:T(8,128)(2,1)S(1)} %collective-permute-done.3.theirs, ...), custom_call_target="tpu_custom_call", output_to_operand_aliasing={{0}: (3, {})} | custom-call | flops 4831838208 | bytes 8388608 | tf_op jit(solution)/shard_map/pallas_call | solution.py:223
  46.1 0.4 collective-permute-start.5
  46.5 1.8 %shard_map.62.refs_0_ = s16[8,528,256]{2,1,0:T(8,128)(2,1)S(1)} custom-call(s32[2,4]{1,0:T(2,128)S(1)} %copy-done, f32[12,256,256]{2,1,0:T(8,128)S(1)} %get-tuple-element.9.keep, s16[1552,256]{1,0:T(8,128)(2,1)S(1)} %collective-permute-done.6.got), custom_call_target="tpu_custom_call" | custom-call | flops 1048576 | bytes 8388608 | tf_op jit(solution)/shard_map/pallas_call | solution.py:223
  48.3 0.2 collective-permute-done.5.got
  48.5 1.8 %shard_map.63 = s16[8,528,256]{2,1,0:T(8,128)(2,1)S(1)} custom-call(s32[2,4]{1,0:T(2,128)S(1)} %copy-done, f32[12,256,256]{2,1,0:T(8,128)S(1)} %get-tuple-element.9.keep, s16[1552,256]{1,0:T(8,128)(2,1)S(1)} %collective-permute-done.5.got, s16[8,528,256]{2,1,0:T(8,128)(2,1)S(1)} %shard_map.62.refs_0_), custom_call_target="tpu_custom_call", output_to_operand_aliasing={{}: (3, {})} | custom-call | flops 1048576 | bytes 8388608 | tf_op jit(solution)/shard_map/pallas_call | solution.py:223
  50.3 21.8 %all_to_all.11.got = s16[8,528,256]{2,1,0:T(8,128)(2,1)S(1)} all-to-all(s16[8,528,256]{2,1,0:T(8,128)(2,1)S(1)} %shard_map.63), channel_id=1, replica_groups={{0,2,4,6,8,10,12,14},{64,66,68,70,72,74,76,78},{1,3,5,7,9,11,13,15},{65..., dimensions={0} | all-to-all | bytes 4325376 | tf_op jit(solution)/shard_map/all_to_all | solution.py:37
  72.1 0.6 shard_map.64
  72.6 0.1 collective-permute-start.7
  72.7 1.5 %collective-permute-done.7 = f32[256,256]{1,0:T(8,128)S(1)} collective-permute-done((f32[256,256]{1,0:T(8,128)S(1)}, f32[256,256]{1,0:T(8,128)S(1)}, u32[]{:S(2)}, u32[]{:S(2)}) %collective-permute-start.7) | collective-permute-done | bytes 262176 | tf_op jit(solution)/shard_map/ppermute | solution.py:41
  74.3 0.8 %broadcast_select_fusion = (f32[256,256]{1,0:T(8,128)}, f32[256,256]{1,0:T(8,128)}) fusion(f32[256,256]{1,0:T(8,128)S(1)} %collective-permute-done.7, f32[256,256]{1,0:T(8,128)S(1)} %get-tuple-element.12, pred[]{:T(512)S(6)} %eq.4), kind=kLoop, calls=%fused_computation | loop fusion | flops 131072 | bytes 1048577 | tf_op jit(solution)/shard_map/jit(_where)/select_n | solution.py:285
  (9 shorter events, 0.0 us)
Async XLA Ops:
  0.6 3.7 %collective-permute-start.2 = (s32[1,256]{1,0:T(1,128)}, s32[1,256]{1,0:T(1,128)S(1)}, u32[]{:S(2)}, u32[]{:S(2)}) collective-permute-start(s32[1,256]{1,0:T(1,128)} %bitcast.1), channel_id=1, source_target_pairs={{0,32},{32,0},{1,33},{33,1},{2,34},{34,2},{3,35},{35,3},{4,36},{36... | collective-permute-start | bytes 3080 | tf_op jit(solution)/shard_map/ppermute | solution.py:41
  2.1 2.2 %collective-permute-start = (bf16[256,256]{1,0:T(8,128)(2,1)}, bf16[256,256]{1,0:T(8,128)(2,1)S(1)}, u32[]{:S(2)}, u32[]{:S(2)}) collective-permute-start(bf16[256,256]{1,0:T(8,128)(2,1)} %param.4), channel_id=1, source_target_pairs={{0,32},{32,0},{1,33},{33,1},{2,34},{34,2},{3,35},{35,3},{4,36},{36... | collective-permute-start | bytes 393224 | tf_op jit(solution)/shard_map/ppermute | solution.py:41
  2.2 2.1 %collective-permute-start.1 = (bf16[256,256]{1,0:T(8,128)(2,1)}, bf16[256,256]{1,0:T(8,128)(2,1)S(1)}, u32[]{:S(2)}, u32[]{:S(2)}) collective-permute-start(bf16[256,256]{1,0:T(8,128)(2,1)} %param.5), channel_id=1, source_target_pairs={{0,32},{32,0},{1,33},{33,1},{2,34},{34,2},{3,35},{35,3},{4,36},{36... | collective-permute-start | bytes 393224 | tf_op jit(solution)/shard_map/ppermute | solution.py:41
  29.5 2.9 %copy-start = (s32[2,4]{1,0:T(2,128)S(1)}, s32[2,4]{1,0:T(2,128)}, u32[]{:S(2)}) copy-start(s32[2,4]{1,0:T(2,128)} %plan.7) | copy-start | bytes 100
  29.7 2.8 %collective-permute-start.4 = (bf16[4,528,256]{2,1,0:T(8,128)(2,1)S(1)}, bf16[4,528,256]{2,1,0:T(8,128)(2,1)S(1)}, u32[]{:S(2)}, u32[]{:S(2)}) collective-permute-start(bf16[4,528,256]{2,1,0:T(8,128)(2,1)S(1)} %get-tuple-element.14), channel_id=1, source_target_pairs={{0,32},{32,0},{1,33},{33,1},{2,34},{34,2},{3,35},{35,3},{4,36},{36... | collective-permute-start | bytes 3244040 | tf_op jit(solution)/shard_map/ppermute | solution.py:41
  29.7 9.6 %collective-permute-start.3 = (bf16[4,528,256]{2,1,0:T(8,128)(2,1)S(1)}, bf16[4,528,256]{2,1,0:T(8,128)(2,1)S(1)}, u32[]{:S(2)}, u32[]{:S(2)}) collective-permute-start(bf16[4,528,256]{2,1,0:T(8,128)(2,1)S(1)} %get-tuple-element.15), channel_id=1, source_target_pairs={{0,32},{32,0},{1,33},{33,1},{2,34},{34,2},{3,35},{35,3},{4,36},{36... | collective-permute-start | bytes 3244040 | tf_op jit(solution)/shard_map/ppermute | solution.py:41
  39.1 7.4 %collective-permute-start.6 = (s16[1552,256]{1,0:T(8,128)(2,1)S(1)}, s16[1552,256]{1,0:T(8,128)(2,1)S(1)}, u32[]{:S(2)}, u32[]{:S(2)}) collective-permute-start(s16[1552,256]{1,0:T(8,128)(2,1)S(1)} %get-tuple-element.11), channel_id=1, source_target_pairs={{0,32},{32,0},{1,33},{33,1},{2,34},{34,2},{3,35},{35,3},{4,36},{36... | collective-permute-start | bytes 2383880 | tf_op jit(solution)/shard_map/ppermute | solution.py:41
  46.1 2.4 %collective-permute-start.5 = (s16[1552,256]{1,0:T(8,128)(2,1)S(1)}, s16[1552,256]{1,0:T(8,128)(2,1)S(1)}, u32[]{:S(2)}, u32[]{:S(2)}) collective-permute-start(s16[1552,256]{1,0:T(8,128)(2,1)S(1)} %get-tuple-element.10), channel_id=1, source_target_pairs={{0,32},{32,0},{1,33},{33,1},{2,34},{34,2},{3,35},{35,3},{4,36},{36... | collective-permute-start | bytes 2383880 | tf_op jit(solution)/shard_map/ppermute | solution.py:41
  72.6 1.6 %collective-permute-start.7 = (f32[256,256]{1,0:T(8,128)S(1)}, f32[256,256]{1,0:T(8,128)S(1)}, u32[]{:S(2)}, u32[]{:S(2)}) collective-permute-start(f32[256,256]{1,0:T(8,128)S(1)} %get-tuple-element.13), channel_id=1, source_target_pairs={{0,32},{32,0},{1,33},{33,1},{2,34},{34,2},{3,35},{35,3},{4,36},{36... | collective-permute-start | bytes 786440 | tf_op jit(solution)/shard_map/ppermute | solution.py:41

commit v8 on v6

--- a/solution.py
+++ b/solution.py
@@ -15,7 +15,6 @@
 NOTE = 16
 PEAK = 32000.0
 VMEM = pl.BlockSpec(memory_space=pltpu.VMEM)
-SMEM = pl.BlockSpec(memory_space=pltpu.SMEM)
 
 
 def member(xl, core, z, y, xh):
@@ -70,7 +69,8 @@
 
 def window(plan, core):
     group = lax.axis_index("xl") * 2 + core
-    return [group, plan[0, group], plan[1, group]]
+    value = plan[...]
+    return [group, group ^ value[0, 0], group ^ value[1, 0]]
 
 
 def place_in(owners, group):
@@ -209,7 +209,7 @@
     return pl.pallas_call(
         kernel,
         out_shape=shapes,
-        in_specs=[VMEM if plan is None or i else SMEM for i in range(len(operands))],
+        in_specs=[VMEM] * len(operands),
         out_specs=jax.tree.map(lambda _: VMEM, shapes),
         scratch_shapes=scratch,
         input_output_aliases=aliases,

time: 75.1 us -> 73.4 us (0.977)
  Pallas kernels: 16.9 us -> 14.6 us
    pallas_call x6, Pallas kernels: 16.9 us -> 14.6 us  [call(): pl.pallas_call(kernel, out_shape=shapes, in_specs=[VMEM] * len(operands),...]
  transfers between devices with their start and end apart: 8 -> 8, of which waited for: 3 -> 3; matrix products, arithmetic and copies ran while one was open for 2% -> 2% of each run, Pallas kernels for 20% -> 18%
where the time goes in v8:
time: 73.4 us; the launch traced here: 73.2 us
  blocking collectives  46.8 us (64%)
  Pallas kernels  14.6 us (20%)
  waiting for transfers between devices  4.68 us (6%)
  starting transfers between devices  3.69 us (5%)
  other arithmetic  2.45 us (3%)
  between operations  0.74 us (1%)
    all_to_all x2, blocking collectives, meet(): lax.all_to_all(value, AXES, 0, 0, axis_index_groups=teams(), tiled=True)  46.8 us
    pallas_call x6, Pallas kernels, call(): pl.pallas_call(kernel, out_shape=shapes, in_specs=[VMEM] * len(operands),...  14.6 us
    ppermute x8, waiting for transfers between devices, swap_core(): return lax.ppermute(value, 'core', [(0, 1), (1, 0)])  4.68 us
    ppermute x8, starting transfers between devices, swap_core(): return lax.ppermute(value, 'core', [(0, 1), (1, 0)])  3.69 us
  transfers between devices with their start and end apart: 8, of which 3 were waited for; matrix products, arithmetic and copies ran while one was open for 2% of the time, Pallas kernels for 18%

profile of v8, /device:TPU:1, one launch (start us, length us, event | category | flops | bytes accessed | tf_op | source)
XLA Modules:
  0.0 73.2 jit_solution(10130843679263788191)
XLA Ops:
  0.6 1.5 %collective-permute-start.2 = (s32[1,256]{1,0:T(1,128)}, s32[1,256]{1,0:T(1,128)S(1)}, u32[]{:S(2)}, u32[]{:S(2)}) collective-permute-start(s32[1,256]{1,0:T(1,128)} %bitcast.1), channel_id=1, source_target_pairs={{0,32},{32,0},{1,33},{33,1},{2,34},{34,2},{3,35},{35,3},{4,36},{36... | collective-permute-start | bytes 3080 | tf_op jit(solution)/shard_map/ppermute | solution.py:40
  2.1 0.1 collective-permute-start
  2.2 0.4 collective-permute-start.1
  2.6 0.9 %broadcast_select_fusion.2.own = bf16[256,256]{1,0:T(8,128)(2,1)S(1)} fusion(bf16[256,256]{1,0:T(8,128)(2,1)} %param.4, bf16[256,256]{1,0:T(8,128)(2,1)} %param.5, pred[]{:T(512)S(6)} %eq.4), kind=kLoop, calls=%fused_computation.2 | loop fusion | flops 65536 | bytes 393217 | tf_op jit(solution)/shard_map/jit(_where)/select_n | solution.py:228
  3.6 0.7 fusion.1
  4.3 0.0 collective-permute-done.2.ids_got
  4.3 0.2 shard_map.59
  4.5 25.0 %all_to_all.10.mine = bf16[8,528,256]{2,1,0:T(8,128)(2,1)S(1)} all-to-all(bf16[8,528,256]{2,1,0:T(8,128)(2,1)S(1)} %shard_map.59), channel_id=1, replica_groups={{0,2,4,6,8,10,12,14},{64,66,68,70,72,74,76,78},{1,3,5,7,9,11,13,15},{65..., dimensions={0} | all-to-all | bytes 4325376 | tf_op jit(solution)/shard_map/all_to_all | solution.py:36
  29.5 0.1 fusion.2
  29.7 0.1 collective-permute-start.4
  29.7 0.5 collective-permute-start.3
  30.2 2.2 %collective-permute-done.4.theirs = bf16[4,528,256]{2,1,0:T(8,128)(2,1)S(1)} collective-permute-done((bf16[4,528,256]{2,1,0:T(8,128)(2,1)S(1)}, bf16[4,528,256]{2,1,0:T(8,128)(2,1)S(1)}, u32[]{:S(2)}, u32[]{:S(2)}) %collective-permute-start.4) | collective-permute-done | bytes 1081376 | tf_op jit(solution)/shard_map/ppermute | solution.py:40
  32.4 6.0 %shard_map.60 = (f32[12,256,256]{2,1,0:T(8,128)S(1)}, s16[1552,256]{1,0:T(8,128)(2,1)S(1)}) custom-call(s32[2,4]{1,0:T(2,128)S(1)} %copy-done, bf16[8,528,256]{2,1,0:T(8,128)(2,1)S(1)} %all_to_all.10.mine, bf16[4,528,256]{2,1,0:T(8,128)(2,1)S(1)} %collective-permute-done.4.theirs), custom_call_target="tpu_custom_call" | custom-call | flops 4831838208 | bytes 8388608 | tf_op jit(solution)/shard_map/pallas_call | solution.py:209
  38.4 0.6 collective-permute-start.6
  39.0 6.0 %shard_map.61 = (f32[12,256,256]{2,1,0:T(8,128)S(1)}, s16[1552,256]{1,0:T(8,128)(2,1)S(1)}) custom-call(s32[2,4]{1,0:T(2,128)S(1)} %copy-done, bf16[8,528,256]{2,1,0:T(8,128)(2,1)S(1)} %all_to_all.10.mine, bf16[4,528,256]{2,1,0:T(8,128)(2,1)S(1)} %collective-permute-done.3.theirs, ...), custom_call_target="tpu_custom_call", output_to_operand_aliasing={{0}: (3, {})} | custom-call | flops 4831838208 | bytes 8388608 | tf_op jit(solution)/shard_map/pallas_call | solution.py:209
  45.0 0.4 collective-permute-start.5
  45.5 1.0 %shard_map.62.refs_0_ = s16[8,528,256]{2,1,0:T(8,128)(2,1)S(1)} custom-call(s32[2,4]{1,0:T(2,128)S(1)} %copy-done, f32[12,256,256]{2,1,0:T(8,128)S(1)} %get-tuple-element.9.keep, s16[1552,256]{1,0:T(8,128)(2,1)S(1)} %collective-permute-done.6.got), custom_call_target="tpu_custom_call" | custom-call | flops 1048576 | bytes 8388608 | tf_op jit(solution)/shard_map/pallas_call | solution.py:209
  46.5 0.9 %collective-permute-done.5.got = s16[1552,256]{1,0:T(8,128)(2,1)S(1)} collective-permute-done((s16[1552,256]{1,0:T(8,128)(2,1)S(1)}, s16[1552,256]{1,0:T(8,128)(2,1)S(1)}, u32[]{:S(2)}, u32[]{:S(2)}) %collective-permute-start.5) | collective-permute-done | bytes 794656 | tf_op jit(solution)/shard_map/ppermute | solution.py:40
  47.4 0.9 %shard_map.63 = s16[8,528,256]{2,1,0:T(8,128)(2,1)S(1)} custom-call(s32[2,4]{1,0:T(2,128)S(1)} %copy-done, f32[12,256,256]{2,1,0:T(8,128)S(1)} %get-tuple-element.9.keep, s16[1552,256]{1,0:T(8,128)(2,1)S(1)} %collective-permute-done.5.got, s16[8,528,256]{2,1,0:T(8,128)(2,1)S(1)} %shard_map.62.refs_0_), custom_call_target="tpu_custom_call", output_to_operand_aliasing={{}: (3, {})} | custom-call | flops 1048576 | bytes 8388608 | tf_op jit(solution)/shard_map/pallas_call | solution.py:209
  48.3 21.8 %all_to_all.11.got = s16[8,528,256]{2,1,0:T(8,128)(2,1)S(1)} all-to-all(s16[8,528,256]{2,1,0:T(8,128)(2,1)S(1)} %shard_map.63), channel_id=1, replica_groups={{0,2,4,6,8,10,12,14},{64,66,68,70,72,74,76,78},{1,3,5,7,9,11,13,15},{65..., dimensions={0} | all-to-all | bytes 4325376 | tf_op jit(solution)/shard_map/all_to_all | solution.py:36
  70.2 0.6 shard_map.64
  70.7 0.1 collective-permute-start.7
  70.8 1.5 %collective-permute-done.7 = f32[256,256]{1,0:T(8,128)S(1)} collective-permute-done((f32[256,256]{1,0:T(8,128)S(1)}, f32[256,256]{1,0:T(8,128)S(1)}, u32[]{:S(2)}, u32[]{:S(2)}) %collective-permute-start.7) | collective-permute-done | bytes 262176 | tf_op jit(solution)/shard_map/ppermute | solution.py:40
  72.3 0.8 %broadcast_select_fusion = (f32[256,256]{1,0:T(8,128)}, f32[256,256]{1,0:T(8,128)}) fusion(f32[256,256]{1,0:T(8,128)S(1)} %collective-permute-done.7, f32[256,256]{1,0:T(8,128)S(1)} %get-tuple-element.12, pred[]{:T(512)S(6)} %eq.4), kind=kLoop, calls=%fused_computation | loop fusion | flops 131072 | bytes 1048577 | tf_op jit(solution)/shard_map/jit(_where)/select_n | solution.py:271
  (9 shorter events, 0.0 us)
Async XLA Ops:
  0.6 3.7 %collective-permute-start.2 = (s32[1,256]{1,0:T(1,128)}, s32[1,256]{1,0:T(1,128)S(1)}, u32[]{:S(2)}, u32[]{:S(2)}) collective-permute-start(s32[1,256]{1,0:T(1,128)} %bitcast.1), channel_id=1, source_target_pairs={{0,32},{32,0},{1,33},{33,1},{2,34},{34,2},{3,35},{35,3},{4,36},{36... | collective-permute-start | bytes 3080 | tf_op jit(solution)/shard_map/ppermute | solution.py:40
  2.1 2.2 %collective-permute-start = (bf16[256,256]{1,0:T(8,128)(2,1)}, bf16[256,256]{1,0:T(8,128)(2,1)S(1)}, u32[]{:S(2)}, u32[]{:S(2)}) collective-permute-start(bf16[256,256]{1,0:T(8,128)(2,1)} %param.4), channel_id=1, source_target_pairs={{0,32},{32,0},{1,33},{33,1},{2,34},{34,2},{3,35},{35,3},{4,36},{36... | collective-permute-start | bytes 393224 | tf_op jit(solution)/shard_map/ppermute | solution.py:40
  2.2 2.1 %collective-permute-start.1 = (bf16[256,256]{1,0:T(8,128)(2,1)}, bf16[256,256]{1,0:T(8,128)(2,1)S(1)}, u32[]{:S(2)}, u32[]{:S(2)}) collective-permute-start(bf16[256,256]{1,0:T(8,128)(2,1)} %param.5), channel_id=1, source_target_pairs={{0,32},{32,0},{1,33},{33,1},{2,34},{34,2},{3,35},{35,3},{4,36},{36... | collective-permute-start | bytes 393224 | tf_op jit(solution)/shard_map/ppermute | solution.py:40
  29.5 2.9 %copy-start = (s32[2,4]{1,0:T(2,128)S(1)}, s32[2,4]{1,0:T(2,128)}, u32[]{:S(2)}) copy-start(s32[2,4]{1,0:T(2,128)} %plan.7) | copy-start | bytes 100
  29.7 2.8 %collective-permute-start.4 = (bf16[4,528,256]{2,1,0:T(8,128)(2,1)S(1)}, bf16[4,528,256]{2,1,0:T(8,128)(2,1)S(1)}, u32[]{:S(2)}, u32[]{:S(2)}) collective-permute-start(bf16[4,528,256]{2,1,0:T(8,128)(2,1)S(1)} %get-tuple-element.14), channel_id=1, source_target_pairs={{0,32},{32,0},{1,33},{33,1},{2,34},{34,2},{3,35},{35,3},{4,36},{36... | collective-permute-start | bytes 3244040 | tf_op jit(solution)/shard_map/ppermute | solution.py:40
  29.7 9.2 %collective-permute-start.3 = (bf16[4,528,256]{2,1,0:T(8,128)(2,1)S(1)}, bf16[4,528,256]{2,1,0:T(8,128)(2,1)S(1)}, u32[]{:S(2)}, u32[]{:S(2)}) collective-permute-start(bf16[4,528,256]{2,1,0:T(8,128)(2,1)S(1)} %get-tuple-element.15), channel_id=1, source_target_pairs={{0,32},{32,0},{1,33},{33,1},{2,34},{34,2},{3,35},{35,3},{4,36},{36... | collective-permute-start | bytes 3244040 | tf_op jit(solution)/shard_map/ppermute | solution.py:40
  38.4 7.1 %collective-permute-start.6 = (s16[1552,256]{1,0:T(8,128)(2,1)S(1)}, s16[1552,256]{1,0:T(8,128)(2,1)S(1)}, u32[]{:S(2)}, u32[]{:S(2)}) collective-permute-start(s16[1552,256]{1,0:T(8,128)(2,1)S(1)} %get-tuple-element.11), channel_id=1, source_target_pairs={{0,32},{32,0},{1,33},{33,1},{2,34},{34,2},{3,35},{35,3},{4,36},{36... | collective-permute-start | bytes 2383880 | tf_op jit(solution)/shard_map/ppermute | solution.py:40
  45.0 2.4 %collective-permute-start.5 = (s16[1552,256]{1,0:T(8,128)(2,1)S(1)}, s16[1552,256]{1,0:T(8,128)(2,1)S(1)}, u32[]{:S(2)}, u32[]{:S(2)}) collective-permute-start(s16[1552,256]{1,0:T(8,128)(2,1)S(1)} %get-tuple-element.10), channel_id=1, source_target_pairs={{0,32},{32,0},{1,33},{33,1},{2,34},{34,2},{3,35},{35,3},{4,36},{36... | collective-permute-start | bytes 2383880 | tf_op jit(solution)/shard_map/ppermute | solution.py:40
  70.7 1.6 %collective-permute-start.7 = (f32[256,256]{1,0:T(8,128)S(1)}, f32[256,256]{1,0:T(8,128)S(1)}, u32[]{:S(2)}, u32[]{:S(2)}) collective-permute-start(f32[256,256]{1,0:T(8,128)S(1)} %get-tuple-element.13), channel_id=1, source_target_pairs={{0,32},{32,0},{1,33},{33,1},{2,34},{34,2},{3,35},{35,3},{4,36},{36... | collective-permute-start | bytes 786440 | tf_op jit(solution)/shard_map/ppermute | solution.py:40

commit v9 on v8

--- a/solution.py
+++ b/solution.py
@@ -100,7 +100,6 @@
     keep, send, sums = refs[-3:]
     half_scale = jnp.bfloat16(0.5 * factor)
     half_bias = 0.5 * logit_bias
-    wide, deep = 4 * ROWS, 2 * ROWS
     z, y = lax.axis_index("z"), lax.axis_index("y")
     outer = jnp.logical_or(z == 0, z == 3)
 
@@ -113,41 +112,41 @@
 
     def body(core):
         owners = window(plan, core)
-        for unit in range(2):
-            a_from, a_source = (mine, 4 * unit) if core == 0 else (theirs, 0)
-            a = [a_from[a_source + s, core * ROWS : (core + 1) * ROWS, :] for s in range(4)]
-            a = jnp.concatenate(a, axis=0)
-            ids = []
-            for s in range(4):
-                note = a_from[a_source + s, 2 * ROWS :, :].astype(jnp.float32)[2 * core : 2 * core + 2]
-                ids.append((note[0:1] * 256.0 + note[1:2]).astype(jnp.int32))
-            ids = jnp.concatenate(ids, axis=1)
-            far = half if core == 0 else unit
-            level = jnp.where(outer, 3 * far, 1 + far)
-            for slot in range(3):
-                group = owners[slot]
-                b_from, b_source = (theirs, 0) if core == 0 else (mine, 4 * unit)
-                b_rows = pl.ds(pl.multiple_of(group % 2 * ROWS, ROWS), ROWS)
-                keys = [b_from[b_source + 2 * xh + group // 2, b_rows, :] for xh in range(2)]
-                keys = jnp.concatenate(keys, axis=0)
+        a_from, b_from = (mine, theirs) if core == 0 else (theirs, mine)
+        a = [a_from[s, core * ROWS : (core + 1) * ROWS, :] for s in range(a_from.shape[0])]
+        a = jnp.concatenate(a, axis=0)
+        ids = []
+        for s in range(a_from.shape[0]):
+            note = a_from[s, 2 * ROWS :, :].astype(jnp.float32)[2 * core : 2 * core + 2]
+            ids.append((note[0:1] * 256.0 + note[1:2]).astype(jnp.int32))
+        ids = jnp.concatenate(ids, axis=1)
+        for slot in range(3):
+            group = owners[slot]
+            b_rows = pl.ds(pl.multiple_of(group % 2 * ROWS, ROWS), ROWS)
+            keys, rows = [], jnp.full_like(ids, -1)
+            for unit in range(b_from.shape[0] // 4):
+                keys += [b_from[4 * unit + 2 * xh + group // 2, b_rows, :] for xh in range(2)]
+                far = half if core == 0 else unit
+                level = jnp.where(outer, 3 * far, 1 + far)
                 here = lax.shift_right_logical(ids, 9) == group * 16 + level * 4 + y
-                rows = jnp.where(here, ids & 511, -1)
-                hit = lax.broadcasted_iota(jnp.int32, (deep, wide), 0) == rows
-                logits = lax.dot_general(
-                    keys * half_scale, a, (((1,), (1,)), ((), ())), preferred_element_type=jnp.float32
-                )
-                weights = jnp.tanh(logits + half_bias) + jnp.where(hit, -1.0, 1.0)
-                weights = weights.astype(jnp.bfloat16)
-                gb = jnp.dot(weights, a, preferred_element_type=jnp.float32)
-                ga = lax.dot_general(
-                    weights, keys, (((0,), (0,)), ((), ())), preferred_element_type=jnp.float32
-                )
-                if core == 0:
-                    add(sums, slot * 2, gb, unit == 0)
-                    add(keep, unit * 4, ga, half == 0 and slot == 0)
-                else:
-                    add(keep, slot * 4 + unit * 2, gb, half == 0)
-                    add(sums, 0, ga, unit == 0 and slot == 0)
+                rows = jnp.where(here, (ids & 511) + unit * 512, rows)
+            keys = jnp.concatenate(keys, axis=0)
+            hit = lax.broadcasted_iota(jnp.int32, (keys.shape[0], a.shape[0]), 0) == rows
+            logits = lax.dot_general(
+                keys * half_scale, a, (((1,), (1,)), ((), ())), preferred_element_type=jnp.float32
+            )
+            weights = jnp.tanh(logits + half_bias) + jnp.where(hit, -1.0, 1.0)
+            weights = weights.astype(jnp.bfloat16)
+            gb = jnp.dot(weights, a, preferred_element_type=jnp.float32)
+            ga = lax.dot_general(
+                weights, keys, (((0,), (0,)), ((), ())), preferred_element_type=jnp.float32
+            )
+            if core == 0:
+                add(sums, slot * 2, gb, True)
+                add(keep, 0, ga, half == 0 and slot == 0)
+            else:
+                add(keep, slot * 4, gb, half == 0)
+                add(sums, 0, ga, slot == 0)
         powers = []
         for i in range(6 if core == 0 else 4):
             powers.append(encode(send, i * ROWS, lambda first, last: sums[i, :, first:last]))

time: 73.4 us -> 73.8 us (level)
  transfers between devices with their start and end apart: 8 -> 8, of which waited for: 3 -> 3; matrix products, arithmetic and copies ran while one was open for 2% -> 2% of each run, Pallas kernels for 18% -> 17%
where the time goes in v9:
time: 73.8 us; the launch traced here: 73.6 us
  blocking collectives  46.8 us (63%)
  Pallas kernels  14.4 us (20%)
  waiting for transfers between devices  4.67 us (6%)
  starting transfers between devices  4.38 us (6%)
  other arithmetic  2.45 us (3%)
  between operations  0.74 us (1%)
    all_to_all x2, blocking collectives, meet(): lax.all_to_all(value, AXES, 0, 0, axis_index_groups=teams(), tiled=True)  46.8 us
    pallas_call x6, Pallas kernels, call(): pl.pallas_call(kernel, out_shape=shapes, in_specs=[VMEM] * len(operands),...  14.4 us
    ppermute x8, waiting for transfers between devices, swap_core(): return lax.ppermute(value, 'core', [(0, 1), (1, 0)])  4.67 us
    ppermute x8, starting transfers between devices, swap_core(): return lax.ppermute(value, 'core', [(0, 1), (1, 0)])  4.38 us
  transfers between devices with their start and end apart: 8, of which 3 were waited for; matrix products, arithmetic and copies ran while one was open for 2% of the time, Pallas kernels for 17%

profile of v9, /device:TPU:1, one launch (start us, length us, event | category | flops | bytes accessed | tf_op | source)
XLA Modules:
  0.0 73.6 jit_solution(17248845198329581807)
XLA Ops:
  0.6 1.5 %collective-permute-start.2 = (s32[1,256]{1,0:T(1,128)}, s32[1,256]{1,0:T(1,128)S(1)}, u32[]{:S(2)}, u32[]{:S(2)}) collective-permute-start(s32[1,256]{1,0:T(1,128)} %bitcast.1), channel_id=1, source_target_pairs={{0,32},{32,0},{1,33},{33,1},{2,34},{34,2},{3,35},{35,3},{4,36},{36... | collective-permute-start | bytes 3080 | tf_op jit(solution)/shard_map/ppermute | solution.py:40
  2.1 0.1 collective-permute-start
  2.2 0.4 collective-permute-start.1
  2.6 0.9 %broadcast_select_fusion.2.own = bf16[256,256]{1,0:T(8,128)(2,1)S(1)} fusion(bf16[256,256]{1,0:T(8,128)(2,1)} %param.4, bf16[256,256]{1,0:T(8,128)(2,1)} %param.5, pred[]{:T(512)S(6)} %eq.4), kind=kLoop, calls=%fused_computation.2 | loop fusion | flops 65536 | bytes 393217 | tf_op jit(solution)/shard_map/jit(_where)/select_n | solution.py:227
  3.6 0.7 fusion.1
  4.3 0.0 collective-permute-done.2.ids_got
  4.3 0.2 shard_map.59
  4.5 25.0 %all_to_all.10.mine = bf16[8,528,256]{2,1,0:T(8,128)(2,1)S(1)} all-to-all(bf16[8,528,256]{2,1,0:T(8,128)(2,1)S(1)} %shard_map.59), channel_id=1, replica_groups={{0,2,4,6,8,10,12,14},{64,66,68,70,72,74,76,78},{1,3,5,7,9,11,13,15},{65..., dimensions={0} | all-to-all | bytes 4325376 | tf_op jit(solution)/shard_map/all_to_all | solution.py:36
  29.5 0.1 fusion.2
  29.7 0.1 collective-permute-start.4
  29.7 0.5 collective-permute-start.3
  30.2 2.2 %collective-permute-done.4.theirs = bf16[4,528,256]{2,1,0:T(8,128)(2,1)S(1)} collective-permute-done((bf16[4,528,256]{2,1,0:T(8,128)(2,1)S(1)}, bf16[4,528,256]{2,1,0:T(8,128)(2,1)S(1)}, u32[]{:S(2)}, u32[]{:S(2)}) %collective-permute-start.4) | collective-permute-done | bytes 1081376 | tf_op jit(solution)/shard_map/ppermute | solution.py:40
  32.4 5.8 %shard_map.60 = (f32[12,256,256]{2,1,0:T(8,128)S(1)}, s16[1552,256]{1,0:T(8,128)(2,1)S(1)}) custom-call(s32[2,4]{1,0:T(2,128)S(1)} %copy-done, bf16[8,528,256]{2,1,0:T(8,128)(2,1)S(1)} %all_to_all.10.mine, bf16[4,528,256]{2,1,0:T(8,128)(2,1)S(1)} %collective-permute-done.4.theirs), custom_call_target="tpu_custom_call" | custom-call | flops 4831838208 | bytes 8388608 | tf_op jit(solution)/shard_map/pallas_call | solution.py:208
  38.3 0.9 %collective-permute-start.6 = (s16[1552,256]{1,0:T(8,128)(2,1)S(1)}, s16[1552,256]{1,0:T(8,128)(2,1)S(1)}, u32[]{:S(2)}, u32[]{:S(2)}) collective-permute-start(s16[1552,256]{1,0:T(8,128)(2,1)S(1)} %get-tuple-element.11), channel_id=1, source_target_pairs={{0,32},{32,0},{1,33},{33,1},{2,34},{34,2},{3,35},{35,3},{4,36},{36... | collective-permute-start | bytes 2383880 | tf_op jit(solution)/shard_map/ppermute | solution.py:40
  39.2 5.9 %shard_map.61 = (f32[12,256,256]{2,1,0:T(8,128)S(1)}, s16[1552,256]{1,0:T(8,128)(2,1)S(1)}) custom-call(s32[2,4]{1,0:T(2,128)S(1)} %copy-done, bf16[8,528,256]{2,1,0:T(8,128)(2,1)S(1)} %all_to_all.10.mine, bf16[4,528,256]{2,1,0:T(8,128)(2,1)S(1)} %collective-permute-done.3.theirs, ...), custom_call_target="tpu_custom_call", output_to_operand_aliasing={{0}: (3, {})} | custom-call | flops 4831838208 | bytes 8388608 | tf_op jit(solution)/shard_map/pallas_call | solution.py:208
  45.1 0.8 %collective-permute-start.5 = (s16[1552,256]{1,0:T(8,128)(2,1)S(1)}, s16[1552,256]{1,0:T(8,128)(2,1)S(1)}, u32[]{:S(2)}, u32[]{:S(2)}) collective-permute-start(s16[1552,256]{1,0:T(8,128)(2,1)S(1)} %get-tuple-element.10), channel_id=1, source_target_pairs={{0,32},{32,0},{1,33},{33,1},{2,34},{34,2},{3,35},{35,3},{4,36},{36... | collective-permute-start | bytes 2383880 | tf_op jit(solution)/shard_map/ppermute | solution.py:40
  45.9 1.0 %shard_map.62.refs_0_ = s16[8,528,256]{2,1,0:T(8,128)(2,1)S(1)} custom-call(s32[2,4]{1,0:T(2,128)S(1)} %copy-done, f32[12,256,256]{2,1,0:T(8,128)S(1)} %get-tuple-element.9.keep, s16[1552,256]{1,0:T(8,128)(2,1)S(1)} %collective-permute-done.6.got), custom_call_target="tpu_custom_call" | custom-call | flops 1048576 | bytes 8388608 | tf_op jit(solution)/shard_map/pallas_call | solution.py:208
  46.9 0.9 %collective-permute-done.5.got = s16[1552,256]{1,0:T(8,128)(2,1)S(1)} collective-permute-done((s16[1552,256]{1,0:T(8,128)(2,1)S(1)}, s16[1552,256]{1,0:T(8,128)(2,1)S(1)}, u32[]{:S(2)}, u32[]{:S(2)}) %collective-permute-start.5) | collective-permute-done | bytes 794656 | tf_op jit(solution)/shard_map/ppermute | solution.py:40
  47.8 0.9 %shard_map.63 = s16[8,528,256]{2,1,0:T(8,128)(2,1)S(1)} custom-call(s32[2,4]{1,0:T(2,128)S(1)} %copy-done, f32[12,256,256]{2,1,0:T(8,128)S(1)} %get-tuple-element.9.keep, s16[1552,256]{1,0:T(8,128)(2,1)S(1)} %collective-permute-done.5.got, s16[8,528,256]{2,1,0:T(8,128)(2,1)S(1)} %shard_map.62.refs_0_), custom_call_target="tpu_custom_call", output_to_operand_aliasing={{}: (3, {})} | custom-call | flops 1048576 | bytes 8388608 | tf_op jit(solution)/shard_map/pallas_call | solution.py:208
  48.8 21.8 %all_to_all.11.got = s16[8,528,256]{2,1,0:T(8,128)(2,1)S(1)} all-to-all(s16[8,528,256]{2,1,0:T(8,128)(2,1)S(1)} %shard_map.63), channel_id=1, replica_groups={{0,2,4,6,8,10,12,14},{64,66,68,70,72,74,76,78},{1,3,5,7,9,11,13,15},{65..., dimensions={0} | all-to-all | bytes 4325376 | tf_op jit(solution)/shard_map/all_to_all | solution.py:36
  70.6 0.6 shard_map.64
  71.2 0.1 collective-permute-start.7
  71.2 1.5 %collective-permute-done.7 = f32[256,256]{1,0:T(8,128)S(1)} collective-permute-done((f32[256,256]{1,0:T(8,128)S(1)}, f32[256,256]{1,0:T(8,128)S(1)}, u32[]{:S(2)}, u32[]{:S(2)}) %collective-permute-start.7) | collective-permute-done | bytes 262176 | tf_op jit(solution)/shard_map/ppermute | solution.py:40
  72.8 0.8 %broadcast_select_fusion = (f32[256,256]{1,0:T(8,128)}, f32[256,256]{1,0:T(8,128)}) fusion(f32[256,256]{1,0:T(8,128)S(1)} %collective-permute-done.7, f32[256,256]{1,0:T(8,128)S(1)} %get-tuple-element.12, pred[]{:T(512)S(6)} %eq.4), kind=kLoop, calls=%fused_computation | loop fusion | flops 131072 | bytes 1048577 | tf_op jit(solution)/shard_map/jit(_where)/select_n | solution.py:270
  (9 shorter events, 0.0 us)
Async XLA Ops:
  0.6 3.7 %collective-permute-start.2 = (s32[1,256]{1,0:T(1,128)}, s32[1,256]{1,0:T(1,128)S(1)}, u32[]{:S(2)}, u32[]{:S(2)}) collective-permute-start(s32[1,256]{1,0:T(1,128)} %bitcast.1), channel_id=1, source_target_pairs={{0,32},{32,0},{1,33},{33,1},{2,34},{34,2},{3,35},{35,3},{4,36},{36... | collective-permute-start | bytes 3080 | tf_op jit(solution)/shard_map/ppermute | solution.py:40
  2.1 2.2 %collective-permute-start = (bf16[256,256]{1,0:T(8,128)(2,1)}, bf16[256,256]{1,0:T(8,128)(2,1)S(1)}, u32[]{:S(2)}, u32[]{:S(2)}) collective-permute-start(bf16[256,256]{1,0:T(8,128)(2,1)} %param.4), channel_id=1, source_target_pairs={{0,32},{32,0},{1,33},{33,1},{2,34},{34,2},{3,35},{35,3},{4,36},{36... | collective-permute-start | bytes 393224 | tf_op jit(solution)/shard_map/ppermute | solution.py:40
  2.2 2.1 %collective-permute-start.1 = (bf16[256,256]{1,0:T(8,128)(2,1)}, bf16[256,256]{1,0:T(8,128)(2,1)S(1)}, u32[]{:S(2)}, u32[]{:S(2)}) collective-permute-start(bf16[256,256]{1,0:T(8,128)(2,1)} %param.5), channel_id=1, source_target_pairs={{0,32},{32,0},{1,33},{33,1},{2,34},{34,2},{3,35},{35,3},{4,36},{36... | collective-permute-start | bytes 393224 | tf_op jit(solution)/shard_map/ppermute | solution.py:40
  29.5 2.9 %copy-start = (s32[2,4]{1,0:T(2,128)S(1)}, s32[2,4]{1,0:T(2,128)}, u32[]{:S(2)}) copy-start(s32[2,4]{1,0:T(2,128)} %plan.7) | copy-start | bytes 100
  29.7 2.8 %collective-permute-start.4 = (bf16[4,528,256]{2,1,0:T(8,128)(2,1)S(1)}, bf16[4,528,256]{2,1,0:T(8,128)(2,1)S(1)}, u32[]{:S(2)}, u32[]{:S(2)}) collective-permute-start(bf16[4,528,256]{2,1,0:T(8,128)(2,1)S(1)} %get-tuple-element.14), channel_id=1, source_target_pairs={{0,32},{32,0},{1,33},{33,1},{2,34},{34,2},{3,35},{35,3},{4,36},{36... | collective-permute-start | bytes 3244040 | tf_op jit(solution)/shard_map/ppermute | solution.py:40
  29.7 9.4 %collective-permute-start.3 = (bf16[4,528,256]{2,1,0:T(8,128)(2,1)S(1)}, bf16[4,528,256]{2,1,0:T(8,128)(2,1)S(1)}, u32[]{:S(2)}, u32[]{:S(2)}) collective-permute-start(bf16[4,528,256]{2,1,0:T(8,128)(2,1)S(1)} %get-tuple-element.15), channel_id=1, source_target_pairs={{0,32},{32,0},{1,33},{33,1},{2,34},{34,2},{3,35},{35,3},{4,36},{36... | collective-permute-start | bytes 3244040 | tf_op jit(solution)/shard_map/ppermute | solution.py:40
  38.3 7.6 %collective-permute-start.6 = (s16[1552,256]{1,0:T(8,128)(2,1)S(1)}, s16[1552,256]{1,0:T(8,128)(2,1)S(1)}, u32[]{:S(2)}, u32[]{:S(2)}) collective-permute-start(s16[1552,256]{1,0:T(8,128)(2,1)S(1)} %get-tuple-element.11), channel_id=1, source_target_pairs={{0,32},{32,0},{1,33},{33,1},{2,34},{34,2},{3,35},{35,3},{4,36},{36... | collective-permute-start | bytes 2383880 | tf_op jit(solution)/shard_map/ppermute | solution.py:40
  45.1 2.7 %collective-permute-start.5 = (s16[1552,256]{1,0:T(8,128)(2,1)S(1)}, s16[1552,256]{1,0:T(8,128)(2,1)S(1)}, u32[]{:S(2)}, u32[]{:S(2)}) collective-permute-start(s16[1552,256]{1,0:T(8,128)(2,1)S(1)} %get-tuple-element.10), channel_id=1, source_target_pairs={{0,32},{32,0},{1,33},{33,1},{2,34},{34,2},{3,35},{35,3},{4,36},{36... | collective-permute-start | bytes 2383880 | tf_op jit(solution)/shard_map/ppermute | solution.py:40
  71.2 1.6 %collective-permute-start.7 = (f32[256,256]{1,0:T(8,128)S(1)}, f32[256,256]{1,0:T(8,128)S(1)}, u32[]{:S(2)}, u32[]{:S(2)}) collective-permute-start(f32[256,256]{1,0:T(8,128)S(1)} %get-tuple-element.13), channel_id=1, source_target_pairs={{0,32},{32,0},{1,33},{33,1},{2,34},{34,2},{3,35},{35,3},{4,36},{36... | collective-permute-start | bytes 786440 | tf_op jit(solution)/shard_map/ppermute | solution.py:40

commit v10 on v8

--- a/solution.py
+++ b/solution.py
@@ -50,6 +50,16 @@
         out[start : start + ROWS, first : first + 128] = scaled.astype(jnp.int16)
         powers.append(power)
     return jnp.concatenate(powers, axis=1)
+
+
+def encode_all(out, blocks):
+    tops = [jnp.max(jnp.abs(blocks[i]), axis=0, keepdims=True) for i in range(blocks.shape[0])]
+    top = jnp.maximum(jnp.concatenate(tops, axis=0), 2.0**-100)
+    power = jnp.ceil(jnp.log2(top) * 128.0) + 1.0
+    scale = PEAK * jnp.exp2(power * (-1.0 / 128.0))
+    for i in range(blocks.shape[0]):
+        out[i * ROWS : (i + 1) * ROWS, :] = (blocks[i] * scale[i : i + 1]).astype(jnp.int16)
+    return [power[i : i + 1] for i in range(blocks.shape[0])]
 
 
 def decode(code, power):
@@ -148,9 +158,12 @@
                 else:
                     add(keep, slot * 4 + unit * 2, gb, half == 0)
                     add(sums, 0, ga, unit == 0 and slot == 0)
-        powers = []
-        for i in range(6 if core == 0 else 4):
-            powers.append(encode(send, i * ROWS, lambda first, last: sums[i, :, first:last]))
+        if core == 0:
+            powers = encode_all(send, sums)
+        else:
+            powers = [
+                encode(send, i * ROWS, lambda first, last: sums[i, :, first:last]) for i in range(4)
+            ]
         send[6 * ROWS :, :] = notes(powers)
 
     on_core(body)
@@ -192,14 +205,14 @@
     on_core(body)
 
 
-def sum_kernel(factor, got, keep, send):
+def sum_kernel(factor, kept, got, out):
     def body(core):
-        for c in range(2):
-            total = jnp.zeros((ROWS, ROWS), jnp.float32)
-            for s in range(8):
-                power = got[s, 2 * ROWS :, :].astype(jnp.float32)[c : c + 1]
-                total += decode(got[s, c * ROWS : (c + 1) * ROWS, :], power)
-            (keep if c == core else send)[...] = total * factor
+        c = core if kept else 1 - core
+        total = jnp.zeros((ROWS, ROWS), jnp.float32)
+        for s in range(8):
+            power = got[s, 2 * ROWS :, :].astype(jnp.float32)[c : c + 1]
+            total += decode(got[s, c * ROWS : (c + 1) * ROWS, :], power)
+        out[...] = total * factor
 
     on_core(body)
 
@@ -266,7 +279,11 @@
     got_far = swap_core(send_far)
     packed = pack(1, keep, got_far, pack(0, keep, got_near))
     one = jax.ShapeDtypeStruct((ROWS, ROWS), f32)
-    keep, send = call(functools.partial(sum_kernel, 0.5 * factor), (one, one), [], 1 << 20, meet(packed))
+    pieces = meet(packed)
+    send, keep = [
+        call(functools.partial(sum_kernel, 0.5 * factor, kept), one, [], 1 << 28, pieces)
+        for kept in (False, True)
+    ]
     got = swap_core(send)
     return jnp.where(core == 0, keep, got), jnp.where(core == 0, got, keep)
 

time: 73.4 us -> 73.1 us (level)
    pallas_call x6 -> x7, Pallas kernels: 14.6 us -> 14.7 us  [call(): pl.pallas_call(kernel, out_shape=shapes, in_specs=[VMEM] * len(operands),...]
where the time goes in v10:
time: 73.1 us; the launch traced here: 72.9 us
  blocking collectives  46.8 us (64%)
  Pallas kernels  14.7 us (20%)
  waiting for transfers between devices  4.36 us (6%)
  starting transfers between devices  3.72 us (5%)
  other arithmetic  2.45 us (3%)
  between operations  0.74 us (1%)
    all_to_all x2, blocking collectives, meet(): lax.all_to_all(value, AXES, 0, 0, axis_index_groups=teams(), tiled=True)  46.8 us
    pallas_call x7, Pallas kernels, call(): pl.pallas_call(kernel, out_shape=shapes, in_specs=[VMEM] * len(operands),...  14.7 us
    ppermute x8, waiting for transfers between devices, swap_core(): return lax.ppermute(value, 'core', [(0, 1), (1, 0)])  4.36 us
    ppermute x8, starting transfers between devices, swap_core(): return lax.ppermute(value, 'core', [(0, 1), (1, 0)])  3.72 us
  transfers between devices with their start and end apart: 8, of which 3 were waited for; matrix products, arithmetic and copies ran while one was open for 2% of the time, Pallas kernels for 18%

profile of v10, /device:TPU:1, one launch (start us, length us, event | category | flops | bytes accessed | tf_op | source)
XLA Modules:
  0.0 72.9 jit_solution(12166923907570333305)
XLA Ops:
  0.6 1.5 %collective-permute-start.2 = (s32[1,256]{1,0:T(1,128)}, s32[1,256]{1,0:T(1,128)S(1)}, u32[]{:S(2)}, u32[]{:S(2)}) collective-permute-start(s32[1,256]{1,0:T(1,128)} %bitcast.1), channel_id=1, source_target_pairs={{0,32},{32,0},{1,33},{33,1},{2,34},{34,2},{3,35},{35,3},{4,36},{36... | collective-permute-start | bytes 3080 | tf_op jit(solution)/shard_map/ppermute | solution.py:40
  2.1 0.1 collective-permute-start
  2.2 0.4 collective-permute-start.1
  2.6 0.9 %broadcast_select_fusion.2.own = bf16[256,256]{1,0:T(8,128)(2,1)S(1)} fusion(bf16[256,256]{1,0:T(8,128)(2,1)} %param.4, bf16[256,256]{1,0:T(8,128)(2,1)} %param.5, pred[]{:T(512)S(6)} %eq.4), kind=kLoop, calls=%fused_computation.2 | loop fusion | flops 65536 | bytes 393217 | tf_op jit(solution)/shard_map/jit(_where)/select_n | solution.py:241
  3.6 0.7 fusion.1
  4.3 0.2 shard_map.59
  4.5 25.0 %all_to_all.10.mine = bf16[8,528,256]{2,1,0:T(8,128)(2,1)S(1)} all-to-all(bf16[8,528,256]{2,1,0:T(8,128)(2,1)S(1)} %shard_map.59), channel_id=1, replica_groups={{0,2,4,6,8,10,12,14},{64,66,68,70,72,74,76,78},{1,3,5,7,9,11,13,15},{65..., dimensions={0} | all-to-all | bytes 4325376 | tf_op jit(solution)/shard_map/all_to_all | solution.py:36
  29.5 0.1 fusion.2
  29.7 0.1 collective-permute-start.4
  29.7 0.5 collective-permute-start.3
  30.2 2.2 %collective-permute-done.4.theirs = bf16[4,528,256]{2,1,0:T(8,128)(2,1)S(1)} collective-permute-done((bf16[4,528,256]{2,1,0:T(8,128)(2,1)S(1)}, bf16[4,528,256]{2,1,0:T(8,128)(2,1)S(1)}, u32[]{:S(2)}, u32[]{:S(2)}) %collective-permute-start.4) | collective-permute-done | bytes 1081376 | tf_op jit(solution)/shard_map/ppermute | solution.py:40
  32.4 6.0 %shard_map.60 = (f32[12,256,256]{2,1,0:T(8,128)S(1)}, s16[1552,256]{1,0:T(8,128)(2,1)S(1)}) custom-call(s32[2,4]{1,0:T(2,128)S(1)} %copy-done, bf16[8,528,256]{2,1,0:T(8,128)(2,1)S(1)} %all_to_all.10.mine, bf16[4,528,256]{2,1,0:T(8,128)(2,1)S(1)} %collective-permute-done.4.theirs), custom_call_target="tpu_custom_call" | custom-call | flops 4831838208 | bytes 8388608 | tf_op jit(solution)/shard_map/pallas_call | solution.py:222
  38.4 0.6 collective-permute-start.6
  39.0 6.0 %shard_map.61 = (f32[12,256,256]{2,1,0:T(8,128)S(1)}, s16[1552,256]{1,0:T(8,128)(2,1)S(1)}) custom-call(s32[2,4]{1,0:T(2,128)S(1)} %copy-done, bf16[8,528,256]{2,1,0:T(8,128)(2,1)S(1)} %all_to_all.10.mine, bf16[4,528,256]{2,1,0:T(8,128)(2,1)S(1)} %collective-permute-done.3.theirs, ...), custom_call_target="tpu_custom_call", output_to_operand_aliasing={{0}: (3, {})} | custom-call | flops 4831838208 | bytes 8388608 | tf_op jit(solution)/shard_map/pallas_call | solution.py:222
  45.1 0.5 collective-permute-start.5
  45.5 1.0 %shard_map.62.refs_0_ = s16[8,528,256]{2,1,0:T(8,128)(2,1)S(1)} custom-call(s32[2,4]{1,0:T(2,128)S(1)} %copy-done, f32[12,256,256]{2,1,0:T(8,128)S(1)} %get-tuple-element.7.keep, s16[1552,256]{1,0:T(8,128)(2,1)S(1)} %collective-permute-done.6.got), custom_call_target="tpu_custom_call" | custom-call | flops 1048576 | bytes 8388608 | tf_op jit(solution)/shard_map/pallas_call | solution.py:222
  46.5 0.9 %collective-permute-done.5.got = s16[1552,256]{1,0:T(8,128)(2,1)S(1)} collective-permute-done((s16[1552,256]{1,0:T(8,128)(2,1)S(1)}, s16[1552,256]{1,0:T(8,128)(2,1)S(1)}, u32[]{:S(2)}, u32[]{:S(2)}) %collective-permute-start.5) | collective-permute-done | bytes 794656 | tf_op jit(solution)/shard_map/ppermute | solution.py:40
  47.4 0.9 %shard_map.63 = s16[8,528,256]{2,1,0:T(8,128)(2,1)S(1)} custom-call(s32[2,4]{1,0:T(2,128)S(1)} %copy-done, f32[12,256,256]{2,1,0:T(8,128)S(1)} %get-tuple-element.7.keep, s16[1552,256]{1,0:T(8,128)(2,1)S(1)} %collective-permute-done.5.got, s16[8,528,256]{2,1,0:T(8,128)(2,1)S(1)} %shard_map.62.refs_0_), custom_call_target="tpu_custom_call", output_to_operand_aliasing={{}: (3, {})} | custom-call | flops 1048576 | bytes 8388608 | tf_op jit(solution)/shard_map/pallas_call | solution.py:222
  48.4 21.8 %all_to_all.11.got = s16[8,528,256]{2,1,0:T(8,128)(2,1)S(1)} all-to-all(s16[8,528,256]{2,1,0:T(8,128)(2,1)S(1)} %shard_map.63), channel_id=1, replica_groups={{0,2,4,6,8,10,12,14},{64,66,68,70,72,74,76,78},{1,3,5,7,9,11,13,15},{65..., dimensions={0} | all-to-all | bytes 4325376 | tf_op jit(solution)/shard_map/all_to_all | solution.py:36
  70.2 0.3 shard_map.65
  70.5 0.1 collective-permute-start.7
  70.5 0.3 shard_map.64
  70.9 1.2 %collective-permute-done.7 = f32[256,256]{1,0:T(8,128)S(1)} collective-permute-done((f32[256,256]{1,0:T(8,128)S(1)}, f32[256,256]{1,0:T(8,128)S(1)}, u32[]{:S(2)}, u32[]{:S(2)}) %collective-permute-start.7) | collective-permute-done | bytes 262176 | tf_op jit(solution)/shard_map/ppermute | solution.py:40
  72.1 0.8 %broadcast_select_fusion = (f32[256,256]{1,0:T(8,128)}, f32[256,256]{1,0:T(8,128)}) fusion(f32[256,256]{1,0:T(8,128)S(1)} %collective-permute-done.7, f32[256,256]{1,0:T(8,128)S(1)} %shard_map.64, pred[]{:T(512)S(6)} %eq.4), kind=kLoop, calls=%fused_computation | loop fusion | flops 131072 | bytes 1048577 | tf_op jit(solution)/shard_map/jit(_where)/select_n | solution.py:288
  (10 shorter events, 0.0 us)
Async XLA Ops:
  0.6 3.7 %collective-permute-start.2 = (s32[1,256]{1,0:T(1,128)}, s32[1,256]{1,0:T(1,128)S(1)}, u32[]{:S(2)}, u32[]{:S(2)}) collective-permute-start(s32[1,256]{1,0:T(1,128)} %bitcast.1), channel_id=1, source_target_pairs={{0,32},{32,0},{1,33},{33,1},{2,34},{34,2},{3,35},{35,3},{4,36},{36... | collective-permute-start | bytes 3080 | tf_op jit(solution)/shard_map/ppermute | solution.py:40
  2.1 2.2 %collective-permute-start = (bf16[256,256]{1,0:T(8,128)(2,1)}, bf16[256,256]{1,0:T(8,128)(2,1)S(1)}, u32[]{:S(2)}, u32[]{:S(2)}) collective-permute-start(bf16[256,256]{1,0:T(8,128)(2,1)} %param.4), channel_id=1, source_target_pairs={{0,32},{32,0},{1,33},{33,1},{2,34},{34,2},{3,35},{35,3},{4,36},{36... | collective-permute-start | bytes 393224 | tf_op jit(solution)/shard_map/ppermute | solution.py:40
  2.2 2.1 %collective-permute-start.1 = (bf16[256,256]{1,0:T(8,128)(2,1)}, bf16[256,256]{1,0:T(8,128)(2,1)S(1)}, u32[]{:S(2)}, u32[]{:S(2)}) collective-permute-start(bf16[256,256]{1,0:T(8,128)(2,1)} %param.5), channel_id=1, source_target_pairs={{0,32},{32,0},{1,33},{33,1},{2,34},{34,2},{3,35},{35,3},{4,36},{36... | collective-permute-start | bytes 393224 | tf_op jit(solution)/shard_map/ppermute | solution.py:40
  29.5 2.9 %copy-start = (s32[2,4]{1,0:T(2,128)S(1)}, s32[2,4]{1,0:T(2,128)}, u32[]{:S(2)}) copy-start(s32[2,4]{1,0:T(2,128)} %plan.7) | copy-start | bytes 100
  29.7 2.8 %collective-permute-start.4 = (bf16[4,528,256]{2,1,0:T(8,128)(2,1)S(1)}, bf16[4,528,256]{2,1,0:T(8,128)(2,1)S(1)}, u32[]{:S(2)}, u32[]{:S(2)}) collective-permute-start(bf16[4,528,256]{2,1,0:T(8,128)(2,1)S(1)} %get-tuple-element.10), channel_id=1, source_target_pairs={{0,32},{32,0},{1,33},{33,1},{2,34},{34,2},{3,35},{35,3},{4,36},{36... | collective-permute-start | bytes 3244040 | tf_op jit(solution)/shard_map/ppermute | solution.py:40
  29.7 9.3 %collective-permute-start.3 = (bf16[4,528,256]{2,1,0:T(8,128)(2,1)S(1)}, bf16[4,528,256]{2,1,0:T(8,128)(2,1)S(1)}, u32[]{:S(2)}, u32[]{:S(2)}) collective-permute-start(bf16[4,528,256]{2,1,0:T(8,128)(2,1)S(1)} %get-tuple-element.11), channel_id=1, source_target_pairs={{0,32},{32,0},{1,33},{33,1},{2,34},{34,2},{3,35},{35,3},{4,36},{36... | collective-permute-start | bytes 3244040 | tf_op jit(solution)/shard_map/ppermute | solution.py:40
  38.4 7.1 %collective-permute-start.6 = (s16[1552,256]{1,0:T(8,128)(2,1)S(1)}, s16[1552,256]{1,0:T(8,128)(2,1)S(1)}, u32[]{:S(2)}, u32[]{:S(2)}) collective-permute-start(s16[1552,256]{1,0:T(8,128)(2,1)S(1)} %get-tuple-element.9), channel_id=1, source_target_pairs={{0,32},{32,0},{1,33},{33,1},{2,34},{34,2},{3,35},{35,3},{4,36},{36... | collective-permute-start | bytes 2383880 | tf_op jit(solution)/shard_map/ppermute | solution.py:40
  45.1 2.4 %collective-permute-start.5 = (s16[1552,256]{1,0:T(8,128)(2,1)S(1)}, s16[1552,256]{1,0:T(8,128)(2,1)S(1)}, u32[]{:S(2)}, u32[]{:S(2)}) collective-permute-start(s16[1552,256]{1,0:T(8,128)(2,1)S(1)} %get-tuple-element.8), channel_id=1, source_target_pairs={{0,32},{32,0},{1,33},{33,1},{2,34},{34,2},{3,35},{35,3},{4,36},{36... | collective-permute-start | bytes 2383880 | tf_op jit(solution)/shard_map/ppermute | solution.py:40
  70.5 1.6 %collective-permute-start.7 = (f32[256,256]{1,0:T(8,128)S(1)}, f32[256,256]{1,0:T(8,128)S(1)}, u32[]{:S(2)}, u32[]{:S(2)}) collective-permute-start(f32[256,256]{1,0:T(8,128)S(1)} %shard_map.65), channel_id=1, source_target_pairs={{0,32},{32,0},{1,33},{33,1},{2,34},{34,2},{3,35},{35,3},{4,36},{36... | collective-permute-start | bytes 786440 | tf_op jit(solution)/shard_map/ppermute | solution.py:40

commit v11 on v10

--- a/solution.py
+++ b/solution.py
@@ -106,6 +106,26 @@
     on_core(body)
 
 
+def pick_kernel(half, plan, mine, out):
+    def body(core):
+        if core == 0:
+            for s in range(4):
+                source = mine.at[half * 4 + s]
+                out[s * ROWS : (s + 1) * ROWS, :] = source[ROWS : 2 * ROWS, :]
+                start = 4 * ROWS + s * NOTE
+                out[start : start + NOTE, :] = source[2 * ROWS :, :]
+        else:
+            owners = window(plan, 0)
+            for slot in range(3):
+                rows = pl.ds(pl.multiple_of(owners[slot] % 2 * ROWS, ROWS), ROWS)
+                for xh in range(2):
+                    start = (slot * 2 + xh) * ROWS
+                    value = mine[half * 4 + 2 * xh + owners[slot] // 2, rows, :]
+                    out[start : start + ROWS, :] = value
+
+    on_core(body)
+
+
 def score_kernel(factor, half, plan, mine, theirs, *refs):
     keep, send, sums = refs[-3:]
     half_scale = jnp.bfloat16(0.5 * factor)
@@ -124,22 +144,29 @@
     def body(core):
         owners = window(plan, core)
         for unit in range(2):
-            a_from, a_source = (mine, 4 * unit) if core == 0 else (theirs, 0)
-            a = [a_from[a_source + s, core * ROWS : (core + 1) * ROWS, :] for s in range(4)]
+            if core == 0:
+                a = [mine[4 * unit + s, 0:ROWS, :] for s in range(4)]
+                tags = [mine[4 * unit + s, 2 * ROWS :, :] for s in range(4)]
+            else:
+                a = [theirs[s * ROWS : (s + 1) * ROWS, :] for s in range(4)]
+                starts = [4 * ROWS + s * NOTE for s in range(4)]
+                tags = [theirs[start : start + NOTE, :] for start in starts]
             a = jnp.concatenate(a, axis=0)
             ids = []
-            for s in range(4):
-                note = a_from[a_source + s, 2 * ROWS :, :].astype(jnp.float32)[2 * core : 2 * core + 2]
+            for tag in tags:
+                note = tag.astype(jnp.float32)[2 * core : 2 * core + 2]
                 ids.append((note[0:1] * 256.0 + note[1:2]).astype(jnp.int32))
             ids = jnp.concatenate(ids, axis=1)
             far = half if core == 0 else unit
             level = jnp.where(outer, 3 * far, 1 + far)
             for slot in range(3):
                 group = owners[slot]
-                b_from, b_source = (theirs, 0) if core == 0 else (mine, 4 * unit)
-                b_rows = pl.ds(pl.multiple_of(group % 2 * ROWS, ROWS), ROWS)
-                keys = [b_from[b_source + 2 * xh + group // 2, b_rows, :] for xh in range(2)]
-                keys = jnp.concatenate(keys, axis=0)
+                if core == 0:
+                    keys = theirs[slot * 2 * ROWS : (slot + 1) * 2 * ROWS, :]
+                else:
+                    b_rows = pl.ds(pl.multiple_of(group % 2 * ROWS, ROWS), ROWS)
+                    keys = [mine[4 * unit + 2 * xh + group // 2, b_rows, :] for xh in range(2)]
+                    keys = jnp.concatenate(keys, axis=0)
                 here = lax.shift_right_logical(ids, 9) == group * 16 + level * 4 + y
                 rows = jnp.where(here, ids & 511, -1)
                 hit = lax.broadcasted_iota(jnp.int32, (deep, wide), 0) == rows
@@ -242,7 +269,11 @@
     own_ids = jnp.stack([positives // 256, positives % 256]).astype(bf16)
     built = jax.ShapeDtypeStruct((8, height, ROWS), bf16)
     mine = meet(call(build_kernel, built, [], 1 << 10, own, own_ids, *got))
-    near, far = swap_core(mine[:4]), swap_core(mine[4:])
+    picked = jax.ShapeDtypeStruct((6 * ROWS, ROWS), bf16)
+    near, far = [
+        swap_core(call(functools.partial(pick_kernel, half), picked, [], 1 << 10, mine, plan=plan))
+        for half in range(2)
+    ]
 
     def score(half, theirs, *keep):
         return call(

time: 73.1 us -> 72.6 us (level)
    pallas_call x7 -> x9, Pallas kernels: 14.7 us -> 14.9 us  [call(): pl.pallas_call(kernel, out_shape=shapes, in_specs=[VMEM] * len(operands),...]
  transfers between devices with their start and end apart: 8 -> 8, of which waited for: 3 -> 3; matrix products, arithmetic and copies ran while one was open for 2% -> 2% of each run, Pallas kernels for 18% -> 19%
where the time goes in v11:
time: 72.6 us; the launch traced here: 72.3 us
  blocking collectives  46.8 us (64%)
  Pallas kernels  14.9 us (21%)
  waiting for transfers between devices  3.86 us (5%)
  starting transfers between devices  3.58 us (5%)
  other arithmetic  2.45 us (3%)
  between operations  0.76 us (1%)
    all_to_all x2, blocking collectives, meet(): lax.all_to_all(value, AXES, 0, 0, axis_index_groups=teams(), tiled=True)  46.8 us
    pallas_call x9, Pallas kernels, call(): pl.pallas_call(kernel, out_shape=shapes, in_specs=[VMEM] * len(operands),...  14.9 us
    ppermute x8, waiting for transfers between devices, swap_core(): return lax.ppermute(value, 'core', [(0, 1), (1, 0)])  3.86 us
    ppermute x8, starting transfers between devices, swap_core(): return lax.ppermute(value, 'core', [(0, 1), (1, 0)])  3.58 us
  transfers between devices with their start and end apart: 8, of which 3 were waited for; matrix products, arithmetic and copies ran while one was open for 2% of the time, Pallas kernels for 19%

profile of v11, /device:TPU:1, one launch (start us, length us, event | category | flops | bytes accessed | tf_op | source)
XLA Modules:
  0.0 72.3 jit_solution(14882533418713520526)
XLA Ops:
  0.6 1.5 %collective-permute-start.2 = (s32[1,256]{1,0:T(1,128)}, s32[1,256]{1,0:T(1,128)S(1)}, u32[]{:S(2)}, u32[]{:S(2)}) collective-permute-start(s32[1,256]{1,0:T(1,128)} %bitcast.1), channel_id=1, source_target_pairs={{0,32},{32,0},{1,33},{33,1},{2,34},{34,2},{3,35},{35,3},{4,36},{36... | collective-permute-start | bytes 3080 | tf_op jit(solution)/shard_map/ppermute | solution.py:40
  2.1 0.1 collective-permute-start
  2.2 0.4 collective-permute-start.1
  2.6 0.9 %broadcast_select_fusion.2.own = bf16[256,256]{1,0:T(8,128)(2,1)S(1)} fusion(bf16[256,256]{1,0:T(8,128)(2,1)} %param.4, bf16[256,256]{1,0:T(8,128)(2,1)} %param.5, pred[]{:T(512)S(6)} %eq.4), kind=kLoop, calls=%fused_computation.2 | loop fusion | flops 65536 | bytes 393217 | tf_op jit(solution)/shard_map/jit(_where)/select_n | solution.py:268
  3.6 0.7 fusion.1
  4.3 0.2 shard_map.59
  4.5 25.0 %all_to_all.10.mine = bf16[8,528,256]{2,1,0:T(8,128)(2,1)S(1)} all-to-all(bf16[8,528,256]{2,1,0:T(8,128)(2,1)S(1)} %shard_map.59), channel_id=1, replica_groups={{0,2,4,6,8,10,12,14},{64,66,68,70,72,74,76,78},{1,3,5,7,9,11,13,15},{65..., dimensions={0} | all-to-all | bytes 4325376 | tf_op jit(solution)/shard_map/all_to_all | solution.py:36
  29.6 0.1 collective-permute-start.4
  29.7 0.1 shard_map.60
  29.8 0.5 collective-permute-start.3
  30.3 1.6 %collective-permute-done.4.theirs = bf16[1536,256]{1,0:T(8,128)(2,1)S(1)} collective-permute-done((bf16[1536,256]{1,0:T(8,128)(2,1)S(1)}, bf16[1536,256]{1,0:T(8,128)(2,1)S(1)}, u32[]{:S(2)}, u32[]{:S(2)}) %collective-permute-start.4) | collective-permute-done | bytes 786464 | tf_op jit(solution)/shard_map/ppermute | solution.py:40
  32.0 6.0 %shard_map.62 = (f32[12,256,256]{2,1,0:T(8,128)S(1)}, s16[1552,256]{1,0:T(8,128)(2,1)S(1)}) custom-call(s32[2,4]{1,0:T(2,128)S(1)} %copy-done, bf16[8,528,256]{2,1,0:T(8,128)(2,1)S(1)} %all_to_all.10.mine, bf16[1536,256]{1,0:T(8,128)(2,1)S(1)} %collective-permute-done.4.theirs), custom_call_target="tpu_custom_call" | custom-call | flops 4831838208 | bytes 8388608 | tf_op jit(solution)/shard_map/pallas_call | solution.py:249
  37.9 0.5 collective-permute-start.6
  38.4 6.1 %shard_map.63 = (f32[12,256,256]{2,1,0:T(8,128)S(1)}, s16[1552,256]{1,0:T(8,128)(2,1)S(1)}) custom-call(s32[2,4]{1,0:T(2,128)S(1)} %copy-done, bf16[8,528,256]{2,1,0:T(8,128)(2,1)S(1)} %all_to_all.10.mine, bf16[1536,256]{1,0:T(8,128)(2,1)S(1)} %collective-permute-done.3.theirs, ...), custom_call_target="tpu_custom_call", output_to_operand_aliasing={{0}: (3, {})} | custom-call | flops 4831838208 | bytes 8388608 | tf_op jit(solution)/shard_map/pallas_call | solution.py:249
  44.5 0.4 collective-permute-start.5
  44.9 1.0 %shard_map.64.refs_0_ = s16[8,528,256]{2,1,0:T(8,128)(2,1)S(1)} custom-call(s32[2,4]{1,0:T(2,128)S(1)} %copy-done, f32[12,256,256]{2,1,0:T(8,128)S(1)} %get-tuple-element.7.keep, s16[1552,256]{1,0:T(8,128)(2,1)S(1)} %collective-permute-done.6.got), custom_call_target="tpu_custom_call" | custom-call | flops 1048576 | bytes 8388608 | tf_op jit(solution)/shard_map/pallas_call | solution.py:249
  45.9 1.0 %collective-permute-done.5.got = s16[1552,256]{1,0:T(8,128)(2,1)S(1)} collective-permute-done((s16[1552,256]{1,0:T(8,128)(2,1)S(1)}, s16[1552,256]{1,0:T(8,128)(2,1)S(1)}, u32[]{:S(2)}, u32[]{:S(2)}) %collective-permute-start.5) | collective-permute-done | bytes 794656 | tf_op jit(solution)/shard_map/ppermute | solution.py:40
  46.9 0.9 %shard_map.65 = s16[8,528,256]{2,1,0:T(8,128)(2,1)S(1)} custom-call(s32[2,4]{1,0:T(2,128)S(1)} %copy-done, f32[12,256,256]{2,1,0:T(8,128)S(1)} %get-tuple-element.7.keep, s16[1552,256]{1,0:T(8,128)(2,1)S(1)} %collective-permute-done.5.got, s16[8,528,256]{2,1,0:T(8,128)(2,1)S(1)} %shard_map.64.refs_0_), custom_call_target="tpu_custom_call", output_to_operand_aliasing={{}: (3, {})} | custom-call | flops 1048576 | bytes 8388608 | tf_op jit(solution)/shard_map/pallas_call | solution.py:249
  47.8 21.8 %all_to_all.11.got = s16[8,528,256]{2,1,0:T(8,128)(2,1)S(1)} all-to-all(s16[8,528,256]{2,1,0:T(8,128)(2,1)S(1)} %shard_map.65), channel_id=1, replica_groups={{0,2,4,6,8,10,12,14},{64,66,68,70,72,74,76,78},{1,3,5,7,9,11,13,15},{65..., dimensions={0} | all-to-all | bytes 4325376 | tf_op jit(solution)/shard_map/all_to_all | solution.py:36
  69.6 0.3 shard_map.67
  69.9 0.1 collective-permute-start.7
  70.0 0.3 shard_map.66
  70.3 1.2 %collective-permute-done.7 = f32[256,256]{1,0:T(8,128)S(1)} collective-permute-done((f32[256,256]{1,0:T(8,128)S(1)}, f32[256,256]{1,0:T(8,128)S(1)}, u32[]{:S(2)}, u32[]{:S(2)}) %collective-permute-start.7) | collective-permute-done | bytes 262176 | tf_op jit(solution)/shard_map/ppermute | solution.py:40
  71.5 0.8 %broadcast_select_fusion = (f32[256,256]{1,0:T(8,128)}, f32[256,256]{1,0:T(8,128)}) fusion(f32[256,256]{1,0:T(8,128)S(1)} %collective-permute-done.7, f32[256,256]{1,0:T(8,128)S(1)} %shard_map.66, pred[]{:T(512)S(6)} %eq.4), kind=kLoop, calls=%fused_computation | loop fusion | flops 131072 | bytes 1048577 | tf_op jit(solution)/shard_map/jit(_where)/select_n | solution.py:319
  (11 shorter events, 0.1 us)
Async XLA Ops:
  0.6 3.7 %collective-permute-start.2 = (s32[1,256]{1,0:T(1,128)}, s32[1,256]{1,0:T(1,128)S(1)}, u32[]{:S(2)}, u32[]{:S(2)}) collective-permute-start(s32[1,256]{1,0:T(1,128)} %bitcast.1), channel_id=1, source_target_pairs={{0,32},{32,0},{1,33},{33,1},{2,34},{34,2},{3,35},{35,3},{4,36},{36... | collective-permute-start | bytes 3080 | tf_op jit(solution)/shard_map/ppermute | solution.py:40
  2.1 2.2 %collective-permute-start = (bf16[256,256]{1,0:T(8,128)(2,1)}, bf16[256,256]{1,0:T(8,128)(2,1)S(1)}, u32[]{:S(2)}, u32[]{:S(2)}) collective-permute-start(bf16[256,256]{1,0:T(8,128)(2,1)} %param.4), channel_id=1, source_target_pairs={{0,32},{32,0},{1,33},{33,1},{2,34},{34,2},{3,35},{35,3},{4,36},{36... | collective-permute-start | bytes 393224 | tf_op jit(solution)/shard_map/ppermute | solution.py:40
  2.2 2.1 %collective-permute-start.1 = (bf16[256,256]{1,0:T(8,128)(2,1)}, bf16[256,256]{1,0:T(8,128)(2,1)S(1)}, u32[]{:S(2)}, u32[]{:S(2)}) collective-permute-start(bf16[256,256]{1,0:T(8,128)(2,1)} %param.5), channel_id=1, source_target_pairs={{0,32},{32,0},{1,33},{33,1},{2,34},{34,2},{3,35},{35,3},{4,36},{36... | collective-permute-start | bytes 393224 | tf_op jit(solution)/shard_map/ppermute | solution.py:40
  4.5 25.0 %copy-start = (s32[2,4]{1,0:T(2,128)S(1)}, s32[2,4]{1,0:T(2,128)}, u32[]{:S(2)}) copy-start(s32[2,4]{1,0:T(2,128)} %plan.11) | copy-start | bytes 100
  29.6 2.4 %collective-permute-start.4 = (bf16[1536,256]{1,0:T(8,128)(2,1)S(1)}, bf16[1536,256]{1,0:T(8,128)(2,1)S(1)}, u32[]{:S(2)}, u32[]{:S(2)}) collective-permute-start(bf16[1536,256]{1,0:T(8,128)(2,1)S(1)} %shard_map.61), channel_id=1, source_target_pairs={{0,32},{32,0},{1,33},{33,1},{2,34},{34,2},{3,35},{35,3},{4,36},{36... | collective-permute-start | bytes 2359304 | tf_op jit(solution)/shard_map/ppermute | solution.py:40
  29.8 8.6 %collective-permute-start.3 = (bf16[1536,256]{1,0:T(8,128)(2,1)S(1)}, bf16[1536,256]{1,0:T(8,128)(2,1)S(1)}, u32[]{:S(2)}, u32[]{:S(2)}) collective-permute-start(bf16[1536,256]{1,0:T(8,128)(2,1)S(1)} %shard_map.60), channel_id=1, source_target_pairs={{0,32},{32,0},{1,33},{33,1},{2,34},{34,2},{3,35},{35,3},{4,36},{36... | collective-permute-start | bytes 2359304 | tf_op jit(solution)/shard_map/ppermute | solution.py:40
  37.9 7.0 %collective-permute-start.6 = (s16[1552,256]{1,0:T(8,128)(2,1)S(1)}, s16[1552,256]{1,0:T(8,128)(2,1)S(1)}, u32[]{:S(2)}, u32[]{:S(2)}) collective-permute-start(s16[1552,256]{1,0:T(8,128)(2,1)S(1)} %get-tuple-element.9), channel_id=1, source_target_pairs={{0,32},{32,0},{1,33},{33,1},{2,34},{34,2},{3,35},{35,3},{4,36},{36... | collective-permute-start | bytes 2383880 | tf_op jit(solution)/shard_map/ppermute | solution.py:40
  44.5 2.4 %collective-permute-start.5 = (s16[1552,256]{1,0:T(8,128)(2,1)S(1)}, s16[1552,256]{1,0:T(8,128)(2,1)S(1)}, u32[]{:S(2)}, u32[]{:S(2)}) collective-permute-start(s16[1552,256]{1,0:T(8,128)(2,1)S(1)} %get-tuple-element.8), channel_id=1, source_target_pairs={{0,32},{32,0},{1,33},{33,1},{2,34},{34,2},{3,35},{35,3},{4,36},{36... | collective-permute-start | bytes 2383880 | tf_op jit(solution)/shard_map/ppermute | solution.py:40
  69.9 1.6 %collective-permute-start.7 = (f32[256,256]{1,0:T(8,128)S(1)}, f32[256,256]{1,0:T(8,128)S(1)}, u32[]{:S(2)}, u32[]{:S(2)}) collective-permute-start(f32[256,256]{1,0:T(8,128)S(1)} %shard_map.67), channel_id=1, source_target_pairs={{0,32},{32,0},{1,33},{33,1},{2,34},{34,2},{3,35},{35,3},{4,36},{36... | collective-permute-start | bytes 786440 | tf_op jit(solution)/shard_map/ppermute | solution.py:40

commit v12 on v11

--- a/solution.py
+++ b/solution.py
@@ -92,10 +92,11 @@
 def build_kernel(own, ids, a_got, b_got, ids_got, out):
     def body(core):
         one, two = (own, a_got) if core == 0 else (b_got, own)
-        value = ids_got[...]
-        rows = [ids[...].astype(jnp.float32)]
-        rows.append(lax.shift_right_logical(value, 8).astype(jnp.float32))
-        rows.append((value & 255).astype(jnp.float32))
+        rows = []
+        for ref in (ids, ids_got):
+            value = ref[...]
+            rows.append(lax.shift_right_logical(value, 8).astype(jnp.float32))
+            rows.append((value & 255).astype(jnp.float32))
         rows.append(jnp.zeros((NOTE - 4, ROWS), jnp.float32))
         note = jnp.concatenate(rows, axis=0).astype(jnp.bfloat16)
         for s in range(8):
@@ -266,7 +267,7 @@
     ids = positives.reshape(1, ROWS)
     got = [swap_core(value) for value in (views_a, views_b, ids)]
     own = jnp.where(core == 0, views_a, views_b)
-    own_ids = jnp.stack([positives // 256, positives % 256]).astype(bf16)
+    own_ids = jnp.where(core == 0, ids, 0)
     built = jax.ShapeDtypeStruct((8, height, ROWS), bf16)
     mine = meet(call(build_kernel, built, [], 1 << 10, own, own_ids, *got))
     picked = jax.ShapeDtypeStruct((6 * ROWS, ROWS), bf16)

time: 72.6 us -> 72.5 us (level)
  transfers between devices with their start and end apart: 8 -> 8, of which waited for: 3 -> 5; matrix products, arithmetic and copies ran while one was open for 2% -> 1% of each run, Pallas kernels for 19% -> 19%
where the time goes in v12:
time: 72.5 us; the launch traced here: 72.3 us
  blocking collectives  47.2 us (65%)
  Pallas kernels  14.9 us (21%)
  waiting for transfers between devices  4.15 us (6%)
  starting transfers between devices  3.58 us (5%)
  other arithmetic  1.76 us (2%)
  between operations  0.74 us (1%)
    all_to_all x2, blocking collectives, meet(): lax.all_to_all(value, AXES, 0, 0, axis_index_groups=teams(), tiled=True)  47.2 us
    pallas_call x9, Pallas kernels, call(): pl.pallas_call(kernel, out_shape=shapes, in_specs=[VMEM] * len(operands),...  14.9 us
    ppermute x8, waiting for transfers between devices, swap_core(): return lax.ppermute(value, 'core', [(0, 1), (1, 0)])  4.15 us
    ppermute x8, starting transfers between devices, swap_core(): return lax.ppermute(value, 'core', [(0, 1), (1, 0)])  3.58 us
  transfers between devices with their start and end apart: 8, of which 5 were waited for; matrix products, arithmetic and copies ran while one was open for 1% of the time, Pallas kernels for 19%

profile of v12, /device:TPU:1, one launch (start us, length us, event | category | flops | bytes accessed | tf_op | source)
XLA Modules:
  0.0 72.3 jit_solution(14609660631954996431)
XLA Ops:
  0.6 1.5 %collective-permute-start.2 = (s32[1,256]{1,0:T(1,128)}, s32[1,256]{1,0:T(1,128)S(1)}, u32[]{:S(2)}, u32[]{:S(2)}) collective-permute-start(s32[1,256]{1,0:T(1,128)} %bitcast.3), channel_id=1, source_target_pairs={{0,32},{32,0},{1,33},{33,1},{2,34},{34,2},{3,35},{35,3},{4,36},{36... | collective-permute-start | bytes 3080 | tf_op jit(solution)/shard_map/ppermute | solution.py:40
  2.1 0.1 collective-permute-start
  2.2 0.4 collective-permute-start.1
  2.6 0.9 %broadcast_select_fusion.2.own = bf16[256,256]{1,0:T(8,128)(2,1)S(1)} fusion(bf16[256,256]{1,0:T(8,128)(2,1)} %param.4, bf16[256,256]{1,0:T(8,128)(2,1)} %param.5, pred[]{:T(512)S(6)} %eq.2), kind=kLoop, calls=%fused_computation.2 | loop fusion | flops 65536 | bytes 393217 | tf_op jit(solution)/shard_map/jit(_where)/select_n | solution.py:269
  3.6 0.1 collective-permute-done.a_got
  3.7 0.2 collective-permute-done.1.b_got
  3.9 0.1 shard_map.59
  4.0 25.0 %all_to_all.10.mine = bf16[8,528,256]{2,1,0:T(8,128)(2,1)S(1)} all-to-all(bf16[8,528,256]{2,1,0:T(8,128)(2,1)S(1)} %shard_map.59), channel_id=1, replica_groups={{0,2,4,6,8,10,12,14},{64,66,68,70,72,74,76,78},{1,3,5,7,9,11,13,15},{65..., dimensions={0} | all-to-all | bytes 4325376 | tf_op jit(solution)/shard_map/all_to_all | solution.py:36
  29.1 0.1 collective-permute-start.4
  29.2 0.1 shard_map.60
  29.3 0.5 collective-permute-start.3
  29.9 1.6 %collective-permute-done.4.theirs = bf16[1536,256]{1,0:T(8,128)(2,1)S(1)} collective-permute-done((bf16[1536,256]{1,0:T(8,128)(2,1)S(1)}, bf16[1536,256]{1,0:T(8,128)(2,1)S(1)}, u32[]{:S(2)}, u32[]{:S(2)}) %collective-permute-start.4) | collective-permute-done | bytes 786464 | tf_op jit(solution)/shard_map/ppermute | solution.py:40
  31.5 6.0 %shard_map.62 = (f32[12,256,256]{2,1,0:T(8,128)S(1)}, s16[1552,256]{1,0:T(8,128)(2,1)S(1)}) custom-call(s32[2,4]{1,0:T(2,128)S(1)} %copy-done, bf16[8,528,256]{2,1,0:T(8,128)(2,1)S(1)} %all_to_all.10.mine, bf16[1536,256]{1,0:T(8,128)(2,1)S(1)} %collective-permute-done.4.theirs), custom_call_target="tpu_custom_call" | custom-call | flops 4831838208 | bytes 8388608 | tf_op jit(solution)/shard_map/pallas_call | solution.py:250
  37.5 0.5 collective-permute-start.6
  38.0 6.1 %shard_map.63 = (f32[12,256,256]{2,1,0:T(8,128)S(1)}, s16[1552,256]{1,0:T(8,128)(2,1)S(1)}) custom-call(s32[2,4]{1,0:T(2,128)S(1)} %copy-done, bf16[8,528,256]{2,1,0:T(8,128)(2,1)S(1)} %all_to_all.10.mine, bf16[1536,256]{1,0:T(8,128)(2,1)S(1)} %collective-permute-done.3.theirs, ...), custom_call_target="tpu_custom_call", output_to_operand_aliasing={{0}: (3, {})} | custom-call | flops 4831838208 | bytes 8388608 | tf_op jit(solution)/shard_map/pallas_call | solution.py:250
  44.1 0.4 collective-permute-start.5
  44.5 1.0 %shard_map.64.refs_0_ = s16[8,528,256]{2,1,0:T(8,128)(2,1)S(1)} custom-call(s32[2,4]{1,0:T(2,128)S(1)} %copy-done, f32[12,256,256]{2,1,0:T(8,128)S(1)} %get-tuple-element.7.keep, s16[1552,256]{1,0:T(8,128)(2,1)S(1)} %collective-permute-done.6.got), custom_call_target="tpu_custom_call" | custom-call | flops 1048576 | bytes 8388608 | tf_op jit(solution)/shard_map/pallas_call | solution.py:250
  45.4 1.0 %collective-permute-done.5.got = s16[1552,256]{1,0:T(8,128)(2,1)S(1)} collective-permute-done((s16[1552,256]{1,0:T(8,128)(2,1)S(1)}, s16[1552,256]{1,0:T(8,128)(2,1)S(1)}, u32[]{:S(2)}, u32[]{:S(2)}) %collective-permute-start.5) | collective-permute-done | bytes 794656 | tf_op jit(solution)/shard_map/ppermute | solution.py:40
  46.4 0.9 %shard_map.65 = s16[8,528,256]{2,1,0:T(8,128)(2,1)S(1)} custom-call(s32[2,4]{1,0:T(2,128)S(1)} %copy-done, f32[12,256,256]{2,1,0:T(8,128)S(1)} %get-tuple-element.7.keep, s16[1552,256]{1,0:T(8,128)(2,1)S(1)} %collective-permute-done.5.got, s16[8,528,256]{2,1,0:T(8,128)(2,1)S(1)} %shard_map.64.refs_0_), custom_call_target="tpu_custom_call", output_to_operand_aliasing={{}: (3, {})} | custom-call | flops 1048576 | bytes 8388608 | tf_op jit(solution)/shard_map/pallas_call | solution.py:250
  47.4 22.2 %all_to_all.11.got = s16[8,528,256]{2,1,0:T(8,128)(2,1)S(1)} all-to-all(s16[8,528,256]{2,1,0:T(8,128)(2,1)S(1)} %shard_map.65), channel_id=1, replica_groups={{0,2,4,6,8,10,12,14},{64,66,68,70,72,74,76,78},{1,3,5,7,9,11,13,15},{65..., dimensions={0} | all-to-all | bytes 4325376 | tf_op jit(solution)/shard_map/all_to_all | solution.py:36
  69.6 0.3 shard_map.67
  69.9 0.3 shard_map.66
  70.2 1.2 %collective-permute-done.7 = f32[256,256]{1,0:T(8,128)S(1)} collective-permute-done((f32[256,256]{1,0:T(8,128)S(1)}, f32[256,256]{1,0:T(8,128)S(1)}, u32[]{:S(2)}, u32[]{:S(2)}) %collective-permute-start.7) | collective-permute-done | bytes 262176 | tf_op jit(solution)/shard_map/ppermute | solution.py:40
  71.5 0.8 %broadcast_select_fusion = (f32[256,256]{1,0:T(8,128)}, f32[256,256]{1,0:T(8,128)}) fusion(f32[256,256]{1,0:T(8,128)S(1)} %collective-permute-done.7, f32[256,256]{1,0:T(8,128)S(1)} %shard_map.66, pred[]{:T(512)S(6)} %eq.2), kind=kLoop, calls=%fused_computation | loop fusion | flops 131072 | bytes 1048577 | tf_op jit(solution)/shard_map/jit(_where)/select_n | solution.py:320
  (8 shorter events, 0.2 us)
Async XLA Ops:
  0.6 3.0 %collective-permute-start.2 = (s32[1,256]{1,0:T(1,128)}, s32[1,256]{1,0:T(1,128)S(1)}, u32[]{:S(2)}, u32[]{:S(2)}) collective-permute-start(s32[1,256]{1,0:T(1,128)} %bitcast.3), channel_id=1, source_target_pairs={{0,32},{32,0},{1,33},{33,1},{2,34},{34,2},{3,35},{35,3},{4,36},{36... | collective-permute-start | bytes 3080 | tf_op jit(solution)/shard_map/ppermute | solution.py:40
  2.1 1.6 %collective-permute-start = (bf16[256,256]{1,0:T(8,128)(2,1)}, bf16[256,256]{1,0:T(8,128)(2,1)S(1)}, u32[]{:S(2)}, u32[]{:S(2)}) collective-permute-start(bf16[256,256]{1,0:T(8,128)(2,1)} %param.4), channel_id=1, source_target_pairs={{0,32},{32,0},{1,33},{33,1},{2,34},{34,2},{3,35},{35,3},{4,36},{36... | collective-permute-start | bytes 393224 | tf_op jit(solution)/shard_map/ppermute | solution.py:40
  2.2 1.7 %collective-permute-start.1 = (bf16[256,256]{1,0:T(8,128)(2,1)}, bf16[256,256]{1,0:T(8,128)(2,1)S(1)}, u32[]{:S(2)}, u32[]{:S(2)}) collective-permute-start(bf16[256,256]{1,0:T(8,128)(2,1)} %param.5), channel_id=1, source_target_pairs={{0,32},{32,0},{1,33},{33,1},{2,34},{34,2},{3,35},{35,3},{4,36},{36... | collective-permute-start | bytes 393224 | tf_op jit(solution)/shard_map/ppermute | solution.py:40
  4.0 25.0 %copy-start = (s32[2,4]{1,0:T(2,128)S(1)}, s32[2,4]{1,0:T(2,128)}, u32[]{:S(2)}) copy-start(s32[2,4]{1,0:T(2,128)} %plan.11) | copy-start | bytes 100
  29.1 2.4 %collective-permute-start.4 = (bf16[1536,256]{1,0:T(8,128)(2,1)S(1)}, bf16[1536,256]{1,0:T(8,128)(2,1)S(1)}, u32[]{:S(2)}, u32[]{:S(2)}) collective-permute-start(bf16[1536,256]{1,0:T(8,128)(2,1)S(1)} %shard_map.61), channel_id=1, source_target_pairs={{0,32},{32,0},{1,33},{33,1},{2,34},{34,2},{3,35},{35,3},{4,36},{36... | collective-permute-start | bytes 2359304 | tf_op jit(solution)/shard_map/ppermute | solution.py:40
  29.3 8.6 %collective-permute-start.3 = (bf16[1536,256]{1,0:T(8,128)(2,1)S(1)}, bf16[1536,256]{1,0:T(8,128)(2,1)S(1)}, u32[]{:S(2)}, u32[]{:S(2)}) collective-permute-start(bf16[1536,256]{1,0:T(8,128)(2,1)S(1)} %shard_map.60), channel_id=1, source_target_pairs={{0,32},{32,0},{1,33},{33,1},{2,34},{34,2},{3,35},{35,3},{4,36},{36... | collective-permute-start | bytes 2359304 | tf_op jit(solution)/shard_map/ppermute | solution.py:40
  37.5 7.0 %collective-permute-start.6 = (s16[1552,256]{1,0:T(8,128)(2,1)S(1)}, s16[1552,256]{1,0:T(8,128)(2,1)S(1)}, u32[]{:S(2)}, u32[]{:S(2)}) collective-permute-start(s16[1552,256]{1,0:T(8,128)(2,1)S(1)} %get-tuple-element.9), channel_id=1, source_target_pairs={{0,32},{32,0},{1,33},{33,1},{2,34},{34,2},{3,35},{35,3},{4,36},{36... | collective-permute-start | bytes 2383880 | tf_op jit(solution)/shard_map/ppermute | solution.py:40
  44.1 2.4 %collective-permute-start.5 = (s16[1552,256]{1,0:T(8,128)(2,1)S(1)}, s16[1552,256]{1,0:T(8,128)(2,1)S(1)}, u32[]{:S(2)}, u32[]{:S(2)}) collective-permute-start(s16[1552,256]{1,0:T(8,128)(2,1)S(1)} %get-tuple-element.8), channel_id=1, source_target_pairs={{0,32},{32,0},{1,33},{33,1},{2,34},{34,2},{3,35},{35,3},{4,36},{36... | collective-permute-start | bytes 2383880 | tf_op jit(solution)/shard_map/ppermute | solution.py:40
  69.8 1.6 %collective-permute-start.7 = (f32[256,256]{1,0:T(8,128)S(1)}, f32[256,256]{1,0:T(8,128)S(1)}, u32[]{:S(2)}, u32[]{:S(2)}) collective-permute-start(f32[256,256]{1,0:T(8,128)S(1)} %shard_map.67), channel_id=1, source_target_pairs={{0,32},{32,0},{1,33},{33,1},{2,34},{34,2},{3,35},{35,3},{4,36},{36... | collective-permute-start | bytes 786440 | tf_op jit(solution)/shard_map/ppermute | solution.py:40
